TPU v7x, 128 devices: a whole 4x4x4 slice. The times are simulated.
128 devices in a mesh: pipe: 4 (over y), fsdp: 32 (over z, x, core).
Axes of the slice: x: 4, y: 4, z: 4, core: 2. Of those that a mesh axis runs over, the one named last changes fastest.
Arguments:
- tokens: bfloat16 [4096, 4096], P('fsdp'), may hold values from -6 to 6
- targets: bfloat16 [4096, 4096], P('fsdp'), may hold values from -6 to 6
- norm_gain: bfloat16 [4, 4096], P('pipe', 'fsdp'), may hold values from 0.099609375 to 1.8984375
- down_weight: bfloat16 [4, 4096, 256], P('pipe', 'fsdp'), may hold values from -0.09375 to 0.09375
- up_weight: bfloat16 [4, 256, 4096], P('pipe', None, 'fsdp'), may hold values from -0.375 to 0.375
- down_vector: bfloat16 [4, 4096, 256], P('pipe', 'fsdp'), may hold values from -1 to 1
- up_vector: bfloat16 [4, 256, 4096], P('pipe', None, 'fsdp'), may hold values from -1 to 1
Outputs:
- next_down: bfloat16 [4, 4096, 256], P('pipe', 'fsdp')
- next_up: bfloat16 [4, 256, 4096], P('pipe', None, 'fsdp')
- quotient: float32 [], replicated
All inputs are finite; a program needn't handle non-finite values.
Results may differ from a plain program's by a relative error of at most 0.02.
Values may be sent and summed in bfloat16 or wider, within the bound.
No kernel may reach another device: no remote copies, remote signals or barrier semaphores. Data moves between devices by JAX's collectives and lax.ppermute only.
A program may use at most 128 MiB of HBM per device.

v0:
```python
import functools

import jax
import jax.numpy as jnp
from jax import lax
from jax.experimental import pallas as pl
from jax.experimental.pallas import tpu as pltpu
from jax.sharding import Mesh, PartitionSpec as P

EPS = 1e-06
D = 4096
RANK = 256
LAYERS = 4
TOKENS = 4096
ROWS = 64
HALF = 2048
F32 = jnp.float32
BF16 = jnp.bfloat16


def shift(value, axis, steps):
    return lax.ppermute(value, axis, [(i, (i + steps) % 4) for i in range(4)])


def swap(value):
    return lax.ppermute(value, "c", [(0, 1), (1, 0)])


def dot(left, right, dims):
    return lax.dot_general(left, right, (dims, ((), ())), preferred_element_type=F32)


def mm(left, right):
    return dot(left, right, ((1,), (0,)))


def mm_nt(left, right):
    return dot(left, right, ((1,), (1,)))


def mm_tn(left, right):
    return dot(left, right, ((0,), (0,)))


def middle(full):
    u, v = full[:, :256], full[:, 256:512]
    r = lax.rsqrt(full[:, 512:513] * (1.0 / D) + EPS)
    c = full[:, 639:640] * (1.0 / D)
    r3c = r * r * r * c
    pre = r * u
    pre_dot = r * v - r3c * u
    s = jax.nn.sigmoid(pre)
    slope = s * (1.0 + pre * (1.0 - s))
    slope2 = s * (1.0 - s) * (2.0 + pre * (1.0 - 2.0 * s))
    act = (pre * s).astype(BF16)
    act_dot = (slope * pre_dot).astype(BF16)
    return u, v, r, c, pre_dot, slope, slope2, act, act_dot


def inner_cotangents(mid, e_full):
    e, e_dot = e_full[:, :256], e_full[:, 256:]
    pre_dot, slope, slope2 = mid[4], mid[5], mid[6]
    s = (e * slope).astype(BF16)
    s_dot = (e_dot * slope + e * slope2 * pre_dot).astype(BF16)
    return s, s_dot


FARS = (0, 3, 1, 2)


def chunk_kernel(gain_hbm, down_hbm, vector_hbm, up_hbm, up_vector_hbm, *refs):
    chunk_ref, column_ref, gain_ref, down_ref, vector_ref, up_ref, up_vector_ref, sems = refs
    copies = [
        pltpu.make_async_copy(source, target, sems.at[i])
        for i, (source, target) in enumerate(
            zip((gain_hbm, down_hbm, vector_hbm, up_hbm, up_vector_hbm), refs[2:7])
        )
    ]
    for copy in copies:
        copy.start()
    for copy in copies:
        copy.wait()
    column = jnp.broadcast_to(gain_ref[...].astype(F32), (128, 128)).T
    column_ref[...] = column
    gain = jnp.concatenate([column, column], 1)
    chunk_ref[0] = (down_ref[0].astype(F32) * gain).astype(BF16)
    chunk_ref[1] = (vector_ref[0].astype(F32) * gain).astype(BF16)
    chunk_ref[2] = up_ref[0].astype(F32).T.astype(BF16)
    chunk_ref[3] = up_vector_ref[0].astype(F32).T.astype(BF16)


def order_kernel(place_ref, own, behind, ahead, across, a_ref, b_ref):
    for far, chunk in zip(FARS, (own, behind, ahead, across)):
        layer = (place_ref[2] + far) & 3
        a_ref[layer] = chunk[:2]
        b_ref[layer] = chunk[2:]


def rows_kernel(place_ref, tokens_ref, targets_ref, keep_ref, give_ref):
    rows = pl.ds(pl.multiple_of(place_ref[2] * 32, 32), 32)
    for i, ref in enumerate((tokens_ref, targets_ref)):
        for slot_z, far_z in enumerate(FARS):
            for slot_x, far_x in enumerate(FARS):
                block = ((place_ref[0] + far_z) & 3) * 4 + ((place_ref[1] + far_x) & 3)
                slot = 4 * slot_z + slot_x
                for out_ref, core in ((keep_ref, place_ref[3]), (give_ref, 1 - place_ref[3])):
                    start = pl.multiple_of((2 * block + core) * 128, 128)
                    out_ref[i, :, 128 * slot : 128 * slot + 128] = ref[rows, pl.ds(start, 128)]


def part_a(refs, layer, i, which):
    return jnp.concatenate(
        [ref[i, layer, which] for ref in refs[:3]] + [refs[3 + i // 2][i % 2, layer, which]], 0
    )


def part_b(refs, layer, i, which):
    if i < 3:
        return refs[i][:, layer, which].reshape(512, RANK)
    return jnp.concatenate([ref[:, layer, which].reshape(256, RANK) for ref in refs[3:]], 0)


def write_sums(part_ref, u, v, s1, s2):
    lane = lax.broadcasted_iota(jnp.int32, (ROWS, 128), 1)
    part_ref[:, :256] = u
    part_ref[:, 256:512] = v
    part_ref[:, 512:] = jnp.where(lane < 64, s1, s2)


def first_kernel(x_ref, *refs):
    a, part_ref = refs[:5], refs[5]
    u = jnp.zeros((ROWS, RANK), F32)
    v = jnp.zeros((ROWS, RANK), F32)
    s1 = jnp.zeros((ROWS, 1), F32)
    for i in range(4):
        h = x_ref[:ROWS, 512 * i : 512 * i + 512]
        hf = h.astype(F32)
        s1 += jnp.sum(hf * hf, axis=1, keepdims=True)
        u += mm(h, part_a(a, 0, i, 0))
        v += mm(h, part_a(a, 0, i, 1))
    write_sums(part_ref, u, v, s1, jnp.zeros((ROWS, 1), F32))


def forward_kernel(layer, x_ref, own_ref, got_ref, *refs):
    b, a = refs[:5], refs[5:10]
    xo_ref, part_ref, full_ref = refs[10:]
    last, layer = (layer - 1) % 2, layer % 2
    full = own_ref[...] + got_ref[...]
    full_ref[...] = full
    mid = middle(full)
    act, act_dot = mid[7], mid[8]
    pair = jnp.concatenate([act, act_dot], 0)
    both = jnp.zeros((2 * ROWS, RANK), F32)
    cross = jnp.zeros((ROWS, RANK), F32)
    s1 = jnp.zeros((ROWS, 1), F32)
    s2 = jnp.zeros((ROWS, 1), F32)
    for i in range(4):
        cols = slice(512 * i, 512 * i + 512)
        step = mm_nt(pair, part_b(b, last, i, 0))
        tail = mm_nt(act, part_b(b, last, i, 1))
        h = (x_ref[:ROWS, cols].astype(F32) + step[:ROWS]).astype(BF16)
        t = (x_ref[ROWS:, cols].astype(F32) + step[ROWS:] + tail).astype(BF16)
        xo_ref[:ROWS, cols] = h
        xo_ref[ROWS:, cols] = t
        hf, tf = h.astype(F32), t.astype(F32)
        s1 += jnp.sum(hf * hf, axis=1, keepdims=True)
        s2 += jnp.sum(hf * tf, axis=1, keepdims=True)
        both += mm(jnp.concatenate([h, t], 0), part_a(a, layer, i, 0))
        cross += mm(h, part_a(a, layer, i, 1))
    write_sums(part_ref, both[:ROWS], both[ROWS:] + cross, s1, s2)


def seed_kernel(x_ref, own_ref, got_ref, goal_ref, *refs):
    cot_ref, part_ref, full_ref = refs[5:]
    full = own_ref[...] + got_ref[...]
    full_ref[...] = full
    mid = middle(full)
    act, act_dot = mid[7], mid[8]
    pair = jnp.concatenate([act, act_dot], 0)
    both = jnp.zeros((2 * ROWS, RANK), F32)
    cross = jnp.zeros((ROWS, RANK), F32)
    for i in range(4):
        cols = slice(512 * i, 512 * i + 512)
        b, q = part_b(refs[:5], 1, i, 0), part_b(refs[:5], 1, i, 1)
        step = mm_nt(pair, b)
        tail = mm_nt(act, q)
        h = (x_ref[:ROWS, cols].astype(F32) + step[:ROWS]).astype(BF16)
        t = (x_ref[ROWS:, cols].astype(F32) + step[ROWS:] + tail).astype(BF16)
        d = (h.astype(F32) - goal_ref[:, cols].astype(F32)).astype(BF16)
        cot_ref[:ROWS, cols] = d
        cot_ref[ROWS:, cols] = t
        both += mm(jnp.concatenate([d, t], 0), b)
        cross += mm(d, q)
    part_ref[:, :256] = both[:ROWS]
    part_ref[:, 256:] = both[ROWS:] + cross


def backward_kernel(layer, x_ref, cot_ref, full_ref, e_own_ref, e_got_ref, *refs):
    a, b = refs[:5], refs[5:10]
    out_ref, part_ref, e_full_ref = refs[10:]
    below, layer = (layer - 1) % 2, layer % 2
    mid = middle(full_ref[...])
    u, v, r, c = mid[:4]
    e_full = e_own_ref[...] + e_got_ref[...]
    e_full_ref[...] = e_full
    s, s_dot = inner_cotangents(mid, e_full)
    pair = jnp.concatenate([s, s_dot], 0)
    sf, sdf = s.astype(F32), s_dot.astype(F32)
    mean = jnp.sum(sf * u, axis=1, keepdims=True) * (1.0 / D)
    mean_dot = jnp.sum(sf * v + sdf * u, axis=1, keepdims=True) * (1.0 / D)
    r3 = r * r * r
    r3c = r3 * c
    r3m = r3 * mean
    by_h = 3.0 * r3m * r * r * c - r3 * mean_dot
    both = jnp.zeros((2 * ROWS, RANK), F32)
    cross = jnp.zeros((ROWS, RANK), F32)
    for i in range(4):
        cols = slice(512 * i, 512 * i + 512)
        ms = mm_nt(pair, part_a(a, layer, i, 0))
        m = ms[:ROWS]
        m_dot = ms[ROWS:] + mm_nt(s, part_a(a, layer, i, 1))
        h, t = x_ref[:ROWS, cols].astype(F32), x_ref[ROWS:, cols].astype(F32)
        bar = r * m - r3m * h
        bar_dot = r * m_dot - r3c * m - r3m * t + by_h * h
        d = (cot_ref[:ROWS, cols].astype(F32) + bar).astype(BF16)
        d_dot = (cot_ref[ROWS:, cols].astype(F32) + bar_dot).astype(BF16)
        out_ref[:ROWS, cols] = d
        out_ref[ROWS:, cols] = d_dot
        both += mm(jnp.concatenate([d, d_dot], 0), part_b(b, below, i, 0))
        cross += mm(d, part_b(b, below, i, 1))
    part_ref[:, :256] = both[:ROWS]
    part_ref[:, 256:] = both[ROWS:] + cross


def hessian_kernel(*refs):
    (x0, cot0, full0, e_own, e_got, x1, cot1, full1, e_full) = refs[:9]
    outs = refs[9:13] + refs[13:14], refs[14:18] + refs[18:19]
    layers = (
        (x0, cot0, full0, lambda: e_own[...] + e_got[...]),
        (x1, cot1, full1, lambda: e_full[...]),
    )
    for i, (x_ref, cot_ref, full_ref, e_sum) in enumerate(layers):
        mid = middle(full_ref[...])
        r, c, act, act_dot = mid[2], mid[3], mid[7], mid[8]
        r3c = r * r * r * c
        s, s_dot = inner_cotangents(mid, e_sum())
        pair = jnp.concatenate([s, s_dot], 0)
        acts = jnp.concatenate([act_dot, act], 0)
        for slot_z, z in enumerate((0, 2, 1, 3)):
            for slot_x, x_ in enumerate((0, 2, 1, 3)):
                block = 4 * z + x_
                cols = slice(128 * block, 128 * block + 128)
                x = x_ref[:, cols].astype(F32)
                h, t = x[:ROWS], x[ROWS:]
                normed = jnp.concatenate(
                    [(r * t - r3c * h).astype(BF16), (r * h).astype(BF16)], 0
                )
                down = mm_tn(normed, pair).astype(BF16)
                up = mm_tn(cot_ref[:, cols], acts).astype(BF16)
                for refs_, slot, inner, value in (
                    (outs[0], slot_z, slot_x, down),
                    (outs[1], slot_x, slot_z, up),
                ):
                    if slot < 3:
                        refs_[slot][inner, i] = value
                    else:
                        refs_[3 + inner // 2][inner % 2, i] = value


def step_kernel(*refs):
    for i in range(2):
        ahead, behind, first, second = refs[4 * i : 4 * i + 4]
        ahead_out, behind_out = refs[8 + 2 * i : 10 + 2 * i]
        ahead_out[:2] = (ahead[:2].astype(F32) + first[...].astype(F32)).astype(BF16)
        ahead_out[2:] = ahead[2:]
        behind_out[:2] = behind[:2]
        behind_out[2:] = (behind[2:].astype(F32) + second[...].astype(F32)).astype(BF16)


def ring_kernel(*refs):
    groups, outs = (refs[3:6], refs[:3]), refs[6:]
    for slot in range(4):
        for group, parts in enumerate(groups):
            total = parts[0][slot].astype(F32)
            for part in parts[1:]:
                total += part[slot].astype(F32)
            outs[slot][2 * group : 2 * group + 2] = total.astype(BF16)


def layer_kernel(place_ref, *refs):
    downs, ups, outs = refs[:4], refs[4:8], refs[8:]
    for slot, far in enumerate((0, 1, 3, 2)):
        layer = (place_ref[2] + far) & 3
        for half, parts in enumerate((downs, ups)):
            total = parts[0][layer].astype(F32)
            for part in parts[1:]:
                total += part[layer].astype(F32)
            outs[slot][128 * half : 128 * half + 128] = total.astype(BF16)


def totals_kernel(b0, b1, b2, b3, gain_ref, vector_ref, share_ref, totals_ref):
    share = b0[...].astype(F32) + b1[...].astype(F32) + b2[...].astype(F32) + b3[...].astype(F32)
    gain = jnp.concatenate([gain_ref[...], gain_ref[...]], 1)
    share = jnp.concatenate([share[:128] * gain, share[128:]], 0)
    share_ref[...] = share
    vector = vector_ref[...].astype(F32)
    lane = lax.broadcasted_iota(jnp.int32, (1, 128), 1)
    totals = jnp.zeros((1, 128), F32)
    for i, product in enumerate((share * share, vector * share, vector * vector)):
        total = jnp.sum(jnp.sum(product, axis=0, keepdims=True), axis=1, keepdims=True)
        totals = jnp.where(lane == i, total, totals)
    totals_ref[...] = totals


def output_kernel(share_ref, totals_ref, down_ref, up_ref, quotient_ref):
    totals = jnp.sum(totals_ref[...], axis=0, keepdims=True)
    means = totals * (1.0 / (2.0 * LAYERS * D * RANK))
    scale = 1.0 / jnp.sqrt(means[:, 0:1] + EPS)
    down_ref[...] = (share_ref[:128] * scale).astype(BF16)
    up_ref[...] = (share_ref[128:] * scale).T.astype(BF16)
    quotient = means[:, 1:2] / (means[:, 2:3] + EPS) * (1.0 / TOKENS)
    quotient_ref[...] = jnp.broadcast_to(quotient, (1, 128))


VMEM = pl.BlockSpec(memory_space=pltpu.VMEM)
ANY = pl.BlockSpec(memory_space=pl.ANY)
SMEM = pl.BlockSpec(memory_space=pltpu.SMEM)


def shape(dims, dtype):
    return jax.ShapeDtypeStruct(dims, dtype)


def call(kernel, in_specs, outs, flops=1 << 20, moved=1 << 20, scratch=()):
    return pl.pallas_call(
        kernel,
        in_specs=in_specs,
        out_specs=[VMEM] * len(outs),
        out_shape=outs,
        scratch_shapes=list(scratch),
        compiler_params=pltpu.CompilerParams(vmem_limit_bytes=24 * 1024 * 1024),
        cost_estimate=pl.CostEstimate(flops=flops, bytes_accessed=moved, transcendentals=0),
    )


def received(blocks, axis):
    own, ahead, behind, across = blocks
    return [own, shift(ahead, axis, 1), shift(behind, axis, -1), shift(across, axis, 2)]


def ring_gather(block, axis):
    behind, ahead = shift(block, axis, 1), shift(block, axis, -1)
    cut = block.shape[0] // 2
    return [block, behind, ahead, shift(behind[:cut], axis, 1), shift(ahead[cut:], axis, -1)]


def slots_stacked(parts, group):
    own, behind, ahead, *across = parts
    layers = slice(2 * group, 2 * group + 2)
    return jnp.stack([own[layers], behind[layers], ahead[layers], across[group]])


def local(tokens, targets, norm_gain, down_weight, up_weight, down_vector, up_vector):
    place = jnp.stack([lax.axis_index(axis) for axis in ("z", "x", "y", "c")]).astype(jnp.int32)
    core = place[3]
    chunk, column = call(
        chunk_kernel,
        [ANY] * 5,
        [shape((4, 128, RANK), BF16), shape((128, 128), F32)],
        scratch=[
            pltpu.VMEM((1, 128), BF16),
            *[pltpu.VMEM((1, 128, RANK), BF16)] * 2,
            *[pltpu.VMEM((1, RANK, 128), BF16)] * 2,
            pltpu.SemaphoreType.DMA((5,)),
        ],
    )(norm_gain, down_weight, down_vector, up_weight, up_vector)
    pair = shape((LAYERS, 2, 128, RANK), BF16)
    a_own, b_own = call(order_kernel, [SMEM] + [VMEM] * 4, [pair, pair])(
        place, chunk, shift(chunk, "y", 1), shift(chunk, "y", -1), shift(chunk, "y", 2)
    )
    a_all, b_all = ring_gather(a_own, "z"), ring_gather(b_own, "x")
    kept, given = call(
        rows_kernel, [SMEM, VMEM, VMEM], [shape((2, 32, HALF), BF16)] * 2, moved=3 << 20
    )(place, tokens, targets)
    got = swap(given)
    rows = jnp.where(
        core == 0, jnp.concatenate([kept, got], 1), jnp.concatenate([got, kept], 1)
    )
    groups = []
    for group in range(2):
        a_group = slots_stacked(a_all, group)
        b_group = slots_stacked(b_all, group)
        if not group:
            a_group, b_group, rows = lax.optimization_barrier((a_group, b_group, rows))
        else:
            a_group, b_group, groups[0] = lax.optimization_barrier(
                (a_group, b_group, groups[0])
            )
        groups.append((ring_gather(a_group, "x"), ring_gather(b_group, "z")))

    h, goal = rows[0], rows[1]
    x = jnp.concatenate([h, jnp.zeros_like(h)], 0)

    def a_of(layer):
        return groups[layer // 2][0]

    def b_of(layer):
        return groups[layer // 2][1]

    wide = shape((2 * ROWS, HALF), BF16)
    sums = shape((ROWS, 640), F32)
    e_sums = shape((ROWS, 512), F32)
    work = 6 * 2 * ROWS * HALF * RANK

    def exchanged(part):
        return part, swap(part)

    states, fulls, cots, e_fulls = [x], [], {}, {}
    (part,) = call(first_kernel, [VMEM] * 6, [sums], work // 3, 3 << 20)(
        x, *a_of(0)
    )
    for layer in range(1, LAYERS):
        x, part, full = call(
            functools.partial(forward_kernel, layer),
            [VMEM] * 13,
            [wide, sums, sums],
            work,
            5 << 20,
        )(x, part, swap(part), *b_of(layer - 1), *a_of(layer))
        states.append(x)
        fulls.append(full)
    cot, part, full = call(
        seed_kernel,
        [VMEM] * 9,
        [wide, e_sums, sums],
        work,
        3 << 20,
    )(x, part, swap(part), goal, *b_of(LAYERS - 1))
    fulls.append(full)

    slot = shape((4, 2, 128, RANK), BF16)
    cut = shape((2, 2, 128, RANK), BF16)
    down_parts, up_parts = [], []
    def backward(layer, cot, e_own, e_got):
        return call(
            functools.partial(backward_kernel, layer),
            [VMEM] * 15,
            [wide, e_sums, e_sums],
            work,
            5 << 20,
        )(states[layer], cot, fulls[layer], e_own, e_got, *a_of(layer), *b_of(layer - 1))

    def hessians(layer, e_own, e_got):
        above = layer + 1
        return call(
            hessian_kernel,
            [VMEM] * 9,
            [slot, slot, slot, cut, cut] * 2,
            2 * work,
            6 << 20,
        )(
            *(states[layer], cots[layer], fulls[layer], e_own, e_got),
            *(states[above], cots[above], fulls[above], e_fulls[above]),
        )

    def first_step(blocks):
        return (
            shift(blocks[3], "z", 1),
            shift(blocks[4], "z", -1),
            shift(blocks[8], "x", 1),
            shift(blocks[9], "x", -1),
        )

    def added(blocks, got):
        return call(step_kernel, [VMEM] * 8, [slot] * 4, moved=5 << 20)(
            *(blocks[1], blocks[2], got[0], got[1]), *(blocks[6], blocks[7], got[2], got[3])
        )

    def second_step(blocks, sent):
        down_parts.extend([blocks[0], shift(sent[0], "z", 1), shift(sent[1], "z", -1)])
        up_parts.extend([blocks[5], shift(sent[2], "x", 1), shift(sent[3], "x", -1)])

    cots[3] = cot
    cot, part, e_fulls[3] = backward(3, cot, part, swap(part))
    cots[2] = cot
    e_own, e_got = part, swap(part)
    blocks = hessians(2, e_own, e_got)
    cot, blocks = lax.optimization_barrier((cot, blocks))
    got = first_step(blocks)
    cot, part, e_fulls[2] = backward(2, cot, e_own, e_got)
    cots[1] = cot
    e_own, e_got = part, swap(part)
    got, e_got = lax.optimization_barrier((got, e_got))
    sent = added(blocks, got)
    cot, sent = lax.optimization_barrier((cot, sent))
    second_step(blocks, sent)
    cot, part, e_fulls[1] = backward(1, cot, e_own, e_got)
    cots[0] = cot
    blocks = hessians(0, part, swap(part))
    blocks, down_parts, up_parts = lax.optimization_barrier((blocks, down_parts, up_parts))
    second_step(blocks, added(blocks, first_step(blocks)))

    four = shape((LAYERS, 128, RANK), BF16)
    downs = call(ring_kernel, [VMEM] * 6, [four] * 4, moved=5 << 20)(*down_parts)
    downs = received(downs, "x")
    ups = call(ring_kernel, [VMEM] * 6, [four] * 4, moved=5 << 20)(*up_parts)
    ups = received(ups, "z")
    blocks = call(
        layer_kernel, [SMEM] + [VMEM] * 8, [shape((256, RANK), BF16)] * 4, moved=2 << 20
    )(place, *downs, *ups)
    share, totals = call(
        totals_kernel,
        [VMEM] * 6,
        [shape((256, RANK), F32), shape((1, 128), F32)],
    )(*received(blocks, "y"), column, jnp.concatenate([down_vector[0], chunk[3]], 0))
    totals = jnp.broadcast_to(totals[None], (128, 1, 128))
    totals = lax.all_to_all(totals, ("y", "z", "x", "c"), 0, 0).reshape(128, 128)
    next_down, next_up, quotient = call(
        output_kernel,
        [VMEM] * 2,
        [shape((128, RANK), BF16), shape((RANK, 128), BF16), shape((1, 128), F32)],
    )(share, totals)
    return (next_down[None], next_up[None], quotient[0, 0])


def solution(mesh):
    fine = Mesh(mesh.devices.reshape(4, 4, 4, 2), ("y", "z", "x", "c"))
    fsdp = ("z", "x", "c")
    placed = (
        P(fsdp, None),
        P(fsdp, None),
        P("y", fsdp),
        P("y", fsdp, None),
        P("y", None, fsdp),
        P("y", fsdp, None),
        P("y", None, fsdp),
    )
    return jax.shard_map(
        local,
        mesh=fine,
        in_specs=placed,
        out_specs=(P("y", fsdp, None), P("y", None, fsdp), P()),
        check_vma=False,
    )
```

profile of v0, /device:TPU:1, one launch (start us, length us, event | category | flops | bytes accessed | tf_op | source)
XLA Modules:
  0.0 245.3 jit_solution(1565156045408046963)
XLA Ops:
  5.2 3.8 %collective-permute-start.2 = (bf16[4,128,256]{2,1,0:T(8,128)(2,1)S(1)}, bf16[4,128,256]{2,1,0:T(8,128)(2,1)S(1)}, u32[]{:S(2)}, u32[]{:S(2)}) collective-permute-start(bf16[4,128,256]{2,1,0:T(8,128)(2,1)S(1)} %get-tuple-element.126.own), channel_id=1, source_target_pairs={{0,64},{32,96},{64,0},{96,32},{1,65},{33,97},{65,1},{97,33},{2,66}... | collective-permute-start | bytes 786440 | tf_op jit(solution)/shard_map/ppermute | solution.py:22
  15.3 5.5 %collective-permute-done.1.ahead = bf16[4,128,256]{2,1,0:T(8,128)(2,1)S(1)} collective-permute-done((bf16[4,128,256]{2,1,0:T(8,128)(2,1)S(1)}, bf16[4,128,256]{2,1,0:T(8,128)(2,1)S(1)}, u32[]{:S(2)}, u32[]{:S(2)}) %collective-permute-start.1) | collective-permute-done | bytes 262176 | tf_op jit(solution)/shard_map/ppermute | solution.py:22
  28.7 8.1 %collective-permute-done.3 = bf16[4,2,128,256]{3,2,1,0:T(8,128)(2,1)S(1)} collective-permute-done((bf16[4,2,128,256]{3,2,1,0:T(8,128)(2,1)S(1)}, bf16[4,2,128,256]{3,2,1,0:T(8,128)(2,1)S(1)}, u32[]{:S(2)}, u32[]{:S(2)}) %collective-permute-start.3) | collective-permute-done | bytes 524320 | tf_op jit(solution)/shard_map/ppermute | solution.py:22
  38.9 5.3 %collective-permute-done.5 = bf16[2,2,128,256]{3,2,1,0:T(8,128)(2,1)S(1)} collective-permute-done((bf16[2,2,128,256]{3,2,1,0:T(8,128)(2,1)S(1)}, bf16[2,2,128,256]{3,2,1,0:T(8,128)(2,1)S(1)}, u32[]{:S(2)}, u32[]{:S(2)}) %collective-permute-start.5) | collective-permute-done | bytes 262176 | tf_op jit(solution)/shard_map/ppermute | solution.py:22
  51.1 15.8 %collective-permute-done.13.refs_2_.refs_7_ = bf16[4,2,2,128,256]{4,3,2,1,0:T(8,128)(2,1)S(1)} collective-permute-done((bf16[4,2,2,128,256]{4,3,2,1,0:T(8,128)(2,1)S(1)}, bf16[4,2,2,128,256]{4,3,2,1,0:T(8,128)(2,1)S(1)}, u32[]{:S(2)}, u32[]{:S(2)}) %collective-permute-start.13) | collective-permute-done | bytes 1048608 | tf_op jit(solution)/shard_map/ppermute | solution.py:22
  67.0 3.5 %collective-permute-start.15 = (bf16[2,2,2,128,256]{4,3,2,1,0:T(8,128)(2,1)S(1)}, bf16[2,2,2,128,256]{4,3,2,1,0:T(8,128)(2,1)S(1)}, u32[]{:S(2)}, u32[]{:S(2)}) collective-permute-start(bf16[2,2,2,128,256]{4,3,2,1,0:T(8,128)(2,1)S(1)} %slice.109), channel_id=1, source_target_pairs={{0,6},{2,0},{4,2},{6,4},{1,7},{3,1},{5,3},{7,5},{8,14},{10,8},{12,... | collective-permute-start | bytes 1572872 | tf_op jit(solution)/shard_map/ppermute | solution.py:22
  77.0 6.7 %collective-permute-done.11 = bf16[2,2,128,256]{3,2,1,0:T(8,128)(2,1)S(1)} collective-permute-done((bf16[2,2,128,256]{3,2,1,0:T(8,128)(2,1)S(1)}, bf16[2,2,128,256]{3,2,1,0:T(8,128)(2,1)S(1)}, u32[]{:S(2)}, u32[]{:S(2)}) %collective-permute-start.11) | collective-permute-done | bytes 262176 | tf_op jit(solution)/shard_map/ppermute | solution.py:22
  90.2 15.8 %collective-permute-done.23.refs_7_.refs_2_ = bf16[4,2,2,128,256]{4,3,2,1,0:T(8,128)(2,1)S(1)} collective-permute-done((bf16[4,2,2,128,256]{4,3,2,1,0:T(8,128)(2,1)S(1)}, bf16[4,2,2,128,256]{4,3,2,1,0:T(8,128)(2,1)S(1)}, u32[]{:S(2)}, u32[]{:S(2)}) %collective-permute-start.23) | collective-permute-done | bytes 1048608 | tf_op jit(solution)/shard_map/ppermute | solution.py:22
  106.0 3.5 %collective-permute-start.25 = (bf16[2,2,2,128,256]{4,3,2,1,0:T(8,128)(2,1)S(1)}, bf16[2,2,2,128,256]{4,3,2,1,0:T(8,128)(2,1)S(1)}, u32[]{:S(2)}, u32[]{:S(2)}) collective-permute-start(bf16[2,2,2,128,256]{4,3,2,1,0:T(8,128)(2,1)S(1)} %slice.113), channel_id=1, source_target_pairs={{0,6},{2,0},{4,2},{6,4},{1,7},{3,1},{5,3},{7,5},{8,14},{10,8},{12,... | collective-permute-start | bytes 1572872 | tf_op jit(solution)/shard_map/ppermute | solution.py:22
  110.2 7.0 %collective-permute-start.20 = (f32[64,640]{1,0:T(8,128)S(1)}, f32[64,640]{1,0:T(8,128)S(1)}, u32[]{:S(2)}, u32[]{:S(2)}) collective-permute-start(f32[64,640]{1,0:T(8,128)S(1)} %shard_map.97.own_ref), channel_id=1, source_target_pairs={{0,1},{1,0},{2,3},{3,2},{4,5},{5,4},{6,7},{7,6},{8,9},{9,8},{10,11... | collective-permute-start | bytes 491528 | tf_op jit(solution)/shard_map/ppermute | solution.py:26
  117.2 3.0 %collective-permute-start.30 = (bf16[2,2,2,128,256]{4,3,2,1,0:T(8,128)(2,1)S(1)}, bf16[2,2,2,128,256]{4,3,2,1,0:T(8,128)(2,1)S(1)}, u32[]{:S(2)}, u32[]{:S(2)}) collective-permute-start(bf16[2,2,2,128,256]{4,3,2,1,0:T(8,128)(2,1)S(1)} %slice.115), channel_id=1, source_target_pairs={{0,24},{8,0},{16,8},{24,16},{1,25},{9,1},{17,9},{25,17},{2,26},{10... | collective-permute-start | bytes 1572872 | tf_op jit(solution)/shard_map/ppermute | solution.py:22
  124.3 3.7 %collective-permute-start.26 = (f32[64,640]{1,0:T(8,128)S(1)}, f32[64,640]{1,0:T(8,128)S(1)}, u32[]{:S(2)}, u32[]{:S(2)}) collective-permute-start(f32[64,640]{1,0:T(8,128)S(1)} %get-tuple-element.148.own_ref), channel_id=1, source_target_pairs={{0,1},{1,0},{2,3},{3,2},{4,5},{5,4},{6,7},{7,6},{8,9},{9,8},{10,11... | collective-permute-start | bytes 491528 | tf_op jit(solution)/shard_map/ppermute | solution.py:26
  128.0 3.5 %collective-permute-done.30.refs_4_.refs_9_ = bf16[2,2,2,128,256]{4,3,2,1,0:T(8,128)(2,1)S(1)} collective-permute-done((bf16[2,2,2,128,256]{4,3,2,1,0:T(8,128)(2,1)S(1)}, bf16[2,2,2,128,256]{4,3,2,1,0:T(8,128)(2,1)S(1)}, u32[]{:S(2)}, u32[]{:S(2)}) %collective-permute-start.30) | collective-permute-done | bytes 524320 | tf_op jit(solution)/shard_map/ppermute | solution.py:22
  131.5 3.2 %collective-permute-done.29.refs_3_.refs_8_ = bf16[2,2,2,128,256]{4,3,2,1,0:T(8,128)(2,1)S(1)} collective-permute-done((bf16[2,2,2,128,256]{4,3,2,1,0:T(8,128)(2,1)S(1)}, bf16[2,2,2,128,256]{4,3,2,1,0:T(8,128)(2,1)S(1)}, u32[]{:S(2)}, u32[]{:S(2)}) %collective-permute-start.29) | collective-permute-done | bytes 524320 | tf_op jit(solution)/shard_map/ppermute | solution.py:22
  147.8 2.9 %collective-permute-start.37 = (bf16[2,2,128,256]{3,2,1,0:T(8,128)(2,1)S(1)}, bf16[2,2,128,256]{3,2,1,0:T(8,128)(2,1)S(1)}, u32[]{:S(2)}, u32[]{:S(2)}) collective-permute-start(bf16[2,2,128,256]{3,2,1,0:T(8,128)(2,1)S(1)} %get-tuple-element.176), channel_id=1, source_target_pairs={{0,6},{2,0},{4,2},{6,4},{1,7},{3,1},{5,3},{7,5},{8,14},{10,8},{12,... | collective-permute-start | bytes 786440 | tf_op jit(solution)/shard_map/ppermute | solution.py:22
  163.5 2.7 %collective-permute-start.39 = (f32[64,512]{1,0:T(8,128)S(1)}, f32[64,512]{1,0:T(8,128)S(1)}, u32[]{:S(2)}, u32[]{:S(2)}) collective-permute-start(f32[64,512]{1,0:T(8,128)S(1)} %get-tuple-element.193.refs_3_), channel_id=1, source_target_pairs={{0,1},{1,0},{2,3},{3,2},{4,5},{5,4},{6,7},{7,6},{8,9},{9,8},{10,11... | collective-permute-start | bytes 393224 | tf_op jit(solution)/shard_map/ppermute | solution.py:26
  172.1 2.7 %collective-permute-start.45 = (bf16[2,2,128,256]{3,2,1,0:T(8,128)(2,1)S(1)}, bf16[2,2,128,256]{3,2,1,0:T(8,128)(2,1)S(1)}, u32[]{:S(2)}, u32[]{:S(2)}) collective-permute-start(bf16[2,2,128,256]{3,2,1,0:T(8,128)(2,1)S(1)} %get-tuple-element.218), channel_id=1, source_target_pairs={{0,24},{8,0},{16,8},{24,16},{1,25},{9,1},{17,9},{25,17},{2,26},{10... | collective-permute-start | bytes 786440 | tf_op jit(solution)/shard_map/ppermute | solution.py:22
  174.8 2.7 %collective-permute-start.47 = (bf16[2,2,128,256]{3,2,1,0:T(8,128)(2,1)S(1)}, bf16[2,2,128,256]{3,2,1,0:T(8,128)(2,1)S(1)}, u32[]{:S(2)}, u32[]{:S(2)}) collective-permute-start(bf16[2,2,128,256]{3,2,1,0:T(8,128)(2,1)S(1)} %get-tuple-element.222), channel_id=1, source_target_pairs={{0,6},{2,0},{4,2},{6,4},{1,7},{3,1},{5,3},{7,5},{8,14},{10,8},{12,... | collective-permute-start | bytes 786440 | tf_op jit(solution)/shard_map/ppermute | solution.py:22
  178.5 3.0 %collective-permute-done.46.refs_6_ = bf16[2,2,128,256]{3,2,1,0:T(8,128)(2,1)S(1)} collective-permute-done((bf16[2,2,128,256]{3,2,1,0:T(8,128)(2,1)S(1)}, bf16[2,2,128,256]{3,2,1,0:T(8,128)(2,1)S(1)}, u32[]{:S(2)}, u32[]{:S(2)}) %collective-permute-start.46) | collective-permute-done | bytes 262176 | tf_op jit(solution)/shard_map/ppermute | solution.py:22
  187.2 4.9 %collective-permute-done.48.refs_4_ = bf16[4,2,128,256]{3,2,1,0:T(8,128)(2,1)S(1)} collective-permute-done((bf16[4,2,128,256]{3,2,1,0:T(8,128)(2,1)S(1)}, bf16[4,2,128,256]{3,2,1,0:T(8,128)(2,1)S(1)}, u32[]{:S(2)}, u32[]{:S(2)}) %collective-permute-start.48) | collective-permute-done | bytes 524320 | tf_op jit(solution)/shard_map/ppermute | solution.py:22
  199.2 2.9 %collective-permute-done.50.refs_1_ = bf16[4,128,256]{2,1,0:T(8,128)(2,1)S(1)} collective-permute-done((bf16[4,128,256]{2,1,0:T(8,128)(2,1)S(1)}, bf16[4,128,256]{2,1,0:T(8,128)(2,1)S(1)}, u32[]{:S(2)}, u32[]{:S(2)}) %collective-permute-start.50) | collective-permute-done | bytes 262176 | tf_op jit(solution)/shard_map/ppermute | solution.py:22
  202.3 6.0 %collective-permute-done.52.refs_3_ = bf16[4,128,256]{2,1,0:T(8,128)(2,1)S(1)} collective-permute-done((bf16[4,128,256]{2,1,0:T(8,128)(2,1)S(1)}, bf16[4,128,256]{2,1,0:T(8,128)(2,1)S(1)}, u32[]{:S(2)}, u32[]{:S(2)}) %collective-permute-start.52) | collective-permute-done | bytes 262176 | tf_op jit(solution)/shard_map/ppermute | solution.py:22
  216.2 3.0 %collective-permute-done.60.b3 = bf16[256,256]{1,0:T(8,128)(2,1)S(1)} collective-permute-done((bf16[256,256]{1,0:T(8,128)(2,1)S(1)}, bf16[256,256]{1,0:T(8,128)(2,1)S(1)}, u32[]{:S(2)}, u32[]{:S(2)}) %collective-permute-start.60) | collective-permute-done | bytes 131104 | tf_op jit(solution)/shard_map/ppermute | solution.py:22
  219.5 24.9 %all_to_all.5 = f32[128,1,128]{2,1,0:T(1,128)S(1)} all-to-all(f32[128,1,128]{2,1,0:T(1,128)S(1)} %broadcast_in_dim.16), channel_id=1, replica_groups=mesh['y'=4,'z'=4,'x'=4,'c'=2] {'y','z','x','c'}, dimensions={0} | all-to-all | bytes 131072 | tf_op jit(solution)/shard_map/all_to_all | solution.py:517
  (160 shorter events, 100.1 us)
Async XLA Ops:
  13.7 14.9 %collective-permute-start.9 = (bf16[2,32,2048]{2,1,0:T(8,128)(2,1)S(1)}, bf16[2,32,2048]{2,1,0:T(8,128)(2,1)S(1)}, u32[]{:S(2)}, u32[]{:S(2)}) collective-permute-start(bf16[2,32,2048]{2,1,0:T(8,128)(2,1)S(1)} %get-tuple-element.130), channel_id=1, source_target_pairs={{0,1},{1,0},{2,3},{3,2},{4,5},{5,4},{6,7},{7,6},{8,9},{9,8},{10,11... | collective-permute-start | bytes 786440 | tf_op jit(solution)/shard_map/ppermute | solution.py:26
  21.8 15.0 %collective-permute-start.3 = (bf16[4,2,128,256]{3,2,1,0:T(8,128)(2,1)S(1)}, bf16[4,2,128,256]{3,2,1,0:T(8,128)(2,1)S(1)}, u32[]{:S(2)}, u32[]{:S(2)}) collective-permute-start(bf16[4,2,128,256]{3,2,1,0:T(8,128)(2,1)S(1)} %get-tuple-element.127), channel_id=1, source_target_pairs={{0,8},{8,16},{16,24},{24,0},{1,9},{9,17},{17,25},{25,1},{2,10},{10... | collective-permute-start | bytes 1572872 | tf_op jit(solution)/shard_map/ppermute | solution.py:22
  23.6 13.4 %collective-permute-start.6 = (bf16[4,2,128,256]{3,2,1,0:T(8,128)(2,1)S(1)}, bf16[4,2,128,256]{3,2,1,0:T(8,128)(2,1)S(1)}, u32[]{:S(2)}, u32[]{:S(2)}) collective-permute-start(bf16[4,2,128,256]{3,2,1,0:T(8,128)(2,1)S(1)} %get-tuple-element.128), channel_id=1, source_target_pairs={{0,2},{2,4},{4,6},{6,0},{1,3},{3,5},{5,7},{7,1},{8,10},{10,12},{12... | collective-permute-start | bytes 1572872 | tf_op jit(solution)/shard_map/ppermute | solution.py:22
  24.9 13.5 %collective-permute-start.4 = (bf16[4,2,128,256]{3,2,1,0:T(8,128)(2,1)S(1)}, bf16[4,2,128,256]{3,2,1,0:T(8,128)(2,1)S(1)}, u32[]{:S(2)}, u32[]{:S(2)}) collective-permute-start(bf16[4,2,128,256]{3,2,1,0:T(8,128)(2,1)S(1)} %get-tuple-element.127), channel_id=1, source_target_pairs={{0,24},{8,0},{16,8},{24,16},{1,25},{9,1},{17,9},{25,17},{2,26},{10... | collective-permute-start | bytes 1572872 | tf_op jit(solution)/shard_map/ppermute | solution.py:22
  44.5 22.4 %collective-permute-start.13 = (bf16[4,2,2,128,256]{4,3,2,1,0:T(8,128)(2,1)S(1)}, bf16[4,2,2,128,256]{4,3,2,1,0:T(8,128)(2,1)S(1)}, u32[]{:S(2)}, u32[]{:S(2)}) collective-permute-start(bf16[4,2,2,128,256]{4,3,2,1,0:T(8,128)(2,1)S(1)} %pad_maximum_fusion.refs_0_.refs_5_), channel_id=1, source_target_pairs={{0,6},{2,0},{4,2},{6,4},{1,7},{3,1},{5,3},{7,5},{8,14},{10,8},{12,... | collective-permute-start | bytes 3145736 | tf_op jit(solution)/shard_map/ppermute | solution.py:22
  47.1 23.3 %collective-permute-start.12 = (bf16[4,2,2,128,256]{4,3,2,1,0:T(8,128)(2,1)S(1)}, bf16[4,2,2,128,256]{4,3,2,1,0:T(8,128)(2,1)S(1)}, u32[]{:S(2)}, u32[]{:S(2)}) collective-permute-start(bf16[4,2,2,128,256]{4,3,2,1,0:T(8,128)(2,1)S(1)} %pad_maximum_fusion.refs_0_.refs_5_), channel_id=1, source_target_pairs={{0,2},{2,4},{4,6},{6,0},{1,3},{3,5},{5,7},{7,1},{8,10},{10,12},{12... | collective-permute-start | bytes 3145736 | tf_op jit(solution)/shard_map/ppermute | solution.py:22
  47.1 23.5 %collective-permute-start.17 = (bf16[4,2,2,128,256]{4,3,2,1,0:T(8,128)(2,1)S(1)}, bf16[4,2,2,128,256]{4,3,2,1,0:T(8,128)(2,1)S(1)}, u32[]{:S(2)}, u32[]{:S(2)}) collective-permute-start(bf16[4,2,2,128,256]{4,3,2,1,0:T(8,128)(2,1)S(1)} %pad_maximum_fusion.1.refs_0_.refs_5_), channel_id=1, source_target_pairs={{0,24},{8,0},{16,8},{24,16},{1,25},{9,1},{17,9},{25,17},{2,26},{10... | collective-permute-start | bytes 3145736 | tf_op jit(solution)/shard_map/ppermute | solution.py:22
  48.5 23.1 %collective-permute-start.16 = (bf16[4,2,2,128,256]{4,3,2,1,0:T(8,128)(2,1)S(1)}, bf16[4,2,2,128,256]{4,3,2,1,0:T(8,128)(2,1)S(1)}, u32[]{:S(2)}, u32[]{:S(2)}) collective-permute-start(bf16[4,2,2,128,256]{4,3,2,1,0:T(8,128)(2,1)S(1)} %pad_maximum_fusion.1.refs_0_.refs_5_), channel_id=1, source_target_pairs={{0,8},{8,16},{16,24},{24,0},{1,9},{9,17},{17,25},{25,1},{2,10},{10... | collective-permute-start | bytes 3145736 | tf_op jit(solution)/shard_map/ppermute | solution.py:22
  48.6 25.9 %collective-permute-start.10 = (bf16[2,2,128,256]{3,2,1,0:T(8,128)(2,1)S(1)}, bf16[2,2,128,256]{3,2,1,0:T(8,128)(2,1)S(1)}, u32[]{:S(2)}, u32[]{:S(2)}) collective-permute-start(bf16[2,2,128,256]{3,2,1,0:T(8,128)(2,1)S(1)} %get-tuple-element.265), channel_id=1, source_target_pairs={{0,24},{8,0},{16,8},{24,16},{1,25},{9,1},{17,9},{25,17},{2,26},{10... | collective-permute-start | bytes 786440 | tf_op jit(solution)/shard_map/ppermute | solution.py:22
  67.0 16.9 %collective-permute-start.15 = (bf16[2,2,2,128,256]{4,3,2,1,0:T(8,128)(2,1)S(1)}, bf16[2,2,2,128,256]{4,3,2,1,0:T(8,128)(2,1)S(1)}, u32[]{:S(2)}, u32[]{:S(2)}) collective-permute-start(bf16[2,2,2,128,256]{4,3,2,1,0:T(8,128)(2,1)S(1)} %slice.109), channel_id=1, source_target_pairs={{0,6},{2,0},{4,2},{6,4},{1,7},{3,1},{5,3},{7,5},{8,14},{10,8},{12,... | collective-permute-start | bytes 1572872 | tf_op jit(solution)/shard_map/ppermute | solution.py:22
  70.5 13.4 %collective-permute-start.14 = (bf16[2,2,2,128,256]{4,3,2,1,0:T(8,128)(2,1)S(1)}, bf16[2,2,2,128,256]{4,3,2,1,0:T(8,128)(2,1)S(1)}, u32[]{:S(2)}, u32[]{:S(2)}) collective-permute-start(bf16[2,2,2,128,256]{4,3,2,1,0:T(8,128)(2,1)S(1)} %slice.108), channel_id=1, source_target_pairs={{0,2},{2,4},{4,6},{6,0},{1,3},{3,5},{5,7},{7,1},{8,10},{10,12},{12... | collective-permute-start | bytes 1572872 | tf_op jit(solution)/shard_map/ppermute | solution.py:22
  70.6 15.1 %collective-permute-start.19 = (bf16[2,2,2,128,256]{4,3,2,1,0:T(8,128)(2,1)S(1)}, bf16[2,2,2,128,256]{4,3,2,1,0:T(8,128)(2,1)S(1)}, u32[]{:S(2)}, u32[]{:S(2)}) collective-permute-start(bf16[2,2,2,128,256]{4,3,2,1,0:T(8,128)(2,1)S(1)} %slice.111), channel_id=1, source_target_pairs={{0,24},{8,0},{16,8},{24,16},{1,25},{9,1},{17,9},{25,17},{2,26},{10... | collective-permute-start | bytes 1572872 | tf_op jit(solution)/shard_map/ppermute | solution.py:22
  71.6 14.1 %collective-permute-start.18 = (bf16[2,2,2,128,256]{4,3,2,1,0:T(8,128)(2,1)S(1)}, bf16[2,2,2,128,256]{4,3,2,1,0:T(8,128)(2,1)S(1)}, u32[]{:S(2)}, u32[]{:S(2)}) collective-permute-start(bf16[2,2,2,128,256]{4,3,2,1,0:T(8,128)(2,1)S(1)} %slice.110), channel_id=1, source_target_pairs={{0,8},{8,16},{16,24},{24,0},{1,9},{9,17},{17,25},{25,1},{2,10},{10... | collective-permute-start | bytes 1572872 | tf_op jit(solution)/shard_map/ppermute | solution.py:22
  85.7 20.3 %collective-permute-start.23 = (bf16[4,2,2,128,256]{4,3,2,1,0:T(8,128)(2,1)S(1)}, bf16[4,2,2,128,256]{4,3,2,1,0:T(8,128)(2,1)S(1)}, u32[]{:S(2)}, u32[]{:S(2)}) collective-permute-start(bf16[4,2,2,128,256]{4,3,2,1,0:T(8,128)(2,1)S(1)} %pad_maximum_fusion.2.refs_5_.refs_0_), channel_id=1, source_target_pairs={{0,6},{2,0},{4,2},{6,4},{1,7},{3,1},{5,3},{7,5},{8,14},{10,8},{12,... | collective-permute-start | bytes 3145736 | tf_op jit(solution)/shard_map/ppermute | solution.py:22
  88.1 21.4 %collective-permute-start.22 = (bf16[4,2,2,128,256]{4,3,2,1,0:T(8,128)(2,1)S(1)}, bf16[4,2,2,128,256]{4,3,2,1,0:T(8,128)(2,1)S(1)}, u32[]{:S(2)}, u32[]{:S(2)}) collective-permute-start(bf16[4,2,2,128,256]{4,3,2,1,0:T(8,128)(2,1)S(1)} %pad_maximum_fusion.2.refs_5_.refs_0_), channel_id=1, source_target_pairs={{0,2},{2,4},{4,6},{6,0},{1,3},{3,5},{5,7},{7,1},{8,10},{10,12},{12... | collective-permute-start | bytes 3145736 | tf_op jit(solution)/shard_map/ppermute | solution.py:22
  88.1 29.1 %collective-permute-start.28 = (bf16[4,2,2,128,256]{4,3,2,1,0:T(8,128)(2,1)S(1)}, bf16[4,2,2,128,256]{4,3,2,1,0:T(8,128)(2,1)S(1)}, u32[]{:S(2)}, u32[]{:S(2)}) collective-permute-start(bf16[4,2,2,128,256]{4,3,2,1,0:T(8,128)(2,1)S(1)} %pad_maximum_fusion.3.refs_0_.refs_5_), channel_id=1, source_target_pairs={{0,24},{8,0},{16,8},{24,16},{1,25},{9,1},{17,9},{25,17},{2,26},{10... | collective-permute-start | bytes 3145736 | tf_op jit(solution)/shard_map/ppermute | solution.py:22
  90.2 30.0 %collective-permute-start.27 = (bf16[4,2,2,128,256]{4,3,2,1,0:T(8,128)(2,1)S(1)}, bf16[4,2,2,128,256]{4,3,2,1,0:T(8,128)(2,1)S(1)}, u32[]{:S(2)}, u32[]{:S(2)}) collective-permute-start(bf16[4,2,2,128,256]{4,3,2,1,0:T(8,128)(2,1)S(1)} %pad_maximum_fusion.3.refs_0_.refs_5_), channel_id=1, source_target_pairs={{0,8},{8,16},{16,24},{24,0},{1,9},{9,17},{17,25},{25,1},{2,10},{10... | collective-permute-start | bytes 3145736 | tf_op jit(solution)/shard_map/ppermute | solution.py:22
  106.0 17.0 %collective-permute-start.25 = (bf16[2,2,2,128,256]{4,3,2,1,0:T(8,128)(2,1)S(1)}, bf16[2,2,2,128,256]{4,3,2,1,0:T(8,128)(2,1)S(1)}, u32[]{:S(2)}, u32[]{:S(2)}) collective-permute-start(bf16[2,2,2,128,256]{4,3,2,1,0:T(8,128)(2,1)S(1)} %slice.113), channel_id=1, source_target_pairs={{0,6},{2,0},{4,2},{6,4},{1,7},{3,1},{5,3},{7,5},{8,14},{10,8},{12,... | collective-permute-start | bytes 1572872 | tf_op jit(solution)/shard_map/ppermute | solution.py:22
  109.6 13.5 %collective-permute-start.24 = (bf16[2,2,2,128,256]{4,3,2,1,0:T(8,128)(2,1)S(1)}, bf16[2,2,2,128,256]{4,3,2,1,0:T(8,128)(2,1)S(1)}, u32[]{:S(2)}, u32[]{:S(2)}) collective-permute-start(bf16[2,2,2,128,256]{4,3,2,1,0:T(8,128)(2,1)S(1)} %slice.112), channel_id=1, source_target_pairs={{0,2},{2,4},{4,6},{6,0},{1,3},{3,5},{5,7},{7,1},{8,10},{10,12},{12... | collective-permute-start | bytes 1572872 | tf_op jit(solution)/shard_map/ppermute | solution.py:22
  117.2 14.3 %collective-permute-start.30 = (bf16[2,2,2,128,256]{4,3,2,1,0:T(8,128)(2,1)S(1)}, bf16[2,2,2,128,256]{4,3,2,1,0:T(8,128)(2,1)S(1)}, u32[]{:S(2)}, u32[]{:S(2)}) collective-permute-start(bf16[2,2,2,128,256]{4,3,2,1,0:T(8,128)(2,1)S(1)} %slice.115), channel_id=1, source_target_pairs={{0,24},{8,0},{16,8},{24,16},{1,25},{9,1},{17,9},{25,17},{2,26},{10... | collective-permute-start | bytes 1572872 | tf_op jit(solution)/shard_map/ppermute | solution.py:22
  120.2 14.5 %collective-permute-start.29 = (bf16[2,2,2,128,256]{4,3,2,1,0:T(8,128)(2,1)S(1)}, bf16[2,2,2,128,256]{4,3,2,1,0:T(8,128)(2,1)S(1)}, u32[]{:S(2)}, u32[]{:S(2)}) collective-permute-start(bf16[2,2,2,128,256]{4,3,2,1,0:T(8,128)(2,1)S(1)} %slice.114), channel_id=1, source_target_pairs={{0,8},{8,16},{16,24},{24,0},{1,9},{9,17},{17,25},{25,1},{2,10},{10... | collective-permute-start | bytes 1572872 | tf_op jit(solution)/shard_map/ppermute | solution.py:22
  156.8 13.2 %collective-permute-start.40 = (bf16[4,2,128,256]{3,2,1,0:T(8,128)(2,1)S(1)}, bf16[4,2,128,256]{3,2,1,0:T(8,128)(2,1)S(1)}, u32[]{:S(2)}, u32[]{:S(2)}) collective-permute-start(bf16[4,2,128,256]{3,2,1,0:T(8,128)(2,1)S(1)} %get-tuple-element.206), channel_id=1, source_target_pairs={{0,8},{8,16},{16,24},{24,0},{1,9},{9,17},{17,25},{25,1},{2,10},{10... | collective-permute-start | bytes 1572872 | tf_op jit(solution)/shard_map/ppermute | solution.py:22
  156.9 13.1 %collective-permute-start.41 = (bf16[4,2,128,256]{3,2,1,0:T(8,128)(2,1)S(1)}, bf16[4,2,128,256]{3,2,1,0:T(8,128)(2,1)S(1)}, u32[]{:S(2)}, u32[]{:S(2)}) collective-permute-start(bf16[4,2,128,256]{3,2,1,0:T(8,128)(2,1)S(1)} %get-tuple-element.207), channel_id=1, source_target_pairs={{0,24},{8,0},{16,8},{24,16},{1,25},{9,1},{17,9},{25,17},{2,26},{10... | collective-permute-start | bytes 1572872 | tf_op jit(solution)/shard_map/ppermute | solution.py:22
  195.2 13.1 %collective-permute-start.52 = (bf16[4,128,256]{2,1,0:T(8,128)(2,1)S(1)}, bf16[4,128,256]{2,1,0:T(8,128)(2,1)S(1)}, u32[]{:S(2)}, u32[]{:S(2)}) collective-permute-start(bf16[4,128,256]{2,1,0:T(8,128)(2,1)S(1)} %get-tuple-element.228), channel_id=1, source_target_pairs={{0,4},{2,6},{4,0},{6,2},{1,5},{3,7},{5,1},{7,3},{8,12},{10,14},{12... | collective-permute-start | bytes 786440 | tf_op jit(solution)/shard_map/ppermute | solution.py:22
  (45 other events, 305.8 us)
where the time goes:
time: 246 us; the launch traced here: 245 us
  waiting for transfers between devices  103 us (42%)
  starting transfers between devices  90.7 us (37%)
  blocking collectives  24.9 us (10%)
  Pallas kernels  17.4 us (7%)
  local copies, waits for them, and re-layouts  7.18 us (3%)
    ppermute x52, waiting for transfers between devices, shift(): return lax.ppermute(value, axis, [(i, (i + steps) % 4) for i in range(4)])  97.3 us
    ppermute x52, starting transfers between devices, shift(): return lax.ppermute(value, axis, [(i, (i + steps) % 4) for i in range(4)])  72 us
    all_to_all x1, blocking collectives, local(): lax.all_to_all(totals, ('y', 'z', 'x', 'c'), 0, 0).reshape(128, 128)  24.9 us
    ppermute x9, starting transfers between devices, swap(): return lax.ppermute(value, 'c', [(0, 1), (1, 0)])  18.7 us
    unnamed x16, local copies, waits for them, and re-layouts  6.46 us
    ppermute x9, waiting for transfers between devices, swap(): return lax.ppermute(value, 'c', [(0, 1), (1, 0)])  6.07 us
  transfers between devices with their start and end apart: 61, of which 30 were waited for; matrix products, arithmetic and copies ran while one was open for 1% of the time, Pallas kernels for 4%

commit v1 on v0

--- a/solution.py
+++ b/solution.py
@@ -348,10 +348,18 @@
     return [own, shift(ahead, axis, 1), shift(behind, axis, -1), shift(across, axis, 2)]
 
 
+def ring_near(block, axis):
+    return shift(block, axis, 1), shift(block, axis, -1)
+
+
+def ring_far(behind, ahead, axis):
+    cut = behind.shape[0] // 2
+    return shift(behind[:cut], axis, 1), shift(ahead[cut:], axis, -1)
+
+
 def ring_gather(block, axis):
-    behind, ahead = shift(block, axis, 1), shift(block, axis, -1)
-    cut = block.shape[0] // 2
-    return [block, behind, ahead, shift(behind[:cut], axis, 1), shift(ahead[cut:], axis, -1)]
+    near = ring_near(block, axis)
+    return [block, *near, *ring_far(*near, axis)]
 
 
 def slots_stacked(parts, group):
@@ -386,18 +394,12 @@
     rows = jnp.where(
         core == 0, jnp.concatenate([kept, got], 1), jnp.concatenate([got, kept], 1)
     )
-    groups = []
-    for group in range(2):
-        a_group = slots_stacked(a_all, group)
-        b_group = slots_stacked(b_all, group)
-        if not group:
-            a_group, b_group, rows = lax.optimization_barrier((a_group, b_group, rows))
-        else:
-            a_group, b_group, groups[0] = lax.optimization_barrier(
-                (a_group, b_group, groups[0])
-            )
-        groups.append((ring_gather(a_group, "x"), ring_gather(b_group, "z")))
-
+    a_group, b_group = slots_stacked(a_all, 0), slots_stacked(b_all, 0)
+    a_group, b_group, rows = lax.optimization_barrier((a_group, b_group, rows))
+    groups = [(ring_gather(a_group, "x"), ring_gather(b_group, "z"))]
+    a_group, b_group = slots_stacked(a_all, 1), slots_stacked(b_all, 1)
+    a_group, b_group, groups[0] = lax.optimization_barrier((a_group, b_group, groups[0]))
+    a_near, b_near = ring_near(a_group, "x"), ring_near(b_group, "z")
     h, goal = rows[0], rows[1]
     x = jnp.concatenate([h, jnp.zeros_like(h)], 0)
 
@@ -429,6 +431,14 @@
         )(x, part, swap(part), *b_of(layer - 1), *a_of(layer))
         states.append(x)
         fulls.append(full)
+        if layer == 1:
+            part, a_near, b_near = lax.optimization_barrier((part, a_near, b_near))
+            groups.append(
+                (
+                    [a_group, *a_near, *ring_far(*a_near, "x")],
+                    [b_group, *b_near, *ring_far(*b_near, "z")],
+                )
+            )
     cot, part, full = call(
         seed_kernel,
         [VMEM] * 9,

time: 246 us -> 245 us (level)
  waiting for transfers between devices: 103 us -> 92.3 us
  starting transfers between devices: 90.7 us -> 99.1 us
    ppermute x52, waiting for transfers between devices: 97.3 us -> 84.2 us  [shift(): return lax.ppermute(value, axis, [(i, (i + steps) % 4) for i in range(4)])]
    ppermute x9, starting transfers between devices: 18.7 us -> 29.5 us  [swap(): return lax.ppermute(value, 'c', [(0, 1), (1, 0)])]
  transfers between devices with their start and end apart: 61 -> 61, of which waited for: 30 -> 32; matrix products, arithmetic and copies ran while one was open for 1% -> 0% of each run, Pallas kernels for 4% -> 4%
where the time goes in v1:
time: 245 us
  starting transfers between devices  99.1 us (40%)
  waiting for transfers between devices  92.3 us (38%)
  blocking collectives  27 us (11%)
  Pallas kernels  17.4 us (7%)
  local copies, waits for them, and re-layouts  7.18 us (3%)
    ppermute x52, waiting for transfers between devices, shift(): return lax.ppermute(value, axis, [(i, (i + steps) % 4) for i in range(4)])  84.2 us
    ppermute x52, starting transfers between devices, shift(): return lax.ppermute(value, axis, [(i, (i + steps) % 4) for i in range(4)])  69.7 us
    ppermute x9, starting transfers between devices, swap(): return lax.ppermute(value, 'c', [(0, 1), (1, 0)])  29.5 us
    all_to_all x1, blocking collectives, local(): lax.all_to_all(totals, ('y', 'z', 'x', 'c'), 0, 0).reshape(128, 128)  27 us
    ppermute x9, waiting for transfers between devices, swap(): return lax.ppermute(value, 'c', [(0, 1), (1, 0)])  8.06 us
    unnamed x16, local copies, waits for them, and re-layouts  6.46 us
  transfers between devices with their start and end apart: 61, of which 32 were waited for; matrix products, arithmetic and copies ran while one was open for 0% of the time, Pallas kernels for 4%

profile of v1, /device:TPU:1, one launch (start us, length us, event | category | flops | bytes accessed | tf_op | source)
XLA Modules:
  0.0 244.7 jit_solution(18371192146442075002)
XLA Ops:
  5.2 3.8 %collective-permute-start.2 = (bf16[4,128,256]{2,1,0:T(8,128)(2,1)S(1)}, bf16[4,128,256]{2,1,0:T(8,128)(2,1)S(1)}, u32[]{:S(2)}, u32[]{:S(2)}) collective-permute-start(bf16[4,128,256]{2,1,0:T(8,128)(2,1)S(1)} %get-tuple-element.131.own), channel_id=1, source_target_pairs={{0,64},{32,96},{64,0},{96,32},{1,65},{33,97},{65,1},{97,33},{2,66}... | collective-permute-start | bytes 786440 | tf_op jit(solution)/shard_map/ppermute | solution.py:22
  15.3 5.5 %collective-permute-done.1.ahead = bf16[4,128,256]{2,1,0:T(8,128)(2,1)S(1)} collective-permute-done((bf16[4,128,256]{2,1,0:T(8,128)(2,1)S(1)}, bf16[4,128,256]{2,1,0:T(8,128)(2,1)S(1)}, u32[]{:S(2)}, u32[]{:S(2)}) %collective-permute-start.1) | collective-permute-done | bytes 262176 | tf_op jit(solution)/shard_map/ppermute | solution.py:22
  28.7 8.1 %collective-permute-done.3 = bf16[4,2,128,256]{3,2,1,0:T(8,128)(2,1)S(1)} collective-permute-done((bf16[4,2,128,256]{3,2,1,0:T(8,128)(2,1)S(1)}, bf16[4,2,128,256]{3,2,1,0:T(8,128)(2,1)S(1)}, u32[]{:S(2)}, u32[]{:S(2)}) %collective-permute-start.3) | collective-permute-done | bytes 524320 | tf_op jit(solution)/shard_map/ppermute | solution.py:22
  38.9 5.3 %collective-permute-done.5 = bf16[2,2,128,256]{3,2,1,0:T(8,128)(2,1)S(1)} collective-permute-done((bf16[2,2,128,256]{3,2,1,0:T(8,128)(2,1)S(1)}, bf16[2,2,128,256]{3,2,1,0:T(8,128)(2,1)S(1)}, u32[]{:S(2)}, u32[]{:S(2)}) %collective-permute-start.5) | collective-permute-done | bytes 262176 | tf_op jit(solution)/shard_map/ppermute | solution.py:22
  51.1 15.8 %collective-permute-done.13.refs_2_.refs_7_ = bf16[4,2,2,128,256]{4,3,2,1,0:T(8,128)(2,1)S(1)} collective-permute-done((bf16[4,2,2,128,256]{4,3,2,1,0:T(8,128)(2,1)S(1)}, bf16[4,2,2,128,256]{4,3,2,1,0:T(8,128)(2,1)S(1)}, u32[]{:S(2)}, u32[]{:S(2)}) %collective-permute-start.13) | collective-permute-done | bytes 1048608 | tf_op jit(solution)/shard_map/ppermute | solution.py:22
  67.0 3.5 %collective-permute-start.15 = (bf16[2,2,2,128,256]{4,3,2,1,0:T(8,128)(2,1)S(1)}, bf16[2,2,2,128,256]{4,3,2,1,0:T(8,128)(2,1)S(1)}, u32[]{:S(2)}, u32[]{:S(2)}) collective-permute-start(bf16[2,2,2,128,256]{4,3,2,1,0:T(8,128)(2,1)S(1)} %slice.109), channel_id=1, source_target_pairs={{0,6},{2,0},{4,2},{6,4},{1,7},{3,1},{5,3},{7,5},{8,14},{10,8},{12,... | collective-permute-start | bytes 1572872 | tf_op jit(solution)/shard_map/ppermute | solution.py:22
  77.0 6.7 %collective-permute-done.11 = bf16[2,2,128,256]{3,2,1,0:T(8,128)(2,1)S(1)} collective-permute-done((bf16[2,2,128,256]{3,2,1,0:T(8,128)(2,1)S(1)}, bf16[2,2,128,256]{3,2,1,0:T(8,128)(2,1)S(1)}, u32[]{:S(2)}, u32[]{:S(2)}) %collective-permute-start.11) | collective-permute-done | bytes 262176 | tf_op jit(solution)/shard_map/ppermute | solution.py:22
  90.8 5.8 %collective-permute-start.20 = (f32[64,640]{1,0:T(8,128)S(1)}, f32[64,640]{1,0:T(8,128)S(1)}, u32[]{:S(2)}, u32[]{:S(2)}) collective-permute-start(f32[64,640]{1,0:T(8,128)S(1)} %shard_map.97.own_ref), channel_id=1, source_target_pairs={{0,1},{1,0},{2,3},{3,2},{4,5},{5,4},{6,7},{7,6},{8,9},{9,8},{10,11... | collective-permute-start | bytes 491528 | tf_op jit(solution)/shard_map/ppermute | solution.py:26
  98.8 8.5 %collective-permute-done.24.refs_2_.refs_7_ = bf16[4,2,2,128,256]{4,3,2,1,0:T(8,128)(2,1)S(1)} collective-permute-done((bf16[4,2,2,128,256]{4,3,2,1,0:T(8,128)(2,1)S(1)}, bf16[4,2,2,128,256]{4,3,2,1,0:T(8,128)(2,1)S(1)}, u32[]{:S(2)}, u32[]{:S(2)}) %collective-permute-start.24) | collective-permute-done | bytes 1048608 | tf_op jit(solution)/shard_map/ppermute | solution.py:22
  114.7 9.5 %collective-permute-start.25 = (f32[64,640]{1,0:T(8,128)S(1)}, f32[64,640]{1,0:T(8,128)S(1)}, u32[]{:S(2)}, u32[]{:S(2)}) collective-permute-start(f32[64,640]{1,0:T(8,128)S(1)} %get-tuple-element.153.own_ref), channel_id=1, source_target_pairs={{0,1},{1,0},{2,3},{3,2},{4,5},{5,4},{6,7},{7,6},{8,9},{9,8},{10,11... | collective-permute-start | bytes 491528 | tf_op jit(solution)/shard_map/ppermute | solution.py:26
  126.5 4.3 %collective-permute-start.28 = (f32[64,640]{1,0:T(8,128)S(1)}, f32[64,640]{1,0:T(8,128)S(1)}, u32[]{:S(2)}, u32[]{:S(2)}) collective-permute-start(f32[64,640]{1,0:T(8,128)S(1)} %get-tuple-element.157.own_ref), channel_id=1, source_target_pairs={{0,1},{1,0},{2,3},{3,2},{4,5},{5,4},{6,7},{7,6},{8,9},{9,8},{10,11... | collective-permute-start | bytes 491528 | tf_op jit(solution)/shard_map/ppermute | solution.py:26
  133.0 2.9 %collective-permute-start.31 = (f32[64,640]{1,0:T(8,128)S(1)}, f32[64,640]{1,0:T(8,128)S(1)}, u32[]{:S(2)}, u32[]{:S(2)}) collective-permute-start(f32[64,640]{1,0:T(8,128)S(1)} %get-tuple-element.161.own_ref), channel_id=1, source_target_pairs={{0,1},{1,0},{2,3},{3,2},{4,5},{5,4},{6,7},{7,6},{8,9},{9,8},{10,11... | collective-permute-start | bytes 491528 | tf_op jit(solution)/shard_map/ppermute | solution.py:26
  143.9 2.7 %collective-permute-start.35 = (bf16[2,2,128,256]{3,2,1,0:T(8,128)(2,1)S(1)}, bf16[2,2,128,256]{3,2,1,0:T(8,128)(2,1)S(1)}, u32[]{:S(2)}, u32[]{:S(2)}) collective-permute-start(bf16[2,2,128,256]{3,2,1,0:T(8,128)(2,1)S(1)} %get-tuple-element.184), channel_id=1, source_target_pairs={{0,24},{8,0},{16,8},{24,16},{1,25},{9,1},{17,9},{25,17},{2,26},{10... | collective-permute-start | bytes 786440 | tf_op jit(solution)/shard_map/ppermute | solution.py:22
  146.6 2.7 %collective-permute-start.37 = (bf16[2,2,128,256]{3,2,1,0:T(8,128)(2,1)S(1)}, bf16[2,2,128,256]{3,2,1,0:T(8,128)(2,1)S(1)}, u32[]{:S(2)}, u32[]{:S(2)}) collective-permute-start(bf16[2,2,128,256]{3,2,1,0:T(8,128)(2,1)S(1)} %get-tuple-element.186), channel_id=1, source_target_pairs={{0,6},{2,0},{4,2},{6,4},{1,7},{3,1},{5,3},{7,5},{8,14},{10,8},{12,... | collective-permute-start | bytes 786440 | tf_op jit(solution)/shard_map/ppermute | solution.py:22
  155.2 2.7 %collective-permute-start.41 = (bf16[4,2,128,256]{3,2,1,0:T(8,128)(2,1)S(1)}, bf16[4,2,128,256]{3,2,1,0:T(8,128)(2,1)S(1)}, u32[]{:S(2)}, u32[]{:S(2)}) collective-permute-start(bf16[4,2,128,256]{3,2,1,0:T(8,128)(2,1)S(1)} %get-tuple-element.217), channel_id=1, source_target_pairs={{0,24},{8,0},{16,8},{24,16},{1,25},{9,1},{17,9},{25,17},{2,26},{10... | collective-permute-start | bytes 1572872 | tf_op jit(solution)/shard_map/ppermute | solution.py:22
  157.9 2.7 %collective-permute-start.43 = (bf16[4,2,128,256]{3,2,1,0:T(8,128)(2,1)S(1)}, bf16[4,2,128,256]{3,2,1,0:T(8,128)(2,1)S(1)}, u32[]{:S(2)}, u32[]{:S(2)}) collective-permute-start(bf16[4,2,128,256]{3,2,1,0:T(8,128)(2,1)S(1)} %get-tuple-element.220), channel_id=1, source_target_pairs={{0,6},{2,0},{4,2},{6,4},{1,7},{3,1},{5,3},{7,5},{8,14},{10,8},{12,... | collective-permute-start | bytes 1572872 | tf_op jit(solution)/shard_map/ppermute | solution.py:22
  161.9 3.0 %collective-permute-start.39 = (f32[64,512]{1,0:T(8,128)S(1)}, f32[64,512]{1,0:T(8,128)S(1)}, u32[]{:S(2)}, u32[]{:S(2)}) collective-permute-start(f32[64,512]{1,0:T(8,128)S(1)} %get-tuple-element.203.refs_3_), channel_id=1, source_target_pairs={{0,1},{1,0},{2,3},{3,2},{4,5},{5,4},{6,7},{7,6},{8,9},{9,8},{10,11... | collective-permute-start | bytes 393224 | tf_op jit(solution)/shard_map/ppermute | solution.py:26
  170.1 2.7 %collective-permute-start.45 = (bf16[2,2,128,256]{3,2,1,0:T(8,128)(2,1)S(1)}, bf16[2,2,128,256]{3,2,1,0:T(8,128)(2,1)S(1)}, u32[]{:S(2)}, u32[]{:S(2)}) collective-permute-start(bf16[2,2,128,256]{3,2,1,0:T(8,128)(2,1)S(1)} %get-tuple-element.228), channel_id=1, source_target_pairs={{0,24},{8,0},{16,8},{24,16},{1,25},{9,1},{17,9},{25,17},{2,26},{10... | collective-permute-start | bytes 786440 | tf_op jit(solution)/shard_map/ppermute | solution.py:22
  176.6 3.0 %collective-permute-done.46.refs_6_ = bf16[2,2,128,256]{3,2,1,0:T(8,128)(2,1)S(1)} collective-permute-done((bf16[2,2,128,256]{3,2,1,0:T(8,128)(2,1)S(1)}, bf16[2,2,128,256]{3,2,1,0:T(8,128)(2,1)S(1)}, u32[]{:S(2)}, u32[]{:S(2)}) %collective-permute-start.46) | collective-permute-done | bytes 262176 | tf_op jit(solution)/shard_map/ppermute | solution.py:22
  185.3 4.5 %collective-permute-done.48.refs_4_ = bf16[4,2,128,256]{3,2,1,0:T(8,128)(2,1)S(1)} collective-permute-done((bf16[4,2,128,256]{3,2,1,0:T(8,128)(2,1)S(1)}, bf16[4,2,128,256]{3,2,1,0:T(8,128)(2,1)S(1)}, u32[]{:S(2)}, u32[]{:S(2)}) %collective-permute-start.48) | collective-permute-done | bytes 524320 | tf_op jit(solution)/shard_map/ppermute | solution.py:22
  197.0 2.9 %collective-permute-done.50.refs_1_ = bf16[4,128,256]{2,1,0:T(8,128)(2,1)S(1)} collective-permute-done((bf16[4,128,256]{2,1,0:T(8,128)(2,1)S(1)}, bf16[4,128,256]{2,1,0:T(8,128)(2,1)S(1)}, u32[]{:S(2)}, u32[]{:S(2)}) %collective-permute-start.50) | collective-permute-done | bytes 262176 | tf_op jit(solution)/shard_map/ppermute | solution.py:22
  200.1 5.9 %collective-permute-done.52.refs_3_ = bf16[4,128,256]{2,1,0:T(8,128)(2,1)S(1)} collective-permute-done((bf16[4,128,256]{2,1,0:T(8,128)(2,1)S(1)}, bf16[4,128,256]{2,1,0:T(8,128)(2,1)S(1)}, u32[]{:S(2)}, u32[]{:S(2)}) %collective-permute-start.52) | collective-permute-done | bytes 262176 | tf_op jit(solution)/shard_map/ppermute | solution.py:22
  213.9 2.8 %collective-permute-done.60.b3 = bf16[256,256]{1,0:T(8,128)(2,1)S(1)} collective-permute-done((bf16[256,256]{1,0:T(8,128)(2,1)S(1)}, bf16[256,256]{1,0:T(8,128)(2,1)S(1)}, u32[]{:S(2)}, u32[]{:S(2)}) %collective-permute-start.60) | collective-permute-done | bytes 131104 | tf_op jit(solution)/shard_map/ppermute | solution.py:22
  216.9 27.0 %all_to_all.5 = f32[128,1,128]{2,1,0:T(1,128)S(1)} all-to-all(f32[128,1,128]{2,1,0:T(1,128)S(1)} %broadcast_in_dim.16), channel_id=1, replica_groups=mesh['y'=4,'z'=4,'x'=4,'c'=2] {'y','z','x','c'}, dimensions={0} | all-to-all | bytes 131072 | tf_op jit(solution)/shard_map/all_to_all | solution.py:527
  (160 shorter events, 101.6 us)
Async XLA Ops:
  13.7 14.9 %collective-permute-start.9 = (bf16[2,32,2048]{2,1,0:T(8,128)(2,1)S(1)}, bf16[2,32,2048]{2,1,0:T(8,128)(2,1)S(1)}, u32[]{:S(2)}, u32[]{:S(2)}) collective-permute-start(bf16[2,32,2048]{2,1,0:T(8,128)(2,1)S(1)} %get-tuple-element.135), channel_id=1, source_target_pairs={{0,1},{1,0},{2,3},{3,2},{4,5},{5,4},{6,7},{7,6},{8,9},{9,8},{10,11... | collective-permute-start | bytes 786440 | tf_op jit(solution)/shard_map/ppermute | solution.py:26
  21.8 15.0 %collective-permute-start.3 = (bf16[4,2,128,256]{3,2,1,0:T(8,128)(2,1)S(1)}, bf16[4,2,128,256]{3,2,1,0:T(8,128)(2,1)S(1)}, u32[]{:S(2)}, u32[]{:S(2)}) collective-permute-start(bf16[4,2,128,256]{3,2,1,0:T(8,128)(2,1)S(1)} %get-tuple-element.132), channel_id=1, source_target_pairs={{0,8},{8,16},{16,24},{24,0},{1,9},{9,17},{17,25},{25,1},{2,10},{10... | collective-permute-start | bytes 1572872 | tf_op jit(solution)/shard_map/ppermute | solution.py:22
  23.6 13.4 %collective-permute-start.6 = (bf16[4,2,128,256]{3,2,1,0:T(8,128)(2,1)S(1)}, bf16[4,2,128,256]{3,2,1,0:T(8,128)(2,1)S(1)}, u32[]{:S(2)}, u32[]{:S(2)}) collective-permute-start(bf16[4,2,128,256]{3,2,1,0:T(8,128)(2,1)S(1)} %get-tuple-element.133), channel_id=1, source_target_pairs={{0,2},{2,4},{4,6},{6,0},{1,3},{3,5},{5,7},{7,1},{8,10},{10,12},{12... | collective-permute-start | bytes 1572872 | tf_op jit(solution)/shard_map/ppermute | solution.py:22
  24.9 13.5 %collective-permute-start.4 = (bf16[4,2,128,256]{3,2,1,0:T(8,128)(2,1)S(1)}, bf16[4,2,128,256]{3,2,1,0:T(8,128)(2,1)S(1)}, u32[]{:S(2)}, u32[]{:S(2)}) collective-permute-start(bf16[4,2,128,256]{3,2,1,0:T(8,128)(2,1)S(1)} %get-tuple-element.132), channel_id=1, source_target_pairs={{0,24},{8,0},{16,8},{24,16},{1,25},{9,1},{17,9},{25,17},{2,26},{10... | collective-permute-start | bytes 1572872 | tf_op jit(solution)/shard_map/ppermute | solution.py:22
  44.5 22.4 %collective-permute-start.13 = (bf16[4,2,2,128,256]{4,3,2,1,0:T(8,128)(2,1)S(1)}, bf16[4,2,2,128,256]{4,3,2,1,0:T(8,128)(2,1)S(1)}, u32[]{:S(2)}, u32[]{:S(2)}) collective-permute-start(bf16[4,2,2,128,256]{4,3,2,1,0:T(8,128)(2,1)S(1)} %pad_maximum_fusion.refs_0_.refs_5_), channel_id=1, source_target_pairs={{0,6},{2,0},{4,2},{6,4},{1,7},{3,1},{5,3},{7,5},{8,14},{10,8},{12,... | collective-permute-start | bytes 3145736 | tf_op jit(solution)/shard_map/ppermute | solution.py:22
  47.1 23.3 %collective-permute-start.12 = (bf16[4,2,2,128,256]{4,3,2,1,0:T(8,128)(2,1)S(1)}, bf16[4,2,2,128,256]{4,3,2,1,0:T(8,128)(2,1)S(1)}, u32[]{:S(2)}, u32[]{:S(2)}) collective-permute-start(bf16[4,2,2,128,256]{4,3,2,1,0:T(8,128)(2,1)S(1)} %pad_maximum_fusion.refs_0_.refs_5_), channel_id=1, source_target_pairs={{0,2},{2,4},{4,6},{6,0},{1,3},{3,5},{5,7},{7,1},{8,10},{10,12},{12... | collective-permute-start | bytes 3145736 | tf_op jit(solution)/shard_map/ppermute | solution.py:22
  47.1 23.5 %collective-permute-start.17 = (bf16[4,2,2,128,256]{4,3,2,1,0:T(8,128)(2,1)S(1)}, bf16[4,2,2,128,256]{4,3,2,1,0:T(8,128)(2,1)S(1)}, u32[]{:S(2)}, u32[]{:S(2)}) collective-permute-start(bf16[4,2,2,128,256]{4,3,2,1,0:T(8,128)(2,1)S(1)} %pad_maximum_fusion.1.refs_0_.refs_5_), channel_id=1, source_target_pairs={{0,24},{8,0},{16,8},{24,16},{1,25},{9,1},{17,9},{25,17},{2,26},{10... | collective-permute-start | bytes 3145736 | tf_op jit(solution)/shard_map/ppermute | solution.py:22
  48.5 23.1 %collective-permute-start.16 = (bf16[4,2,2,128,256]{4,3,2,1,0:T(8,128)(2,1)S(1)}, bf16[4,2,2,128,256]{4,3,2,1,0:T(8,128)(2,1)S(1)}, u32[]{:S(2)}, u32[]{:S(2)}) collective-permute-start(bf16[4,2,2,128,256]{4,3,2,1,0:T(8,128)(2,1)S(1)} %pad_maximum_fusion.1.refs_0_.refs_5_), channel_id=1, source_target_pairs={{0,8},{8,16},{16,24},{24,0},{1,9},{9,17},{17,25},{25,1},{2,10},{10... | collective-permute-start | bytes 3145736 | tf_op jit(solution)/shard_map/ppermute | solution.py:22
  48.6 25.9 %collective-permute-start.10 = (bf16[2,2,128,256]{3,2,1,0:T(8,128)(2,1)S(1)}, bf16[2,2,128,256]{3,2,1,0:T(8,128)(2,1)S(1)}, u32[]{:S(2)}, u32[]{:S(2)}) collective-permute-start(bf16[2,2,128,256]{3,2,1,0:T(8,128)(2,1)S(1)} %get-tuple-element.275), channel_id=1, source_target_pairs={{0,24},{8,0},{16,8},{24,16},{1,25},{9,1},{17,9},{25,17},{2,26},{10... | collective-permute-start | bytes 786440 | tf_op jit(solution)/shard_map/ppermute | solution.py:22
  67.0 16.9 %collective-permute-start.15 = (bf16[2,2,2,128,256]{4,3,2,1,0:T(8,128)(2,1)S(1)}, bf16[2,2,2,128,256]{4,3,2,1,0:T(8,128)(2,1)S(1)}, u32[]{:S(2)}, u32[]{:S(2)}) collective-permute-start(bf16[2,2,2,128,256]{4,3,2,1,0:T(8,128)(2,1)S(1)} %slice.109), channel_id=1, source_target_pairs={{0,6},{2,0},{4,2},{6,4},{1,7},{3,1},{5,3},{7,5},{8,14},{10,8},{12,... | collective-permute-start | bytes 1572872 | tf_op jit(solution)/shard_map/ppermute | solution.py:22
  70.5 13.4 %collective-permute-start.14 = (bf16[2,2,2,128,256]{4,3,2,1,0:T(8,128)(2,1)S(1)}, bf16[2,2,2,128,256]{4,3,2,1,0:T(8,128)(2,1)S(1)}, u32[]{:S(2)}, u32[]{:S(2)}) collective-permute-start(bf16[2,2,2,128,256]{4,3,2,1,0:T(8,128)(2,1)S(1)} %slice.108), channel_id=1, source_target_pairs={{0,2},{2,4},{4,6},{6,0},{1,3},{3,5},{5,7},{7,1},{8,10},{10,12},{12... | collective-permute-start | bytes 1572872 | tf_op jit(solution)/shard_map/ppermute | solution.py:22
  70.6 15.1 %collective-permute-start.19 = (bf16[2,2,2,128,256]{4,3,2,1,0:T(8,128)(2,1)S(1)}, bf16[2,2,2,128,256]{4,3,2,1,0:T(8,128)(2,1)S(1)}, u32[]{:S(2)}, u32[]{:S(2)}) collective-permute-start(bf16[2,2,2,128,256]{4,3,2,1,0:T(8,128)(2,1)S(1)} %slice.111), channel_id=1, source_target_pairs={{0,24},{8,0},{16,8},{24,16},{1,25},{9,1},{17,9},{25,17},{2,26},{10... | collective-permute-start | bytes 1572872 | tf_op jit(solution)/shard_map/ppermute | solution.py:22
  71.6 14.1 %collective-permute-start.18 = (bf16[2,2,2,128,256]{4,3,2,1,0:T(8,128)(2,1)S(1)}, bf16[2,2,2,128,256]{4,3,2,1,0:T(8,128)(2,1)S(1)}, u32[]{:S(2)}, u32[]{:S(2)}) collective-permute-start(bf16[2,2,2,128,256]{4,3,2,1,0:T(8,128)(2,1)S(1)} %slice.110), channel_id=1, source_target_pairs={{0,8},{8,16},{16,24},{24,0},{1,9},{9,17},{17,25},{25,1},{2,10},{10... | collective-permute-start | bytes 1572872 | tf_op jit(solution)/shard_map/ppermute | solution.py:22
  85.7 21.6 %collective-permute-start.24 = (bf16[4,2,2,128,256]{4,3,2,1,0:T(8,128)(2,1)S(1)}, bf16[4,2,2,128,256]{4,3,2,1,0:T(8,128)(2,1)S(1)}, u32[]{:S(2)}, u32[]{:S(2)}) collective-permute-start(bf16[4,2,2,128,256]{4,3,2,1,0:T(8,128)(2,1)S(1)} %pad_maximum_fusion.3.refs_0_.refs_5_), channel_id=1, source_target_pairs={{0,24},{8,0},{16,8},{24,16},{1,25},{9,1},{17,9},{25,17},{2,26},{10... | collective-permute-start | bytes 3145736 | tf_op jit(solution)/shard_map/ppermute | solution.py:22
  87.7 21.2 %collective-permute-start.23 = (bf16[4,2,2,128,256]{4,3,2,1,0:T(8,128)(2,1)S(1)}, bf16[4,2,2,128,256]{4,3,2,1,0:T(8,128)(2,1)S(1)}, u32[]{:S(2)}, u32[]{:S(2)}) collective-permute-start(bf16[4,2,2,128,256]{4,3,2,1,0:T(8,128)(2,1)S(1)} %pad_maximum_fusion.3.refs_0_.refs_5_), channel_id=1, source_target_pairs={{0,8},{8,16},{16,24},{24,0},{1,9},{9,17},{17,25},{25,1},{2,10},{10... | collective-permute-start | bytes 3145736 | tf_op jit(solution)/shard_map/ppermute | solution.py:22
  87.7 21.2 %collective-permute-start.22 = (bf16[4,2,2,128,256]{4,3,2,1,0:T(8,128)(2,1)S(1)}, bf16[4,2,2,128,256]{4,3,2,1,0:T(8,128)(2,1)S(1)}, u32[]{:S(2)}, u32[]{:S(2)}) collective-permute-start(bf16[4,2,2,128,256]{4,3,2,1,0:T(8,128)(2,1)S(1)} %pad_maximum_fusion.2.refs_5_.refs_0_), channel_id=1, source_target_pairs={{0,6},{2,0},{4,2},{6,4},{1,7},{3,1},{5,3},{7,5},{8,14},{10,8},{12,... | collective-permute-start | bytes 3145736 | tf_op jit(solution)/shard_map/ppermute | solution.py:22
  90.2 20.3 %collective-permute-start.21 = (bf16[4,2,2,128,256]{4,3,2,1,0:T(8,128)(2,1)S(1)}, bf16[4,2,2,128,256]{4,3,2,1,0:T(8,128)(2,1)S(1)}, u32[]{:S(2)}, u32[]{:S(2)}) collective-permute-start(bf16[4,2,2,128,256]{4,3,2,1,0:T(8,128)(2,1)S(1)} %pad_maximum_fusion.2.refs_5_.refs_0_), channel_id=1, source_target_pairs={{0,2},{2,4},{4,6},{6,0},{1,3},{3,5},{5,7},{7,1},{8,10},{10,12},{12... | collective-permute-start | bytes 3145736 | tf_op jit(solution)/shard_map/ppermute | solution.py:22
  110.6 14.6 %collective-permute-start.27 = (bf16[2,2,2,128,256]{4,3,2,1,0:T(8,128)(2,1)S(1)}, bf16[2,2,2,128,256]{4,3,2,1,0:T(8,128)(2,1)S(1)}, u32[]{:S(2)}, u32[]{:S(2)}) collective-permute-start(bf16[2,2,2,128,256]{4,3,2,1,0:T(8,128)(2,1)S(1)} %slice.94), channel_id=1, source_target_pairs={{0,6},{2,0},{4,2},{6,4},{1,7},{3,1},{5,3},{7,5},{8,14},{10,8},{12,... | collective-permute-start | bytes 1572872 | tf_op jit(solution)/shard_map/ppermute | solution.py:22
  111.0 14.3 %collective-permute-start.26 = (bf16[2,2,2,128,256]{4,3,2,1,0:T(8,128)(2,1)S(1)}, bf16[2,2,2,128,256]{4,3,2,1,0:T(8,128)(2,1)S(1)}, u32[]{:S(2)}, u32[]{:S(2)}) collective-permute-start(bf16[2,2,2,128,256]{4,3,2,1,0:T(8,128)(2,1)S(1)} %slice.93), channel_id=1, source_target_pairs={{0,2},{2,4},{4,6},{6,0},{1,3},{3,5},{5,7},{7,1},{8,10},{10,12},{12... | collective-permute-start | bytes 1572872 | tf_op jit(solution)/shard_map/ppermute | solution.py:22
  112.2 18.6 %collective-permute-start.30 = (bf16[2,2,2,128,256]{4,3,2,1,0:T(8,128)(2,1)S(1)}, bf16[2,2,2,128,256]{4,3,2,1,0:T(8,128)(2,1)S(1)}, u32[]{:S(2)}, u32[]{:S(2)}) collective-permute-start(bf16[2,2,2,128,256]{4,3,2,1,0:T(8,128)(2,1)S(1)} %slice.96), channel_id=1, source_target_pairs={{0,24},{8,0},{16,8},{24,16},{1,25},{9,1},{17,9},{25,17},{2,26},{10... | collective-permute-start | bytes 1572872 | tf_op jit(solution)/shard_map/ppermute | solution.py:22
  114.7 16.1 %collective-permute-start.29 = (bf16[2,2,2,128,256]{4,3,2,1,0:T(8,128)(2,1)S(1)}, bf16[2,2,2,128,256]{4,3,2,1,0:T(8,128)(2,1)S(1)}, u32[]{:S(2)}, u32[]{:S(2)}) collective-permute-start(bf16[2,2,2,128,256]{4,3,2,1,0:T(8,128)(2,1)S(1)} %slice.95), channel_id=1, source_target_pairs={{0,8},{8,16},{16,24},{24,0},{1,9},{9,17},{17,25},{25,1},{2,10},{10... | collective-permute-start | bytes 1572872 | tf_op jit(solution)/shard_map/ppermute | solution.py:22
  154.9 13.1 %collective-permute-start.40 = (bf16[4,2,128,256]{3,2,1,0:T(8,128)(2,1)S(1)}, bf16[4,2,128,256]{3,2,1,0:T(8,128)(2,1)S(1)}, u32[]{:S(2)}, u32[]{:S(2)}) collective-permute-start(bf16[4,2,128,256]{3,2,1,0:T(8,128)(2,1)S(1)} %get-tuple-element.216), channel_id=1, source_target_pairs={{0,8},{8,16},{16,24},{24,0},{1,9},{9,17},{17,25},{25,1},{2,10},{10... | collective-permute-start | bytes 1572872 | tf_op jit(solution)/shard_map/ppermute | solution.py:22
  155.2 12.8 %collective-permute-start.41 = (bf16[4,2,128,256]{3,2,1,0:T(8,128)(2,1)S(1)}, bf16[4,2,128,256]{3,2,1,0:T(8,128)(2,1)S(1)}, u32[]{:S(2)}, u32[]{:S(2)}) collective-permute-start(bf16[4,2,128,256]{3,2,1,0:T(8,128)(2,1)S(1)} %get-tuple-element.217), channel_id=1, source_target_pairs={{0,24},{8,0},{16,8},{24,16},{1,25},{9,1},{17,9},{25,17},{2,26},{10... | collective-permute-start | bytes 1572872 | tf_op jit(solution)/shard_map/ppermute | solution.py:22
  192.9 13.1 %collective-permute-start.52 = (bf16[4,128,256]{2,1,0:T(8,128)(2,1)S(1)}, bf16[4,128,256]{2,1,0:T(8,128)(2,1)S(1)}, u32[]{:S(2)}, u32[]{:S(2)}) collective-permute-start(bf16[4,128,256]{2,1,0:T(8,128)(2,1)S(1)} %get-tuple-element.238), channel_id=1, source_target_pairs={{0,4},{2,6},{4,0},{6,2},{1,5},{3,7},{5,1},{7,3},{8,12},{10,14},{12... | collective-permute-start | bytes 786440 | tf_op jit(solution)/shard_map/ppermute | solution.py:22
  (45 other events, 306.3 us)

commit v2 on v1

--- a/solution.py
+++ b/solution.py
@@ -232,39 +232,54 @@
     part_ref[:, 256:] = both[ROWS:] + cross
 
 
-def hessian_kernel(*refs):
-    (x0, cot0, full0, e_own, e_got, x1, cot1, full1, e_full) = refs[:9]
-    outs = refs[9:13] + refs[13:14], refs[14:18] + refs[18:19]
-    layers = (
-        (x0, cot0, full0, lambda: e_own[...] + e_got[...]),
-        (x1, cot1, full1, lambda: e_full[...]),
-    )
-    for i, (x_ref, cot_ref, full_ref, e_sum) in enumerate(layers):
+def hessian_layers(refs):
+    e_own, e_got = refs[15:17]
+    for layer in range(LAYERS):
+        if layer == 0:
+            x_ref, cot_ref, full_ref = refs[12:15]
+            e_full = e_own[...] + e_got[...]
+        else:
+            x_ref, cot_ref, full_ref, e_ref = refs[4 * layer - 4 : 4 * layer]
+            e_full = e_ref[...]
         mid = middle(full_ref[...])
         r, c, act, act_dot = mid[2], mid[3], mid[7], mid[8]
-        r3c = r * r * r * c
-        s, s_dot = inner_cotangents(mid, e_sum())
-        pair = jnp.concatenate([s, s_dot], 0)
+        pair = jnp.concatenate(inner_cotangents(mid, e_full), 0)
         acts = jnp.concatenate([act_dot, act], 0)
-        for slot_z, z in enumerate((0, 2, 1, 3)):
-            for slot_x, x_ in enumerate((0, 2, 1, 3)):
-                block = 4 * z + x_
-                cols = slice(128 * block, 128 * block + 128)
-                x = x_ref[:, cols].astype(F32)
-                h, t = x[:ROWS], x[ROWS:]
-                normed = jnp.concatenate(
-                    [(r * t - r3c * h).astype(BF16), (r * h).astype(BF16)], 0
-                )
-                down = mm_tn(normed, pair).astype(BF16)
-                up = mm_tn(cot_ref[:, cols], acts).astype(BF16)
-                for refs_, slot, inner, value in (
-                    (outs[0], slot_z, slot_x, down),
-                    (outs[1], slot_x, slot_z, up),
-                ):
-                    if slot < 3:
-                        refs_[slot][inner, i] = value
-                    else:
-                        refs_[3 + inner // 2][inner % 2, i] = value
+        yield layer, x_ref, cot_ref, r, r * r * r * c, pair, acts
+
+
+def columns(slot_z, slot_x):
+    order = (0, 2, 1, 3)
+    block = 4 * order[slot_z] + order[slot_x]
+    return slice(128 * block, 128 * block + 128)
+
+
+def down_block(x_ref, cols, r, r3c, pair):
+    x = x_ref[:, cols].astype(F32)
+    h, t = x[:ROWS], x[ROWS:]
+    normed = jnp.concatenate([(r * t - r3c * h).astype(BF16), (r * h).astype(BF16)], 0)
+    return mm_tn(normed, pair).astype(BF16)
+
+
+def far_kernel(*refs):
+    outs = refs[17:]
+    for layer, x_ref, cot_ref, r, r3c, pair, acts in hessian_layers(refs):
+        for inner in range(4):
+            cols = columns(3, inner)
+            outs[inner // 2][inner % 2, layer] = down_block(x_ref, cols, r, r3c, pair)
+            up = mm_tn(cot_ref[:, columns(inner, 3)], acts)
+            outs[2 + inner // 2][inner % 2, layer] = up.astype(BF16)
+
+
+def near_kernel(*refs):
+    outs = refs[17:]
+    for layer, x_ref, cot_ref, r, r3c, pair, acts in hessian_layers(refs):
+        for slot in range(3):
+            for inner in range(4):
+                cols = columns(slot, inner)
+                outs[slot][inner, layer] = down_block(x_ref, cols, r, r3c, pair)
+                up = mm_tn(cot_ref[:, columns(inner, slot)], acts)
+                outs[3 + slot][inner, layer] = up.astype(BF16)
 
 
 def step_kernel(*refs):
@@ -277,14 +292,10 @@
         behind_out[2:] = (behind[2:].astype(F32) + second[...].astype(F32)).astype(BF16)
 
 
-def ring_kernel(*refs):
-    groups, outs = (refs[3:6], refs[:3]), refs[6:]
+def ring_kernel(own, behind, ahead, *outs):
     for slot in range(4):
-        for group, parts in enumerate(groups):
-            total = parts[0][slot].astype(F32)
-            for part in parts[1:]:
-                total += part[slot].astype(F32)
-            outs[slot][2 * group : 2 * group + 2] = total.astype(BF16)
+        total = own[slot].astype(F32) + behind[slot].astype(F32) + ahead[slot].astype(F32)
+        outs[slot][...] = total.astype(BF16)
 
 
 def layer_kernel(place_ref, *refs):
@@ -448,9 +459,6 @@
     )(x, part, swap(part), goal, *b_of(LAYERS - 1))
     fulls.append(full)
 
-    slot = shape((4, 2, 128, RANK), BF16)
-    cut = shape((2, 2, 128, RANK), BF16)
-    down_parts, up_parts = [], []
     def backward(layer, cot, e_own, e_got):
         return call(
             functools.partial(backward_kernel, layer),
@@ -460,60 +468,33 @@
             5 << 20,
         )(states[layer], cot, fulls[layer], e_own, e_got, *a_of(layer), *b_of(layer - 1))
 
-    def hessians(layer, e_own, e_got):
-        above = layer + 1
-        return call(
-            hessian_kernel,
-            [VMEM] * 9,
-            [slot, slot, slot, cut, cut] * 2,
-            2 * work,
-            6 << 20,
-        )(
-            *(states[layer], cots[layer], fulls[layer], e_own, e_got),
-            *(states[above], cots[above], fulls[above], e_fulls[above]),
-        )
-
-    def first_step(blocks):
-        return (
-            shift(blocks[3], "z", 1),
-            shift(blocks[4], "z", -1),
-            shift(blocks[8], "x", 1),
-            shift(blocks[9], "x", -1),
-        )
-
-    def added(blocks, got):
-        return call(step_kernel, [VMEM] * 8, [slot] * 4, moved=5 << 20)(
-            *(blocks[1], blocks[2], got[0], got[1]), *(blocks[6], blocks[7], got[2], got[3])
-        )
-
-    def second_step(blocks, sent):
-        down_parts.extend([blocks[0], shift(sent[0], "z", 1), shift(sent[1], "z", -1)])
-        up_parts.extend([blocks[5], shift(sent[2], "x", 1), shift(sent[3], "x", -1)])
-
-    cots[3] = cot
-    cot, part, e_fulls[3] = backward(3, cot, part, swap(part))
-    cots[2] = cot
-    e_own, e_got = part, swap(part)
-    blocks = hessians(2, e_own, e_got)
-    cot, blocks = lax.optimization_barrier((cot, blocks))
-    got = first_step(blocks)
-    cot, part, e_fulls[2] = backward(2, cot, e_own, e_got)
-    cots[1] = cot
-    e_own, e_got = part, swap(part)
-    got, e_got = lax.optimization_barrier((got, e_got))
-    sent = added(blocks, got)
-    cot, sent = lax.optimization_barrier((cot, sent))
-    second_step(blocks, sent)
-    cot, part, e_fulls[1] = backward(1, cot, e_own, e_got)
-    cots[0] = cot
-    blocks = hessians(0, part, swap(part))
-    blocks, down_parts, up_parts = lax.optimization_barrier((blocks, down_parts, up_parts))
-    second_step(blocks, added(blocks, first_step(blocks)))
-
+    operands = []
+    for layer in (3, 2, 1):
+        cots[layer] = cot
+        cot, part, e_fulls[layer] = backward(layer, cot, part, swap(part))
+    for layer in (1, 2, 3):
+        operands += [states[layer], cots[layer], fulls[layer], e_fulls[layer]]
+    operands += [states[0], cot, fulls[0], part, swap(part)]
+
+    slot = shape((4, LAYERS, 128, RANK), BF16)
+    cut = shape((2, LAYERS, 128, RANK), BF16)
     four = shape((LAYERS, 128, RANK), BF16)
-    downs = call(ring_kernel, [VMEM] * 6, [four] * 4, moved=5 << 20)(*down_parts)
+    far = call(far_kernel, [VMEM] * 17, [cut] * 4, work, 6 << 20)(*operands)
+    far = (
+        shift(far[0], "z", 1),
+        shift(far[1], "z", -1),
+        shift(far[2], "x", 1),
+        shift(far[3], "x", -1),
+    )
+    near = call(near_kernel, [VMEM] * 17, [slot] * 6, 3 * work, 10 << 20)(*operands)
+    sent = call(step_kernel, [VMEM] * 8, [slot] * 4, moved=10 << 20)(
+        *(near[1], near[2], far[0], far[1]), *(near[4], near[5], far[2], far[3])
+    )
+    down_parts = near[0], shift(sent[0], "z", 1), shift(sent[1], "z", -1)
+    up_parts = near[3], shift(sent[2], "x", 1), shift(sent[3], "x", -1)
+    downs = call(ring_kernel, [VMEM] * 3, [four] * 4, moved=4 << 20)(*down_parts)
     downs = received(downs, "x")
-    ups = call(ring_kernel, [VMEM] * 6, [four] * 4, moved=5 << 20)(*up_parts)
+    ups = call(ring_kernel, [VMEM] * 3, [four] * 4, moved=4 << 20)(*up_parts)
     ups = received(ups, "z")
     blocks = call(
         layer_kernel, [SMEM] + [VMEM] * 8, [shape((256, RANK), BF16)] * 4, moved=2 << 20

time: 245 us -> 240 us (0.980)
  starting transfers between devices: 99.1 us -> 84.2 us
  waiting for transfers between devices: 92.3 us -> 107 us
  blocking collectives: 27 us -> 21.1 us
    ppermute x52 -> x44, waiting for transfers between devices: 84.2 us -> 99.4 us  [shift(): return lax.ppermute(value, axis, [(i, (i + steps) % 4) for i in range(4)])]
    ppermute x52 -> x44, starting transfers between devices: 69.7 us -> 58.4 us  [shift(): return lax.ppermute(value, axis, [(i, (i + steps) % 4) for i in range(4)])]
    all_to_all x1, blocking collectives: 27 us -> 21.1 us  [local(): lax.all_to_all(totals, ('y', 'z', 'x', 'c'), 0, 0).reshape(128, 128)]
    ppermute x9, starting transfers between devices: 29.5 us -> 25.8 us  [swap(): return lax.ppermute(value, 'c', [(0, 1), (1, 0)])]
  transfers between devices with their start and end apart: 61 -> 53, of which waited for: 32 -> 29; matrix products, arithmetic and copies ran while one was open for 0% -> 0% of each run, Pallas kernels for 4% -> 3%
where the time goes in v2:
time: 240 us; the launch traced here: 239 us
  waiting for transfers between devices  107 us (45%)
  starting transfers between devices  84.2 us (35%)
  blocking collectives  21.1 us (9%)
  Pallas kernels  17.6 us (7%)
  local copies, waits for them, and re-layouts  7.16 us (3%)
    ppermute x44, waiting for transfers between devices, shift(): return lax.ppermute(value, axis, [(i, (i + steps) % 4) for i in range(4)])  99.4 us
    ppermute x44, starting transfers between devices, shift(): return lax.ppermute(value, axis, [(i, (i + steps) % 4) for i in range(4)])  58.4 us
    ppermute x9, starting transfers between devices, swap(): return lax.ppermute(value, 'c', [(0, 1), (1, 0)])  25.8 us
    all_to_all x1, blocking collectives, local(): lax.all_to_all(totals, ('y', 'z', 'x', 'c'), 0, 0).reshape(128, 128)  21.1 us
    ppermute x9, waiting for transfers between devices, swap(): return lax.ppermute(value, 'c', [(0, 1), (1, 0)])  8.06 us
    unnamed x16, local copies, waits for them, and re-layouts  6.46 us
  transfers between devices with their start and end apart: 53, of which 29 were waited for; matrix products, arithmetic and copies ran while one was open for 0% of the time, Pallas kernels for 3%

profile of v2, /device:TPU:1, one launch (start us, length us, event | category | flops | bytes accessed | tf_op | source)
XLA Modules:
  0.0 239.2 jit_solution(8255513809053458275)
XLA Ops:
  5.2 3.8 %collective-permute-start.2 = (bf16[4,128,256]{2,1,0:T(8,128)(2,1)S(1)}, bf16[4,128,256]{2,1,0:T(8,128)(2,1)S(1)}, u32[]{:S(2)}, u32[]{:S(2)}) collective-permute-start(bf16[4,128,256]{2,1,0:T(8,128)(2,1)S(1)} %get-tuple-element.81.own), channel_id=1, source_target_pairs={{0,64},{32,96},{64,0},{96,32},{1,65},{33,97},{65,1},{97,33},{2,66}... | collective-permute-start | bytes 786440 | tf_op jit(solution)/shard_map/ppermute | solution.py:22
  15.3 5.5 %collective-permute-done.1.ahead = bf16[4,128,256]{2,1,0:T(8,128)(2,1)S(1)} collective-permute-done((bf16[4,128,256]{2,1,0:T(8,128)(2,1)S(1)}, bf16[4,128,256]{2,1,0:T(8,128)(2,1)S(1)}, u32[]{:S(2)}, u32[]{:S(2)}) %collective-permute-start.1) | collective-permute-done | bytes 262176 | tf_op jit(solution)/shard_map/ppermute | solution.py:22
  28.7 8.1 %collective-permute-done.3 = bf16[4,2,128,256]{3,2,1,0:T(8,128)(2,1)S(1)} collective-permute-done((bf16[4,2,128,256]{3,2,1,0:T(8,128)(2,1)S(1)}, bf16[4,2,128,256]{3,2,1,0:T(8,128)(2,1)S(1)}, u32[]{:S(2)}, u32[]{:S(2)}) %collective-permute-start.3) | collective-permute-done | bytes 524320 | tf_op jit(solution)/shard_map/ppermute | solution.py:22
  38.9 5.3 %collective-permute-done.5 = bf16[2,2,128,256]{3,2,1,0:T(8,128)(2,1)S(1)} collective-permute-done((bf16[2,2,128,256]{3,2,1,0:T(8,128)(2,1)S(1)}, bf16[2,2,128,256]{3,2,1,0:T(8,128)(2,1)S(1)}, u32[]{:S(2)}, u32[]{:S(2)}) %collective-permute-start.5) | collective-permute-done | bytes 262176 | tf_op jit(solution)/shard_map/ppermute | solution.py:22
  48.6 2.6 %collective-permute-start.10 = (bf16[2,2,128,256]{3,2,1,0:T(8,128)(2,1)S(1)}, bf16[2,2,128,256]{3,2,1,0:T(8,128)(2,1)S(1)}, u32[]{:S(2)}, u32[]{:S(2)}) collective-permute-start(bf16[2,2,128,256]{3,2,1,0:T(8,128)(2,1)S(1)} %get-tuple-element.175), channel_id=1, source_target_pairs={{0,24},{8,0},{16,8},{24,16},{1,25},{9,1},{17,9},{25,17},{2,26},{10... | collective-permute-start | bytes 786440 | tf_op jit(solution)/shard_map/ppermute | solution.py:22
  51.1 15.8 %collective-permute-done.13.refs_2_.refs_7_ = bf16[4,2,2,128,256]{4,3,2,1,0:T(8,128)(2,1)S(1)} collective-permute-done((bf16[4,2,2,128,256]{4,3,2,1,0:T(8,128)(2,1)S(1)}, bf16[4,2,2,128,256]{4,3,2,1,0:T(8,128)(2,1)S(1)}, u32[]{:S(2)}, u32[]{:S(2)}) %collective-permute-start.13) | collective-permute-done | bytes 1048608 | tf_op jit(solution)/shard_map/ppermute | solution.py:22
  66.9 3.5 %collective-permute-start.15 = (bf16[2,2,2,128,256]{4,3,2,1,0:T(8,128)(2,1)S(1)}, bf16[2,2,2,128,256]{4,3,2,1,0:T(8,128)(2,1)S(1)}, u32[]{:S(2)}, u32[]{:S(2)}) collective-permute-start(bf16[2,2,2,128,256]{4,3,2,1,0:T(8,128)(2,1)S(1)} %slice.109), channel_id=1, source_target_pairs={{0,6},{2,0},{4,2},{6,4},{1,7},{3,1},{5,3},{7,5},{8,14},{10,8},{12,... | collective-permute-start | bytes 1572872 | tf_op jit(solution)/shard_map/ppermute | solution.py:22
  77.0 6.7 %collective-permute-done.11 = bf16[2,2,128,256]{3,2,1,0:T(8,128)(2,1)S(1)} collective-permute-done((bf16[2,2,128,256]{3,2,1,0:T(8,128)(2,1)S(1)}, bf16[2,2,128,256]{3,2,1,0:T(8,128)(2,1)S(1)}, u32[]{:S(2)}, u32[]{:S(2)}) %collective-permute-start.11) | collective-permute-done | bytes 262176 | tf_op jit(solution)/shard_map/ppermute | solution.py:22
  90.8 5.8 %collective-permute-start.20 = (f32[64,640]{1,0:T(8,128)S(1)}, f32[64,640]{1,0:T(8,128)S(1)}, u32[]{:S(2)}, u32[]{:S(2)}) collective-permute-start(f32[64,640]{1,0:T(8,128)S(1)} %shard_map.97.own_ref), channel_id=1, source_target_pairs={{0,1},{1,0},{2,3},{3,2},{4,5},{5,4},{6,7},{7,6},{8,9},{9,8},{10,11... | collective-permute-start | bytes 491528 | tf_op jit(solution)/shard_map/ppermute | solution.py:26
  98.8 8.5 %collective-permute-done.24.refs_2_.refs_7_ = bf16[4,2,2,128,256]{4,3,2,1,0:T(8,128)(2,1)S(1)} collective-permute-done((bf16[4,2,2,128,256]{4,3,2,1,0:T(8,128)(2,1)S(1)}, bf16[4,2,2,128,256]{4,3,2,1,0:T(8,128)(2,1)S(1)}, u32[]{:S(2)}, u32[]{:S(2)}) %collective-permute-start.24) | collective-permute-done | bytes 1048608 | tf_op jit(solution)/shard_map/ppermute | solution.py:22
  114.7 9.5 %collective-permute-start.25 = (f32[64,640]{1,0:T(8,128)S(1)}, f32[64,640]{1,0:T(8,128)S(1)}, u32[]{:S(2)}, u32[]{:S(2)}) collective-permute-start(f32[64,640]{1,0:T(8,128)S(1)} %get-tuple-element.103.own_ref), channel_id=1, source_target_pairs={{0,1},{1,0},{2,3},{3,2},{4,5},{5,4},{6,7},{7,6},{8,9},{9,8},{10,11... | collective-permute-start | bytes 491528 | tf_op jit(solution)/shard_map/ppermute | solution.py:26
  126.5 4.3 %collective-permute-start.28 = (f32[64,640]{1,0:T(8,128)S(1)}, f32[64,640]{1,0:T(8,128)S(1)}, u32[]{:S(2)}, u32[]{:S(2)}) collective-permute-start(f32[64,640]{1,0:T(8,128)S(1)} %get-tuple-element.107.own_ref), channel_id=1, source_target_pairs={{0,1},{1,0},{2,3},{3,2},{4,5},{5,4},{6,7},{7,6},{8,9},{9,8},{10,11... | collective-permute-start | bytes 491528 | tf_op jit(solution)/shard_map/ppermute | solution.py:26
  133.0 2.9 %collective-permute-start.31 = (f32[64,640]{1,0:T(8,128)S(1)}, f32[64,640]{1,0:T(8,128)S(1)}, u32[]{:S(2)}, u32[]{:S(2)}) collective-permute-start(f32[64,640]{1,0:T(8,128)S(1)} %get-tuple-element.111.own_ref), channel_id=1, source_target_pairs={{0,1},{1,0},{2,3},{3,2},{4,5},{5,4},{6,7},{7,6},{8,9},{9,8},{10,11... | collective-permute-start | bytes 491528 | tf_op jit(solution)/shard_map/ppermute | solution.py:26
  149.1 2.7 %collective-permute-start.37 = (bf16[2,4,128,256]{3,2,1,0:T(8,128)(2,1)S(1)}, bf16[2,4,128,256]{3,2,1,0:T(8,128)(2,1)S(1)}, u32[]{:S(2)}, u32[]{:S(2)}) collective-permute-start(bf16[2,4,128,256]{3,2,1,0:T(8,128)(2,1)S(1)} %get-tuple-element.131), channel_id=1, source_target_pairs={{0,24},{8,0},{16,8},{24,16},{1,25},{9,1},{17,9},{25,17},{2,26},{10... | collective-permute-start | bytes 1572872 | tf_op jit(solution)/shard_map/ppermute | solution.py:22
  151.8 2.7 %collective-permute-start.39 = (bf16[2,4,128,256]{3,2,1,0:T(8,128)(2,1)S(1)}, bf16[2,4,128,256]{3,2,1,0:T(8,128)(2,1)S(1)}, u32[]{:S(2)}, u32[]{:S(2)}) collective-permute-start(bf16[2,4,128,256]{3,2,1,0:T(8,128)(2,1)S(1)} %get-tuple-element.135), channel_id=1, source_target_pairs={{0,6},{2,0},{4,2},{6,4},{1,7},{3,1},{5,3},{7,5},{8,14},{10,8},{12,... | collective-permute-start | bytes 1572872 | tf_op jit(solution)/shard_map/ppermute | solution.py:22
  156.6 6.9 %collective-permute-done.36.refs_2_ = bf16[2,4,128,256]{3,2,1,0:T(8,128)(2,1)S(1)} collective-permute-done((bf16[2,4,128,256]{3,2,1,0:T(8,128)(2,1)S(1)}, bf16[2,4,128,256]{3,2,1,0:T(8,128)(2,1)S(1)}, u32[]{:S(2)}, u32[]{:S(2)}) %collective-permute-start.36) | collective-permute-done | bytes 524320 | tf_op jit(solution)/shard_map/ppermute | solution.py:22
  166.2 2.7 %collective-permute-start.41 = (bf16[4,4,128,256]{3,2,1,0:T(8,128)(2,1)S(1)}, bf16[4,4,128,256]{3,2,1,0:T(8,128)(2,1)S(1)}, u32[]{:S(2)}, u32[]{:S(2)}) collective-permute-start(bf16[4,4,128,256]{3,2,1,0:T(8,128)(2,1)S(1)} %get-tuple-element.137), channel_id=1, source_target_pairs={{0,24},{8,0},{16,8},{24,16},{1,25},{9,1},{17,9},{25,17},{2,26},{10... | collective-permute-start | bytes 3145736 | tf_op jit(solution)/shard_map/ppermute | solution.py:22
  168.8 2.7 %collective-permute-start.46 = (bf16[4,4,128,256]{3,2,1,0:T(8,128)(2,1)S(1)}, bf16[4,4,128,256]{3,2,1,0:T(8,128)(2,1)S(1)}, u32[]{:S(2)}, u32[]{:S(2)}) collective-permute-start(bf16[4,4,128,256]{3,2,1,0:T(8,128)(2,1)S(1)} %get-tuple-element.144), channel_id=1, source_target_pairs={{0,6},{2,0},{4,2},{6,4},{1,7},{3,1},{5,3},{7,5},{8,14},{10,8},{12,... | collective-permute-start | bytes 3145736 | tf_op jit(solution)/shard_map/ppermute | solution.py:22
  171.5 18.7 %collective-permute-done.40.behind = bf16[4,4,128,256]{3,2,1,0:T(8,128)(2,1)S(1)} collective-permute-done((bf16[4,4,128,256]{3,2,1,0:T(8,128)(2,1)S(1)}, bf16[4,4,128,256]{3,2,1,0:T(8,128)(2,1)S(1)}, u32[]{:S(2)}, u32[]{:S(2)}) %collective-permute-start.40) | collective-permute-done | bytes 1048608 | tf_op jit(solution)/shard_map/ppermute | solution.py:22
  190.6 2.7 %collective-permute-start.43 = (bf16[4,128,256]{2,1,0:T(8,128)(2,1)S(1)}, bf16[4,128,256]{2,1,0:T(8,128)(2,1)S(1)}, u32[]{:S(2)}, u32[]{:S(2)}) collective-permute-start(bf16[4,128,256]{2,1,0:T(8,128)(2,1)S(1)} %get-tuple-element.140), channel_id=1, source_target_pairs={{0,6},{2,0},{4,2},{6,4},{1,7},{3,1},{5,3},{7,5},{8,14},{10,8},{12,... | collective-permute-start | bytes 786440 | tf_op jit(solution)/shard_map/ppermute | solution.py:22
  194.4 2.7 %collective-permute-start.48 = (bf16[4,128,256]{2,1,0:T(8,128)(2,1)S(1)}, bf16[4,128,256]{2,1,0:T(8,128)(2,1)S(1)}, u32[]{:S(2)}, u32[]{:S(2)}) collective-permute-start(bf16[4,128,256]{2,1,0:T(8,128)(2,1)S(1)} %get-tuple-element.147), channel_id=1, source_target_pairs={{0,24},{8,0},{16,8},{24,16},{1,25},{9,1},{17,9},{25,17},{2,26},{10... | collective-permute-start | bytes 786440 | tf_op jit(solution)/shard_map/ppermute | solution.py:22
  199.4 5.3 %collective-permute-done.44.refs_3_ = bf16[4,128,256]{2,1,0:T(8,128)(2,1)S(1)} collective-permute-done((bf16[4,128,256]{2,1,0:T(8,128)(2,1)S(1)}, bf16[4,128,256]{2,1,0:T(8,128)(2,1)S(1)}, u32[]{:S(2)}, u32[]{:S(2)}) %collective-permute-start.44) | collective-permute-done | bytes 262176 | tf_op jit(solution)/shard_map/ppermute | solution.py:22
  214.0 3.0 %collective-permute-done.52.b3 = bf16[256,256]{1,0:T(8,128)(2,1)S(1)} collective-permute-done((bf16[256,256]{1,0:T(8,128)(2,1)S(1)}, bf16[256,256]{1,0:T(8,128)(2,1)S(1)}, u32[]{:S(2)}, u32[]{:S(2)}) %collective-permute-start.52) | collective-permute-done | bytes 131104 | tf_op jit(solution)/shard_map/ppermute | solution.py:22
  217.3 21.1 %all_to_all.5 = f32[128,1,128]{2,1,0:T(1,128)S(1)} all-to-all(f32[128,1,128]{2,1,0:T(1,128)S(1)} %broadcast_in_dim.16), channel_id=1, replica_groups=mesh['y'=4,'z'=4,'x'=4,'c'=2] {'y','z','x','c'}, dimensions={0} | all-to-all | bytes 131072 | tf_op jit(solution)/shard_map/all_to_all | solution.py:508
  (143 shorter events, 84.9 us)
Async XLA Ops:
  13.7 14.9 %collective-permute-start.9 = (bf16[2,32,2048]{2,1,0:T(8,128)(2,1)S(1)}, bf16[2,32,2048]{2,1,0:T(8,128)(2,1)S(1)}, u32[]{:S(2)}, u32[]{:S(2)}) collective-permute-start(bf16[2,32,2048]{2,1,0:T(8,128)(2,1)S(1)} %get-tuple-element.85), channel_id=1, source_target_pairs={{0,1},{1,0},{2,3},{3,2},{4,5},{5,4},{6,7},{7,6},{8,9},{9,8},{10,11... | collective-permute-start | bytes 786440 | tf_op jit(solution)/shard_map/ppermute | solution.py:26
  21.8 15.0 %collective-permute-start.3 = (bf16[4,2,128,256]{3,2,1,0:T(8,128)(2,1)S(1)}, bf16[4,2,128,256]{3,2,1,0:T(8,128)(2,1)S(1)}, u32[]{:S(2)}, u32[]{:S(2)}) collective-permute-start(bf16[4,2,128,256]{3,2,1,0:T(8,128)(2,1)S(1)} %get-tuple-element.82), channel_id=1, source_target_pairs={{0,8},{8,16},{16,24},{24,0},{1,9},{9,17},{17,25},{25,1},{2,10},{10... | collective-permute-start | bytes 1572872 | tf_op jit(solution)/shard_map/ppermute | solution.py:22
  44.5 22.4 %collective-permute-start.13 = (bf16[4,2,2,128,256]{4,3,2,1,0:T(8,128)(2,1)S(1)}, bf16[4,2,2,128,256]{4,3,2,1,0:T(8,128)(2,1)S(1)}, u32[]{:S(2)}, u32[]{:S(2)}) collective-permute-start(bf16[4,2,2,128,256]{4,3,2,1,0:T(8,128)(2,1)S(1)} %pad_maximum_fusion.refs_0_.refs_5_), channel_id=1, source_target_pairs={{0,6},{2,0},{4,2},{6,4},{1,7},{3,1},{5,3},{7,5},{8,14},{10,8},{12,... | collective-permute-start | bytes 3145736 | tf_op jit(solution)/shard_map/ppermute | solution.py:22
  47.1 23.3 %collective-permute-start.12 = (bf16[4,2,2,128,256]{4,3,2,1,0:T(8,128)(2,1)S(1)}, bf16[4,2,2,128,256]{4,3,2,1,0:T(8,128)(2,1)S(1)}, u32[]{:S(2)}, u32[]{:S(2)}) collective-permute-start(bf16[4,2,2,128,256]{4,3,2,1,0:T(8,128)(2,1)S(1)} %pad_maximum_fusion.refs_0_.refs_5_), channel_id=1, source_target_pairs={{0,2},{2,4},{4,6},{6,0},{1,3},{3,5},{5,7},{7,1},{8,10},{10,12},{12... | collective-permute-start | bytes 3145736 | tf_op jit(solution)/shard_map/ppermute | solution.py:22
  47.1 23.5 %collective-permute-start.17 = (bf16[4,2,2,128,256]{4,3,2,1,0:T(8,128)(2,1)S(1)}, bf16[4,2,2,128,256]{4,3,2,1,0:T(8,128)(2,1)S(1)}, u32[]{:S(2)}, u32[]{:S(2)}) collective-permute-start(bf16[4,2,2,128,256]{4,3,2,1,0:T(8,128)(2,1)S(1)} %pad_maximum_fusion.1.refs_0_.refs_5_), channel_id=1, source_target_pairs={{0,24},{8,0},{16,8},{24,16},{1,25},{9,1},{17,9},{25,17},{2,26},{10... | collective-permute-start | bytes 3145736 | tf_op jit(solution)/shard_map/ppermute | solution.py:22
  48.5 23.1 %collective-permute-start.16 = (bf16[4,2,2,128,256]{4,3,2,1,0:T(8,128)(2,1)S(1)}, bf16[4,2,2,128,256]{4,3,2,1,0:T(8,128)(2,1)S(1)}, u32[]{:S(2)}, u32[]{:S(2)}) collective-permute-start(bf16[4,2,2,128,256]{4,3,2,1,0:T(8,128)(2,1)S(1)} %pad_maximum_fusion.1.refs_0_.refs_5_), channel_id=1, source_target_pairs={{0,8},{8,16},{16,24},{24,0},{1,9},{9,17},{17,25},{25,1},{2,10},{10... | collective-permute-start | bytes 3145736 | tf_op jit(solution)/shard_map/ppermute | solution.py:22
  48.6 25.9 %collective-permute-start.10 = (bf16[2,2,128,256]{3,2,1,0:T(8,128)(2,1)S(1)}, bf16[2,2,128,256]{3,2,1,0:T(8,128)(2,1)S(1)}, u32[]{:S(2)}, u32[]{:S(2)}) collective-permute-start(bf16[2,2,128,256]{3,2,1,0:T(8,128)(2,1)S(1)} %get-tuple-element.175), channel_id=1, source_target_pairs={{0,24},{8,0},{16,8},{24,16},{1,25},{9,1},{17,9},{25,17},{2,26},{10... | collective-permute-start | bytes 786440 | tf_op jit(solution)/shard_map/ppermute | solution.py:22
  66.9 16.9 %collective-permute-start.15 = (bf16[2,2,2,128,256]{4,3,2,1,0:T(8,128)(2,1)S(1)}, bf16[2,2,2,128,256]{4,3,2,1,0:T(8,128)(2,1)S(1)}, u32[]{:S(2)}, u32[]{:S(2)}) collective-permute-start(bf16[2,2,2,128,256]{4,3,2,1,0:T(8,128)(2,1)S(1)} %slice.109), channel_id=1, source_target_pairs={{0,6},{2,0},{4,2},{6,4},{1,7},{3,1},{5,3},{7,5},{8,14},{10,8},{12,... | collective-permute-start | bytes 1572872 | tf_op jit(solution)/shard_map/ppermute | solution.py:22
  70.6 15.1 %collective-permute-start.19 = (bf16[2,2,2,128,256]{4,3,2,1,0:T(8,128)(2,1)S(1)}, bf16[2,2,2,128,256]{4,3,2,1,0:T(8,128)(2,1)S(1)}, u32[]{:S(2)}, u32[]{:S(2)}) collective-permute-start(bf16[2,2,2,128,256]{4,3,2,1,0:T(8,128)(2,1)S(1)} %slice.111), channel_id=1, source_target_pairs={{0,24},{8,0},{16,8},{24,16},{1,25},{9,1},{17,9},{25,17},{2,26},{10... | collective-permute-start | bytes 1572872 | tf_op jit(solution)/shard_map/ppermute | solution.py:22
  71.6 14.1 %collective-permute-start.18 = (bf16[2,2,2,128,256]{4,3,2,1,0:T(8,128)(2,1)S(1)}, bf16[2,2,2,128,256]{4,3,2,1,0:T(8,128)(2,1)S(1)}, u32[]{:S(2)}, u32[]{:S(2)}) collective-permute-start(bf16[2,2,2,128,256]{4,3,2,1,0:T(8,128)(2,1)S(1)} %slice.110), channel_id=1, source_target_pairs={{0,8},{8,16},{16,24},{24,0},{1,9},{9,17},{17,25},{25,1},{2,10},{10... | collective-permute-start | bytes 1572872 | tf_op jit(solution)/shard_map/ppermute | solution.py:22
  85.7 21.6 %collective-permute-start.24 = (bf16[4,2,2,128,256]{4,3,2,1,0:T(8,128)(2,1)S(1)}, bf16[4,2,2,128,256]{4,3,2,1,0:T(8,128)(2,1)S(1)}, u32[]{:S(2)}, u32[]{:S(2)}) collective-permute-start(bf16[4,2,2,128,256]{4,3,2,1,0:T(8,128)(2,1)S(1)} %pad_maximum_fusion.3.refs_0_.refs_5_), channel_id=1, source_target_pairs={{0,24},{8,0},{16,8},{24,16},{1,25},{9,1},{17,9},{25,17},{2,26},{10... | collective-permute-start | bytes 3145736 | tf_op jit(solution)/shard_map/ppermute | solution.py:22
  87.7 21.2 %collective-permute-start.23 = (bf16[4,2,2,128,256]{4,3,2,1,0:T(8,128)(2,1)S(1)}, bf16[4,2,2,128,256]{4,3,2,1,0:T(8,128)(2,1)S(1)}, u32[]{:S(2)}, u32[]{:S(2)}) collective-permute-start(bf16[4,2,2,128,256]{4,3,2,1,0:T(8,128)(2,1)S(1)} %pad_maximum_fusion.3.refs_0_.refs_5_), channel_id=1, source_target_pairs={{0,8},{8,16},{16,24},{24,0},{1,9},{9,17},{17,25},{25,1},{2,10},{10... | collective-permute-start | bytes 3145736 | tf_op jit(solution)/shard_map/ppermute | solution.py:22
  87.7 21.2 %collective-permute-start.22 = (bf16[4,2,2,128,256]{4,3,2,1,0:T(8,128)(2,1)S(1)}, bf16[4,2,2,128,256]{4,3,2,1,0:T(8,128)(2,1)S(1)}, u32[]{:S(2)}, u32[]{:S(2)}) collective-permute-start(bf16[4,2,2,128,256]{4,3,2,1,0:T(8,128)(2,1)S(1)} %pad_maximum_fusion.2.refs_5_.refs_0_), channel_id=1, source_target_pairs={{0,6},{2,0},{4,2},{6,4},{1,7},{3,1},{5,3},{7,5},{8,14},{10,8},{12,... | collective-permute-start | bytes 3145736 | tf_op jit(solution)/shard_map/ppermute | solution.py:22
  90.2 20.3 %collective-permute-start.21 = (bf16[4,2,2,128,256]{4,3,2,1,0:T(8,128)(2,1)S(1)}, bf16[4,2,2,128,256]{4,3,2,1,0:T(8,128)(2,1)S(1)}, u32[]{:S(2)}, u32[]{:S(2)}) collective-permute-start(bf16[4,2,2,128,256]{4,3,2,1,0:T(8,128)(2,1)S(1)} %pad_maximum_fusion.2.refs_5_.refs_0_), channel_id=1, source_target_pairs={{0,2},{2,4},{4,6},{6,0},{1,3},{3,5},{5,7},{7,1},{8,10},{10,12},{12... | collective-permute-start | bytes 3145736 | tf_op jit(solution)/shard_map/ppermute | solution.py:22
  110.6 14.6 %collective-permute-start.27 = (bf16[2,2,2,128,256]{4,3,2,1,0:T(8,128)(2,1)S(1)}, bf16[2,2,2,128,256]{4,3,2,1,0:T(8,128)(2,1)S(1)}, u32[]{:S(2)}, u32[]{:S(2)}) collective-permute-start(bf16[2,2,2,128,256]{4,3,2,1,0:T(8,128)(2,1)S(1)} %slice.94), channel_id=1, source_target_pairs={{0,6},{2,0},{4,2},{6,4},{1,7},{3,1},{5,3},{7,5},{8,14},{10,8},{12,... | collective-permute-start | bytes 1572872 | tf_op jit(solution)/shard_map/ppermute | solution.py:22
  110.9 14.3 %collective-permute-start.26 = (bf16[2,2,2,128,256]{4,3,2,1,0:T(8,128)(2,1)S(1)}, bf16[2,2,2,128,256]{4,3,2,1,0:T(8,128)(2,1)S(1)}, u32[]{:S(2)}, u32[]{:S(2)}) collective-permute-start(bf16[2,2,2,128,256]{4,3,2,1,0:T(8,128)(2,1)S(1)} %slice.93), channel_id=1, source_target_pairs={{0,2},{2,4},{4,6},{6,0},{1,3},{3,5},{5,7},{7,1},{8,10},{10,12},{12... | collective-permute-start | bytes 1572872 | tf_op jit(solution)/shard_map/ppermute | solution.py:22
  112.2 18.6 %collective-permute-start.30 = (bf16[2,2,2,128,256]{4,3,2,1,0:T(8,128)(2,1)S(1)}, bf16[2,2,2,128,256]{4,3,2,1,0:T(8,128)(2,1)S(1)}, u32[]{:S(2)}, u32[]{:S(2)}) collective-permute-start(bf16[2,2,2,128,256]{4,3,2,1,0:T(8,128)(2,1)S(1)} %slice.96), channel_id=1, source_target_pairs={{0,24},{8,0},{16,8},{24,16},{1,25},{9,1},{17,9},{25,17},{2,26},{10... | collective-permute-start | bytes 1572872 | tf_op jit(solution)/shard_map/ppermute | solution.py:22
  114.7 16.1 %collective-permute-start.29 = (bf16[2,2,2,128,256]{4,3,2,1,0:T(8,128)(2,1)S(1)}, bf16[2,2,2,128,256]{4,3,2,1,0:T(8,128)(2,1)S(1)}, u32[]{:S(2)}, u32[]{:S(2)}) collective-permute-start(bf16[2,2,2,128,256]{4,3,2,1,0:T(8,128)(2,1)S(1)} %slice.95), channel_id=1, source_target_pairs={{0,8},{8,16},{16,24},{24,0},{1,9},{9,17},{17,25},{25,1},{2,10},{10... | collective-permute-start | bytes 1572872 | tf_op jit(solution)/shard_map/ppermute | solution.py:22
  149.0 14.4 %collective-permute-start.36 = (bf16[2,4,128,256]{3,2,1,0:T(8,128)(2,1)S(1)}, bf16[2,4,128,256]{3,2,1,0:T(8,128)(2,1)S(1)}, u32[]{:S(2)}, u32[]{:S(2)}) collective-permute-start(bf16[2,4,128,256]{3,2,1,0:T(8,128)(2,1)S(1)} %get-tuple-element.130), channel_id=1, source_target_pairs={{0,8},{8,16},{16,24},{24,0},{1,9},{9,17},{17,25},{25,1},{2,10},{10... | collective-permute-start | bytes 1572872 | tf_op jit(solution)/shard_map/ppermute | solution.py:22
  149.1 14.3 %collective-permute-start.37 = (bf16[2,4,128,256]{3,2,1,0:T(8,128)(2,1)S(1)}, bf16[2,4,128,256]{3,2,1,0:T(8,128)(2,1)S(1)}, u32[]{:S(2)}, u32[]{:S(2)}) collective-permute-start(bf16[2,4,128,256]{3,2,1,0:T(8,128)(2,1)S(1)} %get-tuple-element.131), channel_id=1, source_target_pairs={{0,24},{8,0},{16,8},{24,16},{1,25},{9,1},{17,9},{25,17},{2,26},{10... | collective-permute-start | bytes 1572872 | tf_op jit(solution)/shard_map/ppermute | solution.py:22
  166.1 24.1 %collective-permute-start.40 = (bf16[4,4,128,256]{3,2,1,0:T(8,128)(2,1)S(1)}, bf16[4,4,128,256]{3,2,1,0:T(8,128)(2,1)S(1)}, u32[]{:S(2)}, u32[]{:S(2)}) collective-permute-start(bf16[4,4,128,256]{3,2,1,0:T(8,128)(2,1)S(1)} %get-tuple-element.136), channel_id=1, source_target_pairs={{0,8},{8,16},{16,24},{24,0},{1,9},{9,17},{17,25},{25,1},{2,10},{10... | collective-permute-start | bytes 3145736 | tf_op jit(solution)/shard_map/ppermute | solution.py:22
  166.2 24.0 %collective-permute-start.41 = (bf16[4,4,128,256]{3,2,1,0:T(8,128)(2,1)S(1)}, bf16[4,4,128,256]{3,2,1,0:T(8,128)(2,1)S(1)}, u32[]{:S(2)}, u32[]{:S(2)}) collective-permute-start(bf16[4,4,128,256]{3,2,1,0:T(8,128)(2,1)S(1)} %get-tuple-element.137), channel_id=1, source_target_pairs={{0,24},{8,0},{16,8},{24,16},{1,25},{9,1},{17,9},{25,17},{2,26},{10... | collective-permute-start | bytes 3145736 | tf_op jit(solution)/shard_map/ppermute | solution.py:22
  168.8 25.1 %collective-permute-start.45 = (bf16[4,4,128,256]{3,2,1,0:T(8,128)(2,1)S(1)}, bf16[4,4,128,256]{3,2,1,0:T(8,128)(2,1)S(1)}, u32[]{:S(2)}, u32[]{:S(2)}) collective-permute-start(bf16[4,4,128,256]{3,2,1,0:T(8,128)(2,1)S(1)} %get-tuple-element.143), channel_id=1, source_target_pairs={{0,2},{2,4},{4,6},{6,0},{1,3},{3,5},{5,7},{7,1},{8,10},{10,12},{12... | collective-permute-start | bytes 3145736 | tf_op jit(solution)/shard_map/ppermute | solution.py:22
  168.8 25.1 %collective-permute-start.46 = (bf16[4,4,128,256]{3,2,1,0:T(8,128)(2,1)S(1)}, bf16[4,4,128,256]{3,2,1,0:T(8,128)(2,1)S(1)}, u32[]{:S(2)}, u32[]{:S(2)}) collective-permute-start(bf16[4,4,128,256]{3,2,1,0:T(8,128)(2,1)S(1)} %get-tuple-element.144), channel_id=1, source_target_pairs={{0,6},{2,0},{4,2},{6,4},{1,7},{3,1},{5,3},{7,5},{8,14},{10,8},{12,... | collective-permute-start | bytes 3145736 | tf_op jit(solution)/shard_map/ppermute | solution.py:22
  (37 other events, 250.0 us)

commit v3 on v2

--- a/solution.py
+++ b/solution.py
@@ -144,7 +144,7 @@
 def forward_kernel(layer, x_ref, own_ref, got_ref, *refs):
     b, a = refs[:5], refs[5:10]
     xo_ref, part_ref, full_ref = refs[10:]
-    last, layer = (layer - 1) % 2, layer % 2
+    last = layer - 1
     full = own_ref[...] + got_ref[...]
     full_ref[...] = full
     mid = middle(full)
@@ -181,7 +181,7 @@
     cross = jnp.zeros((ROWS, RANK), F32)
     for i in range(4):
         cols = slice(512 * i, 512 * i + 512)
-        b, q = part_b(refs[:5], 1, i, 0), part_b(refs[:5], 1, i, 1)
+        b, q = part_b(refs[:5], LAYERS - 1, i, 0), part_b(refs[:5], LAYERS - 1, i, 1)
         step = mm_nt(pair, b)
         tail = mm_nt(act, q)
         h = (x_ref[:ROWS, cols].astype(F32) + step[:ROWS]).astype(BF16)
@@ -198,7 +198,7 @@
 def backward_kernel(layer, x_ref, cot_ref, full_ref, e_own_ref, e_got_ref, *refs):
     a, b = refs[:5], refs[5:10]
     out_ref, part_ref, e_full_ref = refs[10:]
-    below, layer = (layer - 1) % 2, layer % 2
+    below = layer - 1
     mid = middle(full_ref[...])
     u, v, r, c = mid[:4]
     e_full = e_own_ref[...] + e_got_ref[...]
@@ -342,14 +342,14 @@
     return jax.ShapeDtypeStruct(dims, dtype)
 
 
-def call(kernel, in_specs, outs, flops=1 << 20, moved=1 << 20, scratch=()):
+def call(kernel, in_specs, outs, flops=1 << 20, moved=1 << 20, scratch=(), grant=24):
     return pl.pallas_call(
         kernel,
         in_specs=in_specs,
         out_specs=[VMEM] * len(outs),
         out_shape=outs,
         scratch_shapes=list(scratch),
-        compiler_params=pltpu.CompilerParams(vmem_limit_bytes=24 * 1024 * 1024),
+        compiler_params=pltpu.CompilerParams(vmem_limit_bytes=grant << 20),
         cost_estimate=pl.CostEstimate(flops=flops, bytes_accessed=moved, transcendentals=0),
     )
 
@@ -373,10 +373,9 @@
     return [block, *near, *ring_far(*near, axis)]
 
 
-def slots_stacked(parts, group):
+def slots_stacked(parts):
     own, behind, ahead, *across = parts
-    layers = slice(2 * group, 2 * group + 2)
-    return jnp.stack([own[layers], behind[layers], ahead[layers], across[group]])
+    return jnp.stack([own, behind, ahead, jnp.concatenate(across, 0)])
 
 
 def local(tokens, targets, norm_gain, down_weight, up_weight, down_vector, up_vector):
@@ -392,6 +391,7 @@
             *[pltpu.VMEM((1, RANK, 128), BF16)] * 2,
             pltpu.SemaphoreType.DMA((5,)),
         ],
+        grant=60,
     )(norm_gain, down_weight, down_vector, up_weight, up_vector)
     pair = shape((LAYERS, 2, 128, RANK), BF16)
     a_own, b_own = call(order_kernel, [SMEM] + [VMEM] * 4, [pair, pair])(
@@ -405,20 +405,11 @@
     rows = jnp.where(
         core == 0, jnp.concatenate([kept, got], 1), jnp.concatenate([got, kept], 1)
     )
-    a_group, b_group = slots_stacked(a_all, 0), slots_stacked(b_all, 0)
-    a_group, b_group, rows = lax.optimization_barrier((a_group, b_group, rows))
-    groups = [(ring_gather(a_group, "x"), ring_gather(b_group, "z"))]
-    a_group, b_group = slots_stacked(a_all, 1), slots_stacked(b_all, 1)
-    a_group, b_group, groups[0] = lax.optimization_barrier((a_group, b_group, groups[0]))
-    a_near, b_near = ring_near(a_group, "x"), ring_near(b_group, "z")
+    a_all, b_all = slots_stacked(a_all), slots_stacked(b_all)
+    a_all, b_all, rows = lax.optimization_barrier((a_all, b_all, rows))
+    a_all, b_all = ring_gather(a_all, "x"), ring_gather(b_all, "z")
     h, goal = rows[0], rows[1]
     x = jnp.concatenate([h, jnp.zeros_like(h)], 0)
-
-    def a_of(layer):
-        return groups[layer // 2][0]
-
-    def b_of(layer):
-        return groups[layer // 2][1]
 
     wide = shape((2 * ROWS, HALF), BF16)
     sums = shape((ROWS, 640), F32)
@@ -430,7 +421,7 @@
 
     states, fulls, cots, e_fulls = [x], [], {}, {}
     (part,) = call(first_kernel, [VMEM] * 6, [sums], work // 3, 3 << 20)(
-        x, *a_of(0)
+        x, *a_all
     )
     for layer in range(1, LAYERS):
         x, part, full = call(
@@ -439,24 +430,16 @@
             [wide, sums, sums],
             work,
             5 << 20,
-        )(x, part, swap(part), *b_of(layer - 1), *a_of(layer))
+        )(x, part, swap(part), *b_all, *a_all)
         states.append(x)
         fulls.append(full)
-        if layer == 1:
-            part, a_near, b_near = lax.optimization_barrier((part, a_near, b_near))
-            groups.append(
-                (
-                    [a_group, *a_near, *ring_far(*a_near, "x")],
-                    [b_group, *b_near, *ring_far(*b_near, "z")],
-                )
-            )
     cot, part, full = call(
         seed_kernel,
         [VMEM] * 9,
         [wide, e_sums, sums],
         work,
         3 << 20,
-    )(x, part, swap(part), goal, *b_of(LAYERS - 1))
+    )(x, part, swap(part), goal, *b_all)
     fulls.append(full)
 
     def backward(layer, cot, e_own, e_got):
@@ -466,7 +449,7 @@
             [wide, e_sums, e_sums],
             work,
             5 << 20,
-        )(states[layer], cot, fulls[layer], e_own, e_got, *a_of(layer), *b_of(layer - 1))
+        )(states[layer], cot, fulls[layer], e_own, e_got, *a_all, *b_all)
 
     operands = []
     for layer in (3, 2, 1):

time: 240 us -> 237 us (0.988)
  starting transfers between devices: 84.2 us -> 60.2 us
  waiting for transfers between devices: 107 us -> 127 us
    ppermute x44 -> x36, waiting for transfers between devices: 99.4 us -> 119 us  [shift(): return lax.ppermute(value, axis, [(i, (i + steps) % 4) for i in range(4)])]
    ppermute x9, starting transfers between devices: 25.8 us -> 11.3 us  [swap(): return lax.ppermute(value, 'c', [(0, 1), (1, 0)])]
    ppermute x44 -> x36, starting transfers between devices: 58.4 us -> 48.9 us  [shift(): return lax.ppermute(value, axis, [(i, (i + steps) % 4) for i in range(4)])]
    unnamed x16 -> x14, local copies, waits for them, and re-layouts: 6.46 us -> 4.21 us
  transfers between devices with their start and end apart: 53 -> 45, of which waited for: 29 -> 25; matrix products, arithmetic and copies ran while one was open for 0% -> 2% of each run, Pallas kernels for 3% -> 2%
where the time goes in v3:
time: 237 us
  waiting for transfers between devices  127 us (54%)
  starting transfers between devices  60.2 us (25%)
  blocking collectives  21.1 us (9%)
  Pallas kernels  19.2 us (8%)
  local copies, waits for them, and re-layouts  6.98 us (3%)
    ppermute x36, waiting for transfers between devices, shift(): return lax.ppermute(value, axis, [(i, (i + steps) % 4) for i in range(4)])  119 us
    ppermute x36, starting transfers between devices, shift(): return lax.ppermute(value, axis, [(i, (i + steps) % 4) for i in range(4)])  48.9 us
    all_to_all x1, blocking collectives, local(): lax.all_to_all(totals, ('y', 'z', 'x', 'c'), 0, 0).reshape(128, 128)  21.1 us
    ppermute x9, starting transfers between devices, swap(): return lax.ppermute(value, 'c', [(0, 1), (1, 0)])  11.3 us
    ppermute x9, waiting for transfers between devices, swap(): return lax.ppermute(value, 'c', [(0, 1), (1, 0)])  8.06 us
  transfers between devices with their start and end apart: 45, of which 25 were waited for; matrix products, arithmetic and copies ran while one was open for 2% of the time, Pallas kernels for 2%

profile of v3, /device:TPU:1, one launch (start us, length us, event | category | flops | bytes accessed | tf_op | source)
XLA Modules:
  0.0 237.0 jit_solution(3099926968668913284)
XLA Ops:
  2.5 3.8 %collective-permute-start.2 = (bf16[4,128,256]{2,1,0:T(8,128)(2,1)}, bf16[4,128,256]{2,1,0:T(8,128)(2,1)S(1)}, u32[]{:S(2)}, u32[]{:S(2)}) collective-permute-start(bf16[4,128,256]{2,1,0:T(8,128)(2,1)} %get-tuple-element.64.own), channel_id=1, source_target_pairs={{0,64},{32,96},{64,0},{96,32},{1,65},{33,97},{65,1},{97,33},{2,66}... | collective-permute-start | bytes 786440 | tf_op jit(solution)/shard_map/ppermute | solution.py:22
  7.8 4.4 %collective-permute-done.2.across = bf16[4,128,256]{2,1,0:T(8,128)(2,1)S(1)} collective-permute-done((bf16[4,128,256]{2,1,0:T(8,128)(2,1)}, bf16[4,128,256]{2,1,0:T(8,128)(2,1)S(1)}, u32[]{:S(2)}, u32[]{:S(2)}) %collective-permute-start.2) | collective-permute-done | bytes 262176 | tf_op jit(solution)/shard_map/ppermute | solution.py:22
  12.2 6.1 %collective-permute-done.1.ahead = bf16[4,128,256]{2,1,0:T(8,128)(2,1)S(1)} collective-permute-done((bf16[4,128,256]{2,1,0:T(8,128)(2,1)}, bf16[4,128,256]{2,1,0:T(8,128)(2,1)S(1)}, u32[]{:S(2)}, u32[]{:S(2)}) %collective-permute-start.1) | collective-permute-done | bytes 262176 | tf_op jit(solution)/shard_map/ppermute | solution.py:22
  20.2 3.9 %collective-permute-start.4 = (bf16[4,2,128,256]{3,2,1,0:T(8,128)(2,1)S(1)}, bf16[4,2,128,256]{3,2,1,0:T(8,128)(2,1)S(1)}, u32[]{:S(2)}, u32[]{:S(2)}) collective-permute-start(bf16[4,2,128,256]{3,2,1,0:T(8,128)(2,1)S(1)} %get-tuple-element.65), channel_id=1, source_target_pairs={{0,24},{8,0},{16,8},{24,16},{1,25},{9,1},{17,9},{25,17},{2,26},{10... | collective-permute-start | bytes 1572872 | tf_op jit(solution)/shard_map/ppermute | solution.py:22
  24.1 2.5 %collective-permute-start.8 = (bf16[4,2,128,256]{3,2,1,0:T(8,128)(2,1)S(1)}, bf16[4,2,128,256]{3,2,1,0:T(8,128)(2,1)S(1)}, u32[]{:S(2)}, u32[]{:S(2)}) collective-permute-start(bf16[4,2,128,256]{3,2,1,0:T(8,128)(2,1)S(1)} %get-tuple-element.66), channel_id=1, source_target_pairs={{0,6},{2,0},{4,2},{6,4},{1,7},{3,1},{5,3},{7,5},{8,14},{10,8},{12,... | collective-permute-start | bytes 1572872 | tf_op jit(solution)/shard_map/ppermute | solution.py:22
  31.5 2.7 %collective-permute-done.4 = bf16[4,2,128,256]{3,2,1,0:T(8,128)(2,1)S(1)} collective-permute-done((bf16[4,2,128,256]{3,2,1,0:T(8,128)(2,1)S(1)}, bf16[4,2,128,256]{3,2,1,0:T(8,128)(2,1)S(1)}, u32[]{:S(2)}, u32[]{:S(2)}) %collective-permute-start.4) | collective-permute-done | bytes 524320 | tf_op jit(solution)/shard_map/ppermute | solution.py:22
  35.0 3.4 %collective-permute-start.6 = (bf16[2,2,128,256]{3,2,1,0:T(8,128)(2,1)}, bf16[2,2,128,256]{3,2,1,0:T(8,128)(2,1)}, u32[]{:S(2)}, u32[]{:S(2)}) collective-permute-start(bf16[2,2,128,256]{3,2,1,0:T(8,128)(2,1)} %slice.49), channel_id=1, source_target_pairs={{0,24},{8,0},{16,8},{24,16},{1,25},{9,1},{17,9},{25,17},{2,26},{10... | collective-permute-start | bytes 786440 | tf_op jit(solution)/shard_map/ppermute | solution.py:22
  40.0 2.5 %collective-permute-start.10 = (bf16[2,2,128,256]{3,2,1,0:T(8,128)(2,1)S(1)}, bf16[2,2,128,256]{3,2,1,0:T(8,128)(2,1)S(1)}, u32[]{:S(2)}, u32[]{:S(2)}) collective-permute-start(bf16[2,2,128,256]{3,2,1,0:T(8,128)(2,1)S(1)} %slice.51), channel_id=1, source_target_pairs={{0,6},{2,0},{4,2},{6,4},{1,7},{3,1},{5,3},{7,5},{8,14},{10,8},{12,... | collective-permute-start | bytes 786440 | tf_op jit(solution)/shard_map/ppermute | solution.py:22
  42.7 3.9 %collective-permute-done.5 = bf16[2,2,128,256]{3,2,1,0:T(8,128)(2,1)} collective-permute-done((bf16[2,2,128,256]{3,2,1,0:T(8,128)(2,1)}, bf16[2,2,128,256]{3,2,1,0:T(8,128)(2,1)}, u32[]{:S(2)}, u32[]{:S(2)}) %collective-permute-start.5) | collective-permute-done | bytes 262176 | tf_op jit(solution)/shard_map/ppermute | solution.py:22
  53.7 40.1 %collective-permute-done.13.refs_2_.refs_7_ = bf16[4,4,2,128,256]{4,3,2,1,0:T(8,128)(2,1)S(1)} collective-permute-done((bf16[4,4,2,128,256]{4,3,2,1,0:T(8,128)(2,1)S(1)}, bf16[4,4,2,128,256]{4,3,2,1,0:T(8,128)(2,1)S(1)}, u32[]{:S(2)}, u32[]{:S(2)}) %collective-permute-start.13) | collective-permute-done | bytes 2097184 | tf_op jit(solution)/shard_map/ppermute | solution.py:22
  98.0 17.4 %collective-permute-done.15.refs_4_.refs_9_ = bf16[2,4,2,128,256]{4,3,2,1,0:T(8,128)(2,1)S(1)} collective-permute-done((bf16[2,4,2,128,256]{4,3,2,1,0:T(8,128)(2,1)S(1)}, bf16[2,4,2,128,256]{4,3,2,1,0:T(8,128)(2,1)S(1)}, u32[]{:S(2)}, u32[]{:S(2)}) %collective-permute-start.15) | collective-permute-done | bytes 1048608 | tf_op jit(solution)/shard_map/ppermute | solution.py:22
  117.7 5.7 %collective-permute-start.16 = (f32[64,640]{1,0:T(8,128)S(1)}, f32[64,640]{1,0:T(8,128)S(1)}, u32[]{:S(2)}, u32[]{:S(2)}) collective-permute-start(f32[64,640]{1,0:T(8,128)S(1)} %shard_map.97.own_ref), channel_id=1, source_target_pairs={{0,1},{1,0},{2,3},{3,2},{4,5},{5,4},{6,7},{7,6},{8,9},{9,8},{10,11... | collective-permute-start | bytes 491528 | tf_op jit(solution)/shard_map/ppermute | solution.py:26
  145.7 2.7 %collective-permute-start.29 = (bf16[2,4,128,256]{3,2,1,0:T(8,128)(2,1)S(1)}, bf16[2,4,128,256]{3,2,1,0:T(8,128)(2,1)S(1)}, u32[]{:S(2)}, u32[]{:S(2)}) collective-permute-start(bf16[2,4,128,256]{3,2,1,0:T(8,128)(2,1)S(1)} %get-tuple-element.97), channel_id=1, source_target_pairs={{0,24},{8,0},{16,8},{24,16},{1,25},{9,1},{17,9},{25,17},{2,26},{10... | collective-permute-start | bytes 1572872 | tf_op jit(solution)/shard_map/ppermute | solution.py:22
  148.4 2.7 %collective-permute-start.31 = (bf16[2,4,128,256]{3,2,1,0:T(8,128)(2,1)S(1)}, bf16[2,4,128,256]{3,2,1,0:T(8,128)(2,1)S(1)}, u32[]{:S(2)}, u32[]{:S(2)}) collective-permute-start(bf16[2,4,128,256]{3,2,1,0:T(8,128)(2,1)S(1)} %get-tuple-element.101), channel_id=1, source_target_pairs={{0,6},{2,0},{4,2},{6,4},{1,7},{3,1},{5,3},{7,5},{8,14},{10,8},{12,... | collective-permute-start | bytes 1572872 | tf_op jit(solution)/shard_map/ppermute | solution.py:22
  153.3 6.8 %collective-permute-done.28.refs_2_ = bf16[2,4,128,256]{3,2,1,0:T(8,128)(2,1)S(1)} collective-permute-done((bf16[2,4,128,256]{3,2,1,0:T(8,128)(2,1)S(1)}, bf16[2,4,128,256]{3,2,1,0:T(8,128)(2,1)S(1)}, u32[]{:S(2)}, u32[]{:S(2)}) %collective-permute-start.28) | collective-permute-done | bytes 524320 | tf_op jit(solution)/shard_map/ppermute | solution.py:22
  162.7 2.7 %collective-permute-start.33 = (bf16[4,4,128,256]{3,2,1,0:T(8,128)(2,1)S(1)}, bf16[4,4,128,256]{3,2,1,0:T(8,128)(2,1)S(1)}, u32[]{:S(2)}, u32[]{:S(2)}) collective-permute-start(bf16[4,4,128,256]{3,2,1,0:T(8,128)(2,1)S(1)} %get-tuple-element.103), channel_id=1, source_target_pairs={{0,24},{8,0},{16,8},{24,16},{1,25},{9,1},{17,9},{25,17},{2,26},{10... | collective-permute-start | bytes 3145736 | tf_op jit(solution)/shard_map/ppermute | solution.py:22
  165.4 2.7 %collective-permute-start.38 = (bf16[4,4,128,256]{3,2,1,0:T(8,128)(2,1)S(1)}, bf16[4,4,128,256]{3,2,1,0:T(8,128)(2,1)S(1)}, u32[]{:S(2)}, u32[]{:S(2)}) collective-permute-start(bf16[4,4,128,256]{3,2,1,0:T(8,128)(2,1)S(1)} %get-tuple-element.110), channel_id=1, source_target_pairs={{0,6},{2,0},{4,2},{6,4},{1,7},{3,1},{5,3},{7,5},{8,14},{10,8},{12,... | collective-permute-start | bytes 3145736 | tf_op jit(solution)/shard_map/ppermute | solution.py:22
  168.1 18.7 %collective-permute-done.32.behind = bf16[4,4,128,256]{3,2,1,0:T(8,128)(2,1)S(1)} collective-permute-done((bf16[4,4,128,256]{3,2,1,0:T(8,128)(2,1)S(1)}, bf16[4,4,128,256]{3,2,1,0:T(8,128)(2,1)S(1)}, u32[]{:S(2)}, u32[]{:S(2)}) %collective-permute-start.32) | collective-permute-done | bytes 1048608 | tf_op jit(solution)/shard_map/ppermute | solution.py:22
  187.2 2.7 %collective-permute-start.35 = (bf16[4,128,256]{2,1,0:T(8,128)(2,1)S(1)}, bf16[4,128,256]{2,1,0:T(8,128)(2,1)S(1)}, u32[]{:S(2)}, u32[]{:S(2)}) collective-permute-start(bf16[4,128,256]{2,1,0:T(8,128)(2,1)S(1)} %get-tuple-element.106), channel_id=1, source_target_pairs={{0,6},{2,0},{4,2},{6,4},{1,7},{3,1},{5,3},{7,5},{8,14},{10,8},{12,... | collective-permute-start | bytes 786440 | tf_op jit(solution)/shard_map/ppermute | solution.py:22
  191.0 2.7 %collective-permute-start.40 = (bf16[4,128,256]{2,1,0:T(8,128)(2,1)S(1)}, bf16[4,128,256]{2,1,0:T(8,128)(2,1)S(1)}, u32[]{:S(2)}, u32[]{:S(2)}) collective-permute-start(bf16[4,128,256]{2,1,0:T(8,128)(2,1)S(1)} %get-tuple-element.113), channel_id=1, source_target_pairs={{0,24},{8,0},{16,8},{24,16},{1,25},{9,1},{17,9},{25,17},{2,26},{10... | collective-permute-start | bytes 786440 | tf_op jit(solution)/shard_map/ppermute | solution.py:22
  195.9 5.3 %collective-permute-done.36.refs_3_ = bf16[4,128,256]{2,1,0:T(8,128)(2,1)S(1)} collective-permute-done((bf16[4,128,256]{2,1,0:T(8,128)(2,1)S(1)}, bf16[4,128,256]{2,1,0:T(8,128)(2,1)S(1)}, u32[]{:S(2)}, u32[]{:S(2)}) %collective-permute-start.36) | collective-permute-done | bytes 262176 | tf_op jit(solution)/shard_map/ppermute | solution.py:22
  204.4 3.1 %collective-permute-start.42 = (bf16[256,256]{1,0:T(8,128)(2,1)S(1)}, bf16[256,256]{1,0:T(8,128)(2,1)S(1)}, u32[]{:S(2)}, u32[]{:S(2)}) collective-permute-start(bf16[256,256]{1,0:T(8,128)(2,1)S(1)} %get-tuple-element.116), channel_id=1, source_target_pairs={{0,32},{32,64},{64,96},{96,0},{1,33},{33,65},{65,97},{97,1},{2,34}... | collective-permute-start | bytes 393224 | tf_op jit(solution)/shard_map/ppermute | solution.py:22
  211.9 2.9 %collective-permute-done.44.b3 = bf16[256,256]{1,0:T(8,128)(2,1)S(1)} collective-permute-done((bf16[256,256]{1,0:T(8,128)(2,1)S(1)}, bf16[256,256]{1,0:T(8,128)(2,1)S(1)}, u32[]{:S(2)}, u32[]{:S(2)}) %collective-permute-start.44) | collective-permute-done | bytes 131104 | tf_op jit(solution)/shard_map/ppermute | solution.py:22
  215.1 21.1 %all_to_all.5 = f32[128,1,128]{2,1,0:T(1,128)S(1)} all-to-all(f32[128,1,128]{2,1,0:T(1,128)S(1)} %broadcast_in_dim.16), channel_id=1, replica_groups=mesh['y'=4,'z'=4,'x'=4,'c'=2] {'y','z','x','c'}, dimensions={0} | all-to-all | bytes 131072 | tf_op jit(solution)/shard_map/all_to_all | solution.py:491
  (119 shorter events, 65.7 us)
Async XLA Ops:
  6.3 12.1 %collective-permute-start.1 = (bf16[4,128,256]{2,1,0:T(8,128)(2,1)}, bf16[4,128,256]{2,1,0:T(8,128)(2,1)S(1)}, u32[]{:S(2)}, u32[]{:S(2)}) collective-permute-start(bf16[4,128,256]{2,1,0:T(8,128)(2,1)} %get-tuple-element.64.own), channel_id=1, source_target_pairs={{0,96},{32,0},{64,32},{96,64},{1,97},{33,1},{65,33},{97,65},{2,98}... | collective-permute-start | bytes 786440 | tf_op jit(solution)/shard_map/ppermute | solution.py:22
  7.1 11.6 %collective-permute-start = (bf16[4,128,256]{2,1,0:T(8,128)(2,1)}, bf16[4,128,256]{2,1,0:T(8,128)(2,1)S(1)}, u32[]{:S(2)}, u32[]{:S(2)}) collective-permute-start(bf16[4,128,256]{2,1,0:T(8,128)(2,1)} %get-tuple-element.64.own), channel_id=1, source_target_pairs={{0,32},{32,64},{64,96},{96,0},{1,33},{33,65},{65,97},{97,1},{2,34}... | collective-permute-start | bytes 786440 | tf_op jit(solution)/shard_map/ppermute | solution.py:22
  20.2 14.0 %collective-permute-start.4 = (bf16[4,2,128,256]{3,2,1,0:T(8,128)(2,1)S(1)}, bf16[4,2,128,256]{3,2,1,0:T(8,128)(2,1)S(1)}, u32[]{:S(2)}, u32[]{:S(2)}) collective-permute-start(bf16[4,2,128,256]{3,2,1,0:T(8,128)(2,1)S(1)} %get-tuple-element.65), channel_id=1, source_target_pairs={{0,24},{8,0},{16,8},{24,16},{1,25},{9,1},{17,9},{25,17},{2,26},{10... | collective-permute-start | bytes 1572872 | tf_op jit(solution)/shard_map/ppermute | solution.py:22
  24.1 14.2 %collective-permute-start.3 = (bf16[4,2,128,256]{3,2,1,0:T(8,128)(2,1)S(1)}, bf16[4,2,128,256]{3,2,1,0:T(8,128)(2,1)S(1)}, u32[]{:S(2)}, u32[]{:S(2)}) collective-permute-start(bf16[4,2,128,256]{3,2,1,0:T(8,128)(2,1)S(1)} %get-tuple-element.65), channel_id=1, source_target_pairs={{0,8},{8,16},{16,24},{24,0},{1,9},{9,17},{17,25},{25,1},{2,10},{10... | collective-permute-start | bytes 1572872 | tf_op jit(solution)/shard_map/ppermute | solution.py:22
  24.1 15.9 %collective-permute-start.8 = (bf16[4,2,128,256]{3,2,1,0:T(8,128)(2,1)S(1)}, bf16[4,2,128,256]{3,2,1,0:T(8,128)(2,1)S(1)}, u32[]{:S(2)}, u32[]{:S(2)}) collective-permute-start(bf16[4,2,128,256]{3,2,1,0:T(8,128)(2,1)S(1)} %get-tuple-element.66), channel_id=1, source_target_pairs={{0,6},{2,0},{4,2},{6,4},{1,7},{3,1},{5,3},{7,5},{8,14},{10,8},{12,... | collective-permute-start | bytes 1572872 | tf_op jit(solution)/shard_map/ppermute | solution.py:22
  26.6 16.0 %collective-permute-start.7 = (bf16[4,2,128,256]{3,2,1,0:T(8,128)(2,1)S(1)}, bf16[4,2,128,256]{3,2,1,0:T(8,128)(2,1)S(1)}, u32[]{:S(2)}, u32[]{:S(2)}) collective-permute-start(bf16[4,2,128,256]{3,2,1,0:T(8,128)(2,1)S(1)} %get-tuple-element.66), channel_id=1, source_target_pairs={{0,2},{2,4},{4,6},{6,0},{1,3},{3,5},{5,7},{7,1},{8,10},{10,12},{12... | collective-permute-start | bytes 1572872 | tf_op jit(solution)/shard_map/ppermute | solution.py:22
  49.8 43.9 %collective-permute-start.13 = (bf16[4,4,2,128,256]{4,3,2,1,0:T(8,128)(2,1)S(1)}, bf16[4,4,2,128,256]{4,3,2,1,0:T(8,128)(2,1)S(1)}, u32[]{:S(2)}, u32[]{:S(2)}) collective-permute-start(bf16[4,4,2,128,256]{4,3,2,1,0:T(8,128)(2,1)S(1)} %pad_maximum_fusion.refs_0_.refs_5_), channel_id=1, source_target_pairs={{0,6},{2,0},{4,2},{6,4},{1,7},{3,1},{5,3},{7,5},{8,14},{10,8},{12,... | collective-permute-start | bytes 6291464 | tf_op jit(solution)/shard_map/ppermute | solution.py:22
  50.9 45.0 %collective-permute-start.12 = (bf16[4,4,2,128,256]{4,3,2,1,0:T(8,128)(2,1)S(1)}, bf16[4,4,2,128,256]{4,3,2,1,0:T(8,128)(2,1)S(1)}, u32[]{:S(2)}, u32[]{:S(2)}) collective-permute-start(bf16[4,4,2,128,256]{4,3,2,1,0:T(8,128)(2,1)S(1)} %pad_maximum_fusion.refs_0_.refs_5_), channel_id=1, source_target_pairs={{0,2},{2,4},{4,6},{6,0},{1,3},{3,5},{5,7},{7,1},{8,10},{10,12},{12... | collective-permute-start | bytes 6291464 | tf_op jit(solution)/shard_map/ppermute | solution.py:22
  51.4 44.7 %collective-permute-start.18 = (bf16[4,4,2,128,256]{4,3,2,1,0:T(8,128)(2,1)S(1)}, bf16[4,4,2,128,256]{4,3,2,1,0:T(8,128)(2,1)S(1)}, u32[]{:S(2)}, u32[]{:S(2)}) collective-permute-start(bf16[4,4,2,128,256]{4,3,2,1,0:T(8,128)(2,1)S(1)} %pad_maximum_fusion.1.refs_0_.refs_5_), channel_id=1, source_target_pairs={{0,24},{8,0},{16,8},{24,16},{1,25},{9,1},{17,9},{25,17},{2,26},{10... | collective-permute-start | bytes 6291464 | tf_op jit(solution)/shard_map/ppermute | solution.py:22
  53.6 43.9 %collective-permute-start.17 = (bf16[4,4,2,128,256]{4,3,2,1,0:T(8,128)(2,1)S(1)}, bf16[4,4,2,128,256]{4,3,2,1,0:T(8,128)(2,1)S(1)}, u32[]{:S(2)}, u32[]{:S(2)}) collective-permute-start(bf16[4,4,2,128,256]{4,3,2,1,0:T(8,128)(2,1)S(1)} %pad_maximum_fusion.1.refs_0_.refs_5_), channel_id=1, source_target_pairs={{0,8},{8,16},{16,24},{24,0},{1,9},{9,17},{17,25},{25,1},{2,10},{10... | collective-permute-start | bytes 6291464 | tf_op jit(solution)/shard_map/ppermute | solution.py:22
  93.8 21.5 %collective-permute-start.15 = (bf16[2,4,2,128,256]{4,3,2,1,0:T(8,128)(2,1)S(1)}, bf16[2,4,2,128,256]{4,3,2,1,0:T(8,128)(2,1)S(1)}, u32[]{:S(2)}, u32[]{:S(2)}) collective-permute-start(bf16[2,4,2,128,256]{4,3,2,1,0:T(8,128)(2,1)S(1)} %slice.53), channel_id=1, source_target_pairs={{0,6},{2,0},{4,2},{6,4},{1,7},{3,1},{5,3},{7,5},{8,14},{10,8},{12,... | collective-permute-start | bytes 3145736 | tf_op jit(solution)/shard_map/ppermute | solution.py:22
  96.0 21.2 %collective-permute-start.14 = (bf16[2,4,2,128,256]{4,3,2,1,0:T(8,128)(2,1)S(1)}, bf16[2,4,2,128,256]{4,3,2,1,0:T(8,128)(2,1)S(1)}, u32[]{:S(2)}, u32[]{:S(2)}) collective-permute-start(bf16[2,4,2,128,256]{4,3,2,1,0:T(8,128)(2,1)S(1)} %slice.52), channel_id=1, source_target_pairs={{0,2},{2,4},{4,6},{6,0},{1,3},{3,5},{5,7},{7,1},{8,10},{10,12},{12... | collective-permute-start | bytes 3145736 | tf_op jit(solution)/shard_map/ppermute | solution.py:22
  96.2 27.2 %collective-permute-start.20 = (bf16[2,4,2,128,256]{4,3,2,1,0:T(8,128)(2,1)S(1)}, bf16[2,4,2,128,256]{4,3,2,1,0:T(8,128)(2,1)S(1)}, u32[]{:S(2)}, u32[]{:S(2)}) collective-permute-start(bf16[2,4,2,128,256]{4,3,2,1,0:T(8,128)(2,1)S(1)} %slice.55), channel_id=1, source_target_pairs={{0,24},{8,0},{16,8},{24,16},{1,25},{9,1},{17,9},{25,17},{2,26},{10... | collective-permute-start | bytes 3145736 | tf_op jit(solution)/shard_map/ppermute | solution.py:22
  97.7 25.7 %collective-permute-start.19 = (bf16[2,4,2,128,256]{4,3,2,1,0:T(8,128)(2,1)S(1)}, bf16[2,4,2,128,256]{4,3,2,1,0:T(8,128)(2,1)S(1)}, u32[]{:S(2)}, u32[]{:S(2)}) collective-permute-start(bf16[2,4,2,128,256]{4,3,2,1,0:T(8,128)(2,1)S(1)} %slice.54), channel_id=1, source_target_pairs={{0,8},{8,16},{16,24},{24,0},{1,9},{9,17},{17,25},{25,1},{2,10},{10... | collective-permute-start | bytes 3145736 | tf_op jit(solution)/shard_map/ppermute | solution.py:22
  145.6 14.4 %collective-permute-start.28 = (bf16[2,4,128,256]{3,2,1,0:T(8,128)(2,1)S(1)}, bf16[2,4,128,256]{3,2,1,0:T(8,128)(2,1)S(1)}, u32[]{:S(2)}, u32[]{:S(2)}) collective-permute-start(bf16[2,4,128,256]{3,2,1,0:T(8,128)(2,1)S(1)} %get-tuple-element.96), channel_id=1, source_target_pairs={{0,8},{8,16},{16,24},{24,0},{1,9},{9,17},{17,25},{25,1},{2,10},{10... | collective-permute-start | bytes 1572872 | tf_op jit(solution)/shard_map/ppermute | solution.py:22
  145.7 14.3 %collective-permute-start.29 = (bf16[2,4,128,256]{3,2,1,0:T(8,128)(2,1)S(1)}, bf16[2,4,128,256]{3,2,1,0:T(8,128)(2,1)S(1)}, u32[]{:S(2)}, u32[]{:S(2)}) collective-permute-start(bf16[2,4,128,256]{3,2,1,0:T(8,128)(2,1)S(1)} %get-tuple-element.97), channel_id=1, source_target_pairs={{0,24},{8,0},{16,8},{24,16},{1,25},{9,1},{17,9},{25,17},{2,26},{10... | collective-permute-start | bytes 1572872 | tf_op jit(solution)/shard_map/ppermute | solution.py:22
  148.4 13.7 %collective-permute-start.30 = (bf16[2,4,128,256]{3,2,1,0:T(8,128)(2,1)S(1)}, bf16[2,4,128,256]{3,2,1,0:T(8,128)(2,1)S(1)}, u32[]{:S(2)}, u32[]{:S(2)}) collective-permute-start(bf16[2,4,128,256]{3,2,1,0:T(8,128)(2,1)S(1)} %get-tuple-element.100), channel_id=1, source_target_pairs={{0,2},{2,4},{4,6},{6,0},{1,3},{3,5},{5,7},{7,1},{8,10},{10,12},{12... | collective-permute-start | bytes 1572872 | tf_op jit(solution)/shard_map/ppermute | solution.py:22
  148.4 13.7 %collective-permute-start.31 = (bf16[2,4,128,256]{3,2,1,0:T(8,128)(2,1)S(1)}, bf16[2,4,128,256]{3,2,1,0:T(8,128)(2,1)S(1)}, u32[]{:S(2)}, u32[]{:S(2)}) collective-permute-start(bf16[2,4,128,256]{3,2,1,0:T(8,128)(2,1)S(1)} %get-tuple-element.101), channel_id=1, source_target_pairs={{0,6},{2,0},{4,2},{6,4},{1,7},{3,1},{5,3},{7,5},{8,14},{10,8},{12,... | collective-permute-start | bytes 1572872 | tf_op jit(solution)/shard_map/ppermute | solution.py:22
  162.6 24.1 %collective-permute-start.32 = (bf16[4,4,128,256]{3,2,1,0:T(8,128)(2,1)S(1)}, bf16[4,4,128,256]{3,2,1,0:T(8,128)(2,1)S(1)}, u32[]{:S(2)}, u32[]{:S(2)}) collective-permute-start(bf16[4,4,128,256]{3,2,1,0:T(8,128)(2,1)S(1)} %get-tuple-element.102), channel_id=1, source_target_pairs={{0,8},{8,16},{16,24},{24,0},{1,9},{9,17},{17,25},{25,1},{2,10},{10... | collective-permute-start | bytes 3145736 | tf_op jit(solution)/shard_map/ppermute | solution.py:22
  162.7 24.0 %collective-permute-start.33 = (bf16[4,4,128,256]{3,2,1,0:T(8,128)(2,1)S(1)}, bf16[4,4,128,256]{3,2,1,0:T(8,128)(2,1)S(1)}, u32[]{:S(2)}, u32[]{:S(2)}) collective-permute-start(bf16[4,4,128,256]{3,2,1,0:T(8,128)(2,1)S(1)} %get-tuple-element.103), channel_id=1, source_target_pairs={{0,24},{8,0},{16,8},{24,16},{1,25},{9,1},{17,9},{25,17},{2,26},{10... | collective-permute-start | bytes 3145736 | tf_op jit(solution)/shard_map/ppermute | solution.py:22
  165.4 25.1 %collective-permute-start.37 = (bf16[4,4,128,256]{3,2,1,0:T(8,128)(2,1)S(1)}, bf16[4,4,128,256]{3,2,1,0:T(8,128)(2,1)S(1)}, u32[]{:S(2)}, u32[]{:S(2)}) collective-permute-start(bf16[4,4,128,256]{3,2,1,0:T(8,128)(2,1)S(1)} %get-tuple-element.109), channel_id=1, source_target_pairs={{0,2},{2,4},{4,6},{6,0},{1,3},{3,5},{5,7},{7,1},{8,10},{10,12},{12... | collective-permute-start | bytes 3145736 | tf_op jit(solution)/shard_map/ppermute | solution.py:22
  165.4 25.1 %collective-permute-start.38 = (bf16[4,4,128,256]{3,2,1,0:T(8,128)(2,1)S(1)}, bf16[4,4,128,256]{3,2,1,0:T(8,128)(2,1)S(1)}, u32[]{:S(2)}, u32[]{:S(2)}) collective-permute-start(bf16[4,4,128,256]{3,2,1,0:T(8,128)(2,1)S(1)} %get-tuple-element.110), channel_id=1, source_target_pairs={{0,6},{2,0},{4,2},{6,4},{1,7},{3,1},{5,3},{7,5},{8,14},{10,8},{12,... | collective-permute-start | bytes 3145736 | tf_op jit(solution)/shard_map/ppermute | solution.py:22
  189.9 11.4 %collective-permute-start.36 = (bf16[4,128,256]{2,1,0:T(8,128)(2,1)S(1)}, bf16[4,128,256]{2,1,0:T(8,128)(2,1)S(1)}, u32[]{:S(2)}, u32[]{:S(2)}) collective-permute-start(bf16[4,128,256]{2,1,0:T(8,128)(2,1)S(1)} %get-tuple-element.107), channel_id=1, source_target_pairs={{0,4},{2,6},{4,0},{6,2},{1,5},{3,7},{5,1},{7,3},{8,12},{10,14},{12... | collective-permute-start | bytes 786440 | tf_op jit(solution)/shard_map/ppermute | solution.py:22
  190.9 10.4 %collective-permute-start.39 = (bf16[4,128,256]{2,1,0:T(8,128)(2,1)S(1)}, bf16[4,128,256]{2,1,0:T(8,128)(2,1)S(1)}, u32[]{:S(2)}, u32[]{:S(2)}) collective-permute-start(bf16[4,128,256]{2,1,0:T(8,128)(2,1)S(1)} %get-tuple-element.112), channel_id=1, source_target_pairs={{0,8},{8,16},{16,24},{24,0},{1,9},{9,17},{17,25},{25,1},{2,10},{10... | collective-permute-start | bytes 786440 | tf_op jit(solution)/shard_map/ppermute | solution.py:22
  (28 other events, 177.6 us)

commit v4 on v3

--- a/solution.py
+++ b/solution.py
@@ -406,7 +406,7 @@
         core == 0, jnp.concatenate([kept, got], 1), jnp.concatenate([got, kept], 1)
     )
     a_all, b_all = slots_stacked(a_all), slots_stacked(b_all)
-    a_all, b_all, rows = lax.optimization_barrier((a_all, b_all, rows))
+    b_all, rows = lax.optimization_barrier((b_all, rows))
     a_all, b_all = ring_gather(a_all, "x"), ring_gather(b_all, "z")
     h, goal = rows[0], rows[1]
     x = jnp.concatenate([h, jnp.zeros_like(h)], 0)

time: 237 us -> 237 us (level)
  waiting for transfers between devices: 127 us -> 123 us
  starting transfers between devices: 60.2 us -> 63.5 us
    ppermute x36, waiting for transfers between devices: 119 us -> 115 us  [shift(): return lax.ppermute(value, axis, [(i, (i + steps) % 4) for i in range(4)])]
    ppermute x36, starting transfers between devices: 48.9 us -> 52.2 us  [shift(): return lax.ppermute(value, axis, [(i, (i + steps) % 4) for i in range(4)])]
  transfers between devices with their start and end apart: 45 -> 45, of which waited for: 25 -> 23; matrix products, arithmetic and copies ran while one was open for 2% -> 2% of each run, Pallas kernels for 2% -> 2%
where the time goes in v4:
time: 237 us
  waiting for transfers between devices  123 us (52%)
  starting transfers between devices  63.5 us (27%)
  blocking collectives  21.1 us (9%)
  Pallas kernels  19.2 us (8%)
  local copies, waits for them, and re-layouts  6.98 us (3%)
    ppermute x36, waiting for transfers between devices, shift(): return lax.ppermute(value, axis, [(i, (i + steps) % 4) for i in range(4)])  115 us
    ppermute x36, starting transfers between devices, shift(): return lax.ppermute(value, axis, [(i, (i + steps) % 4) for i in range(4)])  52.2 us
    all_to_all x1, blocking collectives, local(): lax.all_to_all(totals, ('y', 'z', 'x', 'c'), 0, 0).reshape(128, 128)  21.1 us
    ppermute x9, starting transfers between devices, swap(): return lax.ppermute(value, 'c', [(0, 1), (1, 0)])  11.3 us
    ppermute x9, waiting for transfers between devices, swap(): return lax.ppermute(value, 'c', [(0, 1), (1, 0)])  8.06 us
  transfers between devices with their start and end apart: 45, of which 23 were waited for; matrix products, arithmetic and copies ran while one was open for 2% of the time, Pallas kernels for 2%

profile of v4, /device:TPU:1, one launch (start us, length us, event | category | flops | bytes accessed | tf_op | source)
XLA Modules:
  0.0 236.7 jit_solution(561849269388855)
XLA Ops:
  2.5 3.8 %collective-permute-start.2 = (bf16[4,128,256]{2,1,0:T(8,128)(2,1)}, bf16[4,128,256]{2,1,0:T(8,128)(2,1)S(1)}, u32[]{:S(2)}, u32[]{:S(2)}) collective-permute-start(bf16[4,128,256]{2,1,0:T(8,128)(2,1)} %get-tuple-element.63.own), channel_id=1, source_target_pairs={{0,64},{32,96},{64,0},{96,32},{1,65},{33,97},{65,1},{97,33},{2,66}... | collective-permute-start | bytes 786440 | tf_op jit(solution)/shard_map/ppermute | solution.py:22
  7.8 4.4 %collective-permute-done.2.across = bf16[4,128,256]{2,1,0:T(8,128)(2,1)S(1)} collective-permute-done((bf16[4,128,256]{2,1,0:T(8,128)(2,1)}, bf16[4,128,256]{2,1,0:T(8,128)(2,1)S(1)}, u32[]{:S(2)}, u32[]{:S(2)}) %collective-permute-start.2) | collective-permute-done | bytes 262176 | tf_op jit(solution)/shard_map/ppermute | solution.py:22
  12.2 6.1 %collective-permute-done.1.ahead = bf16[4,128,256]{2,1,0:T(8,128)(2,1)S(1)} collective-permute-done((bf16[4,128,256]{2,1,0:T(8,128)(2,1)}, bf16[4,128,256]{2,1,0:T(8,128)(2,1)S(1)}, u32[]{:S(2)}, u32[]{:S(2)}) %collective-permute-start.1) | collective-permute-done | bytes 262176 | tf_op jit(solution)/shard_map/ppermute | solution.py:22
  20.2 3.9 %collective-permute-start.9 = (bf16[4,2,128,256]{3,2,1,0:T(8,128)(2,1)S(1)}, bf16[4,2,128,256]{3,2,1,0:T(8,128)(2,1)S(1)}, u32[]{:S(2)}, u32[]{:S(2)}) collective-permute-start(bf16[4,2,128,256]{3,2,1,0:T(8,128)(2,1)S(1)} %get-tuple-element.68), channel_id=1, source_target_pairs={{0,24},{8,0},{16,8},{24,16},{1,25},{9,1},{17,9},{25,17},{2,26},{10... | collective-permute-start | bytes 1572872 | tf_op jit(solution)/shard_map/ppermute | solution.py:22
  31.5 2.7 %collective-permute-done.9 = bf16[4,2,128,256]{3,2,1,0:T(8,128)(2,1)S(1)} collective-permute-done((bf16[4,2,128,256]{3,2,1,0:T(8,128)(2,1)S(1)}, bf16[4,2,128,256]{3,2,1,0:T(8,128)(2,1)S(1)}, u32[]{:S(2)}, u32[]{:S(2)}) %collective-permute-start.9) | collective-permute-done | bytes 524320 | tf_op jit(solution)/shard_map/ppermute | solution.py:22
  35.0 3.4 %collective-permute-start.11 = (bf16[2,2,128,256]{3,2,1,0:T(8,128)(2,1)}, bf16[2,2,128,256]{3,2,1,0:T(8,128)(2,1)}, u32[]{:S(2)}, u32[]{:S(2)}) collective-permute-start(bf16[2,2,128,256]{3,2,1,0:T(8,128)(2,1)} %slice.51), channel_id=1, source_target_pairs={{0,24},{8,0},{16,8},{24,16},{1,25},{9,1},{17,9},{25,17},{2,26},{10... | collective-permute-start | bytes 786440 | tf_op jit(solution)/shard_map/ppermute | solution.py:22
  40.0 2.5 %collective-permute-start.6 = (bf16[2,2,128,256]{3,2,1,0:T(8,128)(2,1)S(1)}, bf16[2,2,128,256]{3,2,1,0:T(8,128)(2,1)S(1)}, u32[]{:S(2)}, u32[]{:S(2)}) collective-permute-start(bf16[2,2,128,256]{3,2,1,0:T(8,128)(2,1)S(1)} %slice.49), channel_id=1, source_target_pairs={{0,6},{2,0},{4,2},{6,4},{1,7},{3,1},{5,3},{7,5},{8,14},{10,8},{12,... | collective-permute-start | bytes 786440 | tf_op jit(solution)/shard_map/ppermute | solution.py:22
  42.7 3.9 %collective-permute-done.10 = bf16[2,2,128,256]{3,2,1,0:T(8,128)(2,1)} collective-permute-done((bf16[2,2,128,256]{3,2,1,0:T(8,128)(2,1)}, bf16[2,2,128,256]{3,2,1,0:T(8,128)(2,1)}, u32[]{:S(2)}, u32[]{:S(2)}) %collective-permute-start.10) | collective-permute-done | bytes 262176 | tf_op jit(solution)/shard_map/ppermute | solution.py:22
  48.0 2.5 %collective-permute-start.13 = (bf16[4,4,2,128,256]{4,3,2,1,0:T(8,128)(2,1)S(1)}, bf16[4,4,2,128,256]{4,3,2,1,0:T(8,128)(2,1)S(1)}, u32[]{:S(2)}, u32[]{:S(2)}) collective-permute-start(bf16[4,4,2,128,256]{4,3,2,1,0:T(8,128)(2,1)S(1)} %pad_maximum_fusion.1.refs_0_.refs_5_), channel_id=1, source_target_pairs={{0,6},{2,0},{4,2},{6,4},{1,7},{3,1},{5,3},{7,5},{8,14},{10,8},{12,... | collective-permute-start | bytes 6291464 | tf_op jit(solution)/shard_map/ppermute | solution.py:22
  52.4 39.5 %collective-permute-done.13.refs_2_.refs_7_ = bf16[4,4,2,128,256]{4,3,2,1,0:T(8,128)(2,1)S(1)} collective-permute-done((bf16[4,4,2,128,256]{4,3,2,1,0:T(8,128)(2,1)S(1)}, bf16[4,4,2,128,256]{4,3,2,1,0:T(8,128)(2,1)S(1)}, u32[]{:S(2)}, u32[]{:S(2)}) %collective-permute-start.13) | collective-permute-done | bytes 2097184 | tf_op jit(solution)/shard_map/ppermute | solution.py:22
  92.1 3.5 %collective-permute-start.15 = (bf16[2,4,2,128,256]{4,3,2,1,0:T(8,128)(2,1)S(1)}, bf16[2,4,2,128,256]{4,3,2,1,0:T(8,128)(2,1)S(1)}, u32[]{:S(2)}, u32[]{:S(2)}) collective-permute-start(bf16[2,4,2,128,256]{4,3,2,1,0:T(8,128)(2,1)S(1)} %slice.53), channel_id=1, source_target_pairs={{0,6},{2,0},{4,2},{6,4},{1,7},{3,1},{5,3},{7,5},{8,14},{10,8},{12,... | collective-permute-start | bytes 3145736 | tf_op jit(solution)/shard_map/ppermute | solution.py:22
  98.3 15.3 %collective-permute-done.15.refs_4_.refs_9_ = bf16[2,4,2,128,256]{4,3,2,1,0:T(8,128)(2,1)S(1)} collective-permute-done((bf16[2,4,2,128,256]{4,3,2,1,0:T(8,128)(2,1)S(1)}, bf16[2,4,2,128,256]{4,3,2,1,0:T(8,128)(2,1)S(1)}, u32[]{:S(2)}, u32[]{:S(2)}) %collective-permute-start.15) | collective-permute-done | bytes 1048608 | tf_op jit(solution)/shard_map/ppermute | solution.py:22
  113.6 3.3 %collective-permute-done.14.refs_3_.refs_8_ = bf16[2,4,2,128,256]{4,3,2,1,0:T(8,128)(2,1)S(1)} collective-permute-done((bf16[2,4,2,128,256]{4,3,2,1,0:T(8,128)(2,1)S(1)}, bf16[2,4,2,128,256]{4,3,2,1,0:T(8,128)(2,1)S(1)}, u32[]{:S(2)}, u32[]{:S(2)}) %collective-permute-start.14) | collective-permute-done | bytes 1048608 | tf_op jit(solution)/shard_map/ppermute | solution.py:22
  117.3 5.7 %collective-permute-start.16 = (f32[64,640]{1,0:T(8,128)S(1)}, f32[64,640]{1,0:T(8,128)S(1)}, u32[]{:S(2)}, u32[]{:S(2)}) collective-permute-start(f32[64,640]{1,0:T(8,128)S(1)} %shard_map.97.own_ref), channel_id=1, source_target_pairs={{0,1},{1,0},{2,3},{3,2},{4,5},{5,4},{6,7},{7,6},{8,9},{9,8},{10,11... | collective-permute-start | bytes 491528 | tf_op jit(solution)/shard_map/ppermute | solution.py:26
  145.3 2.7 %collective-permute-start.29 = (bf16[2,4,128,256]{3,2,1,0:T(8,128)(2,1)S(1)}, bf16[2,4,128,256]{3,2,1,0:T(8,128)(2,1)S(1)}, u32[]{:S(2)}, u32[]{:S(2)}) collective-permute-start(bf16[2,4,128,256]{3,2,1,0:T(8,128)(2,1)S(1)} %get-tuple-element.95), channel_id=1, source_target_pairs={{0,24},{8,0},{16,8},{24,16},{1,25},{9,1},{17,9},{25,17},{2,26},{10... | collective-permute-start | bytes 1572872 | tf_op jit(solution)/shard_map/ppermute | solution.py:22
  148.0 2.7 %collective-permute-start.31 = (bf16[2,4,128,256]{3,2,1,0:T(8,128)(2,1)S(1)}, bf16[2,4,128,256]{3,2,1,0:T(8,128)(2,1)S(1)}, u32[]{:S(2)}, u32[]{:S(2)}) collective-permute-start(bf16[2,4,128,256]{3,2,1,0:T(8,128)(2,1)S(1)} %get-tuple-element.99), channel_id=1, source_target_pairs={{0,6},{2,0},{4,2},{6,4},{1,7},{3,1},{5,3},{7,5},{8,14},{10,8},{12,... | collective-permute-start | bytes 1572872 | tf_op jit(solution)/shard_map/ppermute | solution.py:22
  152.9 6.8 %collective-permute-done.28.refs_2_ = bf16[2,4,128,256]{3,2,1,0:T(8,128)(2,1)S(1)} collective-permute-done((bf16[2,4,128,256]{3,2,1,0:T(8,128)(2,1)S(1)}, bf16[2,4,128,256]{3,2,1,0:T(8,128)(2,1)S(1)}, u32[]{:S(2)}, u32[]{:S(2)}) %collective-permute-start.28) | collective-permute-done | bytes 524320 | tf_op jit(solution)/shard_map/ppermute | solution.py:22
  162.3 2.7 %collective-permute-start.33 = (bf16[4,4,128,256]{3,2,1,0:T(8,128)(2,1)S(1)}, bf16[4,4,128,256]{3,2,1,0:T(8,128)(2,1)S(1)}, u32[]{:S(2)}, u32[]{:S(2)}) collective-permute-start(bf16[4,4,128,256]{3,2,1,0:T(8,128)(2,1)S(1)} %get-tuple-element.101), channel_id=1, source_target_pairs={{0,24},{8,0},{16,8},{24,16},{1,25},{9,1},{17,9},{25,17},{2,26},{10... | collective-permute-start | bytes 3145736 | tf_op jit(solution)/shard_map/ppermute | solution.py:22
  167.7 18.7 %collective-permute-done.32.behind = bf16[4,4,128,256]{3,2,1,0:T(8,128)(2,1)S(1)} collective-permute-done((bf16[4,4,128,256]{3,2,1,0:T(8,128)(2,1)S(1)}, bf16[4,4,128,256]{3,2,1,0:T(8,128)(2,1)S(1)}, u32[]{:S(2)}, u32[]{:S(2)}) %collective-permute-start.32) | collective-permute-done | bytes 1048608 | tf_op jit(solution)/shard_map/ppermute | solution.py:22
  190.8 2.7 %collective-permute-start.40 = (bf16[4,128,256]{2,1,0:T(8,128)(2,1)S(1)}, bf16[4,128,256]{2,1,0:T(8,128)(2,1)S(1)}, u32[]{:S(2)}, u32[]{:S(2)}) collective-permute-start(bf16[4,128,256]{2,1,0:T(8,128)(2,1)S(1)} %get-tuple-element.111), channel_id=1, source_target_pairs={{0,24},{8,0},{16,8},{24,16},{1,25},{9,1},{17,9},{25,17},{2,26},{10... | collective-permute-start | bytes 786440 | tf_op jit(solution)/shard_map/ppermute | solution.py:22
  194.4 6.5 %collective-permute-done.36.refs_3_ = bf16[4,128,256]{2,1,0:T(8,128)(2,1)S(1)} collective-permute-done((bf16[4,128,256]{2,1,0:T(8,128)(2,1)S(1)}, bf16[4,128,256]{2,1,0:T(8,128)(2,1)S(1)}, u32[]{:S(2)}, u32[]{:S(2)}) %collective-permute-start.36) | collective-permute-done | bytes 262176 | tf_op jit(solution)/shard_map/ppermute | solution.py:22
  203.3 3.8 %collective-permute-start.42 = (bf16[256,256]{1,0:T(8,128)(2,1)S(1)}, bf16[256,256]{1,0:T(8,128)(2,1)S(1)}, u32[]{:S(2)}, u32[]{:S(2)}) collective-permute-start(bf16[256,256]{1,0:T(8,128)(2,1)S(1)} %get-tuple-element.114), channel_id=1, source_target_pairs={{0,32},{32,64},{64,96},{96,0},{1,33},{33,65},{65,97},{97,1},{2,34}... | collective-permute-start | bytes 393224 | tf_op jit(solution)/shard_map/ppermute | solution.py:22
  211.6 2.9 %collective-permute-done.44.b3 = bf16[256,256]{1,0:T(8,128)(2,1)S(1)} collective-permute-done((bf16[256,256]{1,0:T(8,128)(2,1)S(1)}, bf16[256,256]{1,0:T(8,128)(2,1)S(1)}, u32[]{:S(2)}, u32[]{:S(2)}) %collective-permute-start.44) | collective-permute-done | bytes 131104 | tf_op jit(solution)/shard_map/ppermute | solution.py:22
  214.7 21.1 %all_to_all.5 = f32[128,1,128]{2,1,0:T(1,128)S(1)} all-to-all(f32[128,1,128]{2,1,0:T(1,128)S(1)} %broadcast_in_dim.16), channel_id=1, replica_groups=mesh['y'=4,'z'=4,'x'=4,'c'=2] {'y','z','x','c'}, dimensions={0} | all-to-all | bytes 131072 | tf_op jit(solution)/shard_map/all_to_all | solution.py:491
  (119 shorter events, 64.7 us)
Async XLA Ops:
  6.3 12.1 %collective-permute-start.1 = (bf16[4,128,256]{2,1,0:T(8,128)(2,1)}, bf16[4,128,256]{2,1,0:T(8,128)(2,1)S(1)}, u32[]{:S(2)}, u32[]{:S(2)}) collective-permute-start(bf16[4,128,256]{2,1,0:T(8,128)(2,1)} %get-tuple-element.63.own), channel_id=1, source_target_pairs={{0,96},{32,0},{64,32},{96,64},{1,97},{33,1},{65,33},{97,65},{2,98}... | collective-permute-start | bytes 786440 | tf_op jit(solution)/shard_map/ppermute | solution.py:22
  7.1 11.6 %collective-permute-start = (bf16[4,128,256]{2,1,0:T(8,128)(2,1)}, bf16[4,128,256]{2,1,0:T(8,128)(2,1)S(1)}, u32[]{:S(2)}, u32[]{:S(2)}) collective-permute-start(bf16[4,128,256]{2,1,0:T(8,128)(2,1)} %get-tuple-element.63.own), channel_id=1, source_target_pairs={{0,32},{32,64},{64,96},{96,0},{1,33},{33,65},{65,97},{97,1},{2,34}... | collective-permute-start | bytes 786440 | tf_op jit(solution)/shard_map/ppermute | solution.py:22
  20.2 14.0 %collective-permute-start.9 = (bf16[4,2,128,256]{3,2,1,0:T(8,128)(2,1)S(1)}, bf16[4,2,128,256]{3,2,1,0:T(8,128)(2,1)S(1)}, u32[]{:S(2)}, u32[]{:S(2)}) collective-permute-start(bf16[4,2,128,256]{3,2,1,0:T(8,128)(2,1)S(1)} %get-tuple-element.68), channel_id=1, source_target_pairs={{0,24},{8,0},{16,8},{24,16},{1,25},{9,1},{17,9},{25,17},{2,26},{10... | collective-permute-start | bytes 1572872 | tf_op jit(solution)/shard_map/ppermute | solution.py:22
  24.1 14.2 %collective-permute-start.8 = (bf16[4,2,128,256]{3,2,1,0:T(8,128)(2,1)S(1)}, bf16[4,2,128,256]{3,2,1,0:T(8,128)(2,1)S(1)}, u32[]{:S(2)}, u32[]{:S(2)}) collective-permute-start(bf16[4,2,128,256]{3,2,1,0:T(8,128)(2,1)S(1)} %get-tuple-element.68), channel_id=1, source_target_pairs={{0,8},{8,16},{16,24},{24,0},{1,9},{9,17},{17,25},{25,1},{2,10},{10... | collective-permute-start | bytes 1572872 | tf_op jit(solution)/shard_map/ppermute | solution.py:22
  24.1 15.9 %collective-permute-start.4 = (bf16[4,2,128,256]{3,2,1,0:T(8,128)(2,1)S(1)}, bf16[4,2,128,256]{3,2,1,0:T(8,128)(2,1)S(1)}, u32[]{:S(2)}, u32[]{:S(2)}) collective-permute-start(bf16[4,2,128,256]{3,2,1,0:T(8,128)(2,1)S(1)} %get-tuple-element.64), channel_id=1, source_target_pairs={{0,6},{2,0},{4,2},{6,4},{1,7},{3,1},{5,3},{7,5},{8,14},{10,8},{12,... | collective-permute-start | bytes 1572872 | tf_op jit(solution)/shard_map/ppermute | solution.py:22
  26.6 16.0 %collective-permute-start.3 = (bf16[4,2,128,256]{3,2,1,0:T(8,128)(2,1)S(1)}, bf16[4,2,128,256]{3,2,1,0:T(8,128)(2,1)S(1)}, u32[]{:S(2)}, u32[]{:S(2)}) collective-permute-start(bf16[4,2,128,256]{3,2,1,0:T(8,128)(2,1)S(1)} %get-tuple-element.64), channel_id=1, source_target_pairs={{0,2},{2,4},{4,6},{6,0},{1,3},{3,5},{5,7},{7,1},{8,10},{10,12},{12... | collective-permute-start | bytes 1572872 | tf_op jit(solution)/shard_map/ppermute | solution.py:22
  40.0 10.5 %collective-permute-start.6 = (bf16[2,2,128,256]{3,2,1,0:T(8,128)(2,1)S(1)}, bf16[2,2,128,256]{3,2,1,0:T(8,128)(2,1)S(1)}, u32[]{:S(2)}, u32[]{:S(2)}) collective-permute-start(bf16[2,2,128,256]{3,2,1,0:T(8,128)(2,1)S(1)} %slice.49), channel_id=1, source_target_pairs={{0,6},{2,0},{4,2},{6,4},{1,7},{3,1},{5,3},{7,5},{8,14},{10,8},{12,... | collective-permute-start | bytes 786440 | tf_op jit(solution)/shard_map/ppermute | solution.py:22
  48.0 44.0 %collective-permute-start.13 = (bf16[4,4,2,128,256]{4,3,2,1,0:T(8,128)(2,1)S(1)}, bf16[4,4,2,128,256]{4,3,2,1,0:T(8,128)(2,1)S(1)}, u32[]{:S(2)}, u32[]{:S(2)}) collective-permute-start(bf16[4,4,2,128,256]{4,3,2,1,0:T(8,128)(2,1)S(1)} %pad_maximum_fusion.1.refs_0_.refs_5_), channel_id=1, source_target_pairs={{0,6},{2,0},{4,2},{6,4},{1,7},{3,1},{5,3},{7,5},{8,14},{10,8},{12,... | collective-permute-start | bytes 6291464 | tf_op jit(solution)/shard_map/ppermute | solution.py:22
  50.5 45.0 %collective-permute-start.12 = (bf16[4,4,2,128,256]{4,3,2,1,0:T(8,128)(2,1)S(1)}, bf16[4,4,2,128,256]{4,3,2,1,0:T(8,128)(2,1)S(1)}, u32[]{:S(2)}, u32[]{:S(2)}) collective-permute-start(bf16[4,4,2,128,256]{4,3,2,1,0:T(8,128)(2,1)S(1)} %pad_maximum_fusion.1.refs_0_.refs_5_), channel_id=1, source_target_pairs={{0,2},{2,4},{4,6},{6,0},{1,3},{3,5},{5,7},{7,1},{8,10},{10,12},{12... | collective-permute-start | bytes 6291464 | tf_op jit(solution)/shard_map/ppermute | solution.py:22
  50.9 44.8 %collective-permute-start.18 = (bf16[4,4,2,128,256]{4,3,2,1,0:T(8,128)(2,1)S(1)}, bf16[4,4,2,128,256]{4,3,2,1,0:T(8,128)(2,1)S(1)}, u32[]{:S(2)}, u32[]{:S(2)}) collective-permute-start(bf16[4,4,2,128,256]{4,3,2,1,0:T(8,128)(2,1)S(1)} %pad_maximum_fusion.refs_0_.refs_5_), channel_id=1, source_target_pairs={{0,24},{8,0},{16,8},{24,16},{1,25},{9,1},{17,9},{25,17},{2,26},{10... | collective-permute-start | bytes 6291464 | tf_op jit(solution)/shard_map/ppermute | solution.py:22
  52.2 45.9 %collective-permute-start.17 = (bf16[4,4,2,128,256]{4,3,2,1,0:T(8,128)(2,1)S(1)}, bf16[4,4,2,128,256]{4,3,2,1,0:T(8,128)(2,1)S(1)}, u32[]{:S(2)}, u32[]{:S(2)}) collective-permute-start(bf16[4,4,2,128,256]{4,3,2,1,0:T(8,128)(2,1)S(1)} %pad_maximum_fusion.refs_0_.refs_5_), channel_id=1, source_target_pairs={{0,8},{8,16},{16,24},{24,0},{1,9},{9,17},{17,25},{25,1},{2,10},{10... | collective-permute-start | bytes 6291464 | tf_op jit(solution)/shard_map/ppermute | solution.py:22
  92.1 21.5 %collective-permute-start.15 = (bf16[2,4,2,128,256]{4,3,2,1,0:T(8,128)(2,1)S(1)}, bf16[2,4,2,128,256]{4,3,2,1,0:T(8,128)(2,1)S(1)}, u32[]{:S(2)}, u32[]{:S(2)}) collective-permute-start(bf16[2,4,2,128,256]{4,3,2,1,0:T(8,128)(2,1)S(1)} %slice.53), channel_id=1, source_target_pairs={{0,6},{2,0},{4,2},{6,4},{1,7},{3,1},{5,3},{7,5},{8,14},{10,8},{12,... | collective-permute-start | bytes 3145736 | tf_op jit(solution)/shard_map/ppermute | solution.py:22
  95.6 21.2 %collective-permute-start.14 = (bf16[2,4,2,128,256]{4,3,2,1,0:T(8,128)(2,1)S(1)}, bf16[2,4,2,128,256]{4,3,2,1,0:T(8,128)(2,1)S(1)}, u32[]{:S(2)}, u32[]{:S(2)}) collective-permute-start(bf16[2,4,2,128,256]{4,3,2,1,0:T(8,128)(2,1)S(1)} %slice.52), channel_id=1, source_target_pairs={{0,2},{2,4},{4,6},{6,0},{1,3},{3,5},{5,7},{7,1},{8,10},{10,12},{12... | collective-permute-start | bytes 3145736 | tf_op jit(solution)/shard_map/ppermute | solution.py:22
  95.8 27.2 %collective-permute-start.20 = (bf16[2,4,2,128,256]{4,3,2,1,0:T(8,128)(2,1)S(1)}, bf16[2,4,2,128,256]{4,3,2,1,0:T(8,128)(2,1)S(1)}, u32[]{:S(2)}, u32[]{:S(2)}) collective-permute-start(bf16[2,4,2,128,256]{4,3,2,1,0:T(8,128)(2,1)S(1)} %slice.55), channel_id=1, source_target_pairs={{0,24},{8,0},{16,8},{24,16},{1,25},{9,1},{17,9},{25,17},{2,26},{10... | collective-permute-start | bytes 3145736 | tf_op jit(solution)/shard_map/ppermute | solution.py:22
  98.1 24.9 %collective-permute-start.19 = (bf16[2,4,2,128,256]{4,3,2,1,0:T(8,128)(2,1)S(1)}, bf16[2,4,2,128,256]{4,3,2,1,0:T(8,128)(2,1)S(1)}, u32[]{:S(2)}, u32[]{:S(2)}) collective-permute-start(bf16[2,4,2,128,256]{4,3,2,1,0:T(8,128)(2,1)S(1)} %slice.54), channel_id=1, source_target_pairs={{0,8},{8,16},{16,24},{24,0},{1,9},{9,17},{17,25},{25,1},{2,10},{10... | collective-permute-start | bytes 3145736 | tf_op jit(solution)/shard_map/ppermute | solution.py:22
  145.2 14.4 %collective-permute-start.28 = (bf16[2,4,128,256]{3,2,1,0:T(8,128)(2,1)S(1)}, bf16[2,4,128,256]{3,2,1,0:T(8,128)(2,1)S(1)}, u32[]{:S(2)}, u32[]{:S(2)}) collective-permute-start(bf16[2,4,128,256]{3,2,1,0:T(8,128)(2,1)S(1)} %get-tuple-element.94), channel_id=1, source_target_pairs={{0,8},{8,16},{16,24},{24,0},{1,9},{9,17},{17,25},{25,1},{2,10},{10... | collective-permute-start | bytes 1572872 | tf_op jit(solution)/shard_map/ppermute | solution.py:22
  145.3 14.3 %collective-permute-start.29 = (bf16[2,4,128,256]{3,2,1,0:T(8,128)(2,1)S(1)}, bf16[2,4,128,256]{3,2,1,0:T(8,128)(2,1)S(1)}, u32[]{:S(2)}, u32[]{:S(2)}) collective-permute-start(bf16[2,4,128,256]{3,2,1,0:T(8,128)(2,1)S(1)} %get-tuple-element.95), channel_id=1, source_target_pairs={{0,24},{8,0},{16,8},{24,16},{1,25},{9,1},{17,9},{25,17},{2,26},{10... | collective-permute-start | bytes 1572872 | tf_op jit(solution)/shard_map/ppermute | solution.py:22
  148.0 13.7 %collective-permute-start.30 = (bf16[2,4,128,256]{3,2,1,0:T(8,128)(2,1)S(1)}, bf16[2,4,128,256]{3,2,1,0:T(8,128)(2,1)S(1)}, u32[]{:S(2)}, u32[]{:S(2)}) collective-permute-start(bf16[2,4,128,256]{3,2,1,0:T(8,128)(2,1)S(1)} %get-tuple-element.98), channel_id=1, source_target_pairs={{0,2},{2,4},{4,6},{6,0},{1,3},{3,5},{5,7},{7,1},{8,10},{10,12},{12... | collective-permute-start | bytes 1572872 | tf_op jit(solution)/shard_map/ppermute | solution.py:22
  148.0 13.7 %collective-permute-start.31 = (bf16[2,4,128,256]{3,2,1,0:T(8,128)(2,1)S(1)}, bf16[2,4,128,256]{3,2,1,0:T(8,128)(2,1)S(1)}, u32[]{:S(2)}, u32[]{:S(2)}) collective-permute-start(bf16[2,4,128,256]{3,2,1,0:T(8,128)(2,1)S(1)} %get-tuple-element.99), channel_id=1, source_target_pairs={{0,6},{2,0},{4,2},{6,4},{1,7},{3,1},{5,3},{7,5},{8,14},{10,8},{12,... | collective-permute-start | bytes 1572872 | tf_op jit(solution)/shard_map/ppermute | solution.py:22
  162.3 24.1 %collective-permute-start.32 = (bf16[4,4,128,256]{3,2,1,0:T(8,128)(2,1)S(1)}, bf16[4,4,128,256]{3,2,1,0:T(8,128)(2,1)S(1)}, u32[]{:S(2)}, u32[]{:S(2)}) collective-permute-start(bf16[4,4,128,256]{3,2,1,0:T(8,128)(2,1)S(1)} %get-tuple-element.100), channel_id=1, source_target_pairs={{0,8},{8,16},{16,24},{24,0},{1,9},{9,17},{17,25},{25,1},{2,10},{10... | collective-permute-start | bytes 3145736 | tf_op jit(solution)/shard_map/ppermute | solution.py:22
  162.3 24.0 %collective-permute-start.33 = (bf16[4,4,128,256]{3,2,1,0:T(8,128)(2,1)S(1)}, bf16[4,4,128,256]{3,2,1,0:T(8,128)(2,1)S(1)}, u32[]{:S(2)}, u32[]{:S(2)}) collective-permute-start(bf16[4,4,128,256]{3,2,1,0:T(8,128)(2,1)S(1)} %get-tuple-element.101), channel_id=1, source_target_pairs={{0,24},{8,0},{16,8},{24,16},{1,25},{9,1},{17,9},{25,17},{2,26},{10... | collective-permute-start | bytes 3145736 | tf_op jit(solution)/shard_map/ppermute | solution.py:22
  165.0 25.3 %collective-permute-start.37 = (bf16[4,4,128,256]{3,2,1,0:T(8,128)(2,1)S(1)}, bf16[4,4,128,256]{3,2,1,0:T(8,128)(2,1)S(1)}, u32[]{:S(2)}, u32[]{:S(2)}) collective-permute-start(bf16[4,4,128,256]{3,2,1,0:T(8,128)(2,1)S(1)} %get-tuple-element.107), channel_id=1, source_target_pairs={{0,2},{2,4},{4,6},{6,0},{1,3},{3,5},{5,7},{7,1},{8,10},{10,12},{12... | collective-permute-start | bytes 3145736 | tf_op jit(solution)/shard_map/ppermute | solution.py:22
  165.9 24.5 %collective-permute-start.38 = (bf16[4,4,128,256]{3,2,1,0:T(8,128)(2,1)S(1)}, bf16[4,4,128,256]{3,2,1,0:T(8,128)(2,1)S(1)}, u32[]{:S(2)}, u32[]{:S(2)}) collective-permute-start(bf16[4,4,128,256]{3,2,1,0:T(8,128)(2,1)S(1)} %get-tuple-element.108), channel_id=1, source_target_pairs={{0,6},{2,0},{4,2},{6,4},{1,7},{3,1},{5,3},{7,5},{8,14},{10,8},{12,... | collective-permute-start | bytes 3145736 | tf_op jit(solution)/shard_map/ppermute | solution.py:22
  189.5 11.4 %collective-permute-start.36 = (bf16[4,128,256]{2,1,0:T(8,128)(2,1)S(1)}, bf16[4,128,256]{2,1,0:T(8,128)(2,1)S(1)}, u32[]{:S(2)}, u32[]{:S(2)}) collective-permute-start(bf16[4,128,256]{2,1,0:T(8,128)(2,1)S(1)} %get-tuple-element.105), channel_id=1, source_target_pairs={{0,4},{2,6},{4,0},{6,2},{1,5},{3,7},{5,1},{7,3},{8,12},{10,14},{12... | collective-permute-start | bytes 786440 | tf_op jit(solution)/shard_map/ppermute | solution.py:22
  (28 other events, 178.3 us)

commit v5 on v3

--- a/solution.py
+++ b/solution.py
@@ -94,6 +94,19 @@
         layer = (place_ref[2] + far) & 3
         a_ref[layer] = chunk[:2]
         b_ref[layer] = chunk[2:]
+
+
+def halves_kernel(behind, ahead, behind_out, ahead_out):
+    behind_out[...] = behind[:2]
+    ahead_out[...] = ahead[2:]
+
+
+def slots_kernel(own, behind, ahead, across_low, across_high, out_ref):
+    out_ref[0] = own[...]
+    out_ref[1] = behind[...]
+    out_ref[2] = ahead[...]
+    out_ref[3, :2] = across_low[...]
+    out_ref[3, 2:] = across_high[...]
 
 
 def rows_kernel(place_ref, tokens_ref, targets_ref, keep_ref, give_ref):
@@ -373,11 +386,6 @@
     return [block, *near, *ring_far(*near, axis)]
 
 
-def slots_stacked(parts):
-    own, behind, ahead, *across = parts
-    return jnp.stack([own, behind, ahead, jnp.concatenate(across, 0)])
-
-
 def local(tokens, targets, norm_gain, down_weight, up_weight, down_vector, up_vector):
     place = jnp.stack([lax.axis_index(axis) for axis in ("z", "x", "y", "c")]).astype(jnp.int32)
     core = place[3]
@@ -397,7 +405,16 @@
     a_own, b_own = call(order_kernel, [SMEM] + [VMEM] * 4, [pair, pair])(
         place, chunk, shift(chunk, "y", 1), shift(chunk, "y", -1), shift(chunk, "y", 2)
     )
-    a_all, b_all = ring_gather(a_own, "z"), ring_gather(b_own, "x")
+
+    def first_ring(own, axis):
+        near = shift(own, axis, 1), shift(own, axis, -1)
+        half = shape((2, 2, 128, RANK), BF16)
+        behind, ahead = call(halves_kernel, [VMEM] * 2, [half] * 2)(*near)
+        parts = own, *near, shift(behind, axis, 1), shift(ahead, axis, -1)
+        (stacked,) = call(slots_kernel, [VMEM] * 5, [shape((4, *own.shape), BF16)])(*parts)
+        return stacked
+
+    a_all, b_all = first_ring(a_own, "z"), first_ring(b_own, "x")
     kept, given = call(
         rows_kernel, [SMEM, VMEM, VMEM], [shape((2, 32, HALF), BF16)] * 2, moved=3 << 20
     )(place, tokens, targets)
@@ -405,7 +422,6 @@
     rows = jnp.where(
         core == 0, jnp.concatenate([kept, got], 1), jnp.concatenate([got, kept], 1)
     )
-    a_all, b_all = slots_stacked(a_all), slots_stacked(b_all)
     a_all, b_all, rows = lax.optimization_barrier((a_all, b_all, rows))
     a_all, b_all = ring_gather(a_all, "x"), ring_gather(b_all, "z")
     h, goal = rows[0], rows[1]

time: 237 us -> 237 us (level)
  Pallas kernels: 19.2 us -> 23.5 us
  waiting for transfers between devices: 127 us -> 124 us
    pallas_call x0 -> x4, Pallas kernels: none -> 3.91 us  [the longest x2 2.25 us: first_ring(): call(slots_kernel, [VMEM] * 5, [shape((4, *own.shape), BF16)])(*parts)]
    ppermute x36, waiting for transfers between devices: 119 us -> 116 us  [shift(): return lax.ppermute(value, axis, [(i, (i + steps) % 4) for i in range(4)])]
  transfers between devices with their start and end apart: 45 -> 45, of which waited for: 25 -> 25; matrix products, arithmetic and copies ran while one was open for 2% -> 1% of each run, Pallas kernels for 2% -> 3%
where the time goes in v5:
time: 237 us; the launch traced here: 236 us
  waiting for transfers between devices  124 us (52%)
  starting transfers between devices  59.7 us (25%)
  Pallas kernels  23.5 us (10%)
  blocking collectives  21.8 us (9%)
  local copies, waits for them, and re-layouts  4.71 us (2%)
    ppermute x36, waiting for transfers between devices, shift(): return lax.ppermute(value, axis, [(i, (i + steps) % 4) for i in range(4)])  116 us
    ppermute x36, starting transfers between devices, shift(): return lax.ppermute(value, axis, [(i, (i + steps) % 4) for i in range(4)])  48.2 us
    all_to_all x1, blocking collectives, local(): lax.all_to_all(totals, ('y', 'z', 'x', 'c'), 0, 0).reshape(128, 128)  21.8 us
    ppermute x9, starting transfers between devices, swap(): return lax.ppermute(value, 'c', [(0, 1), (1, 0)])  11.5 us
    ppermute x9, waiting for transfers between devices, swap(): return lax.ppermute(value, 'c', [(0, 1), (1, 0)])  8.07 us
  transfers between devices with their start and end apart: 45, of which 25 were waited for; matrix products, arithmetic and copies ran while one was open for 1% of the time, Pallas kernels for 3%

profile of v5, /device:TPU:1, one launch (start us, length us, event | category | flops | bytes accessed | tf_op | source)
XLA Modules:
  0.0 236.2 jit_solution(8519800511415419951)
XLA Ops:
  2.5 3.8 %collective-permute-start.2 = (bf16[4,128,256]{2,1,0:T(8,128)(2,1)}, bf16[4,128,256]{2,1,0:T(8,128)(2,1)S(1)}, u32[]{:S(2)}, u32[]{:S(2)}) collective-permute-start(bf16[4,128,256]{2,1,0:T(8,128)(2,1)} %get-tuple-element.68.own), channel_id=1, source_target_pairs={{0,64},{32,96},{64,0},{96,32},{1,65},{33,97},{65,1},{97,33},{2,66}... | collective-permute-start | bytes 786440 | tf_op jit(solution)/shard_map/ppermute | solution.py:22
  7.8 4.4 %collective-permute-done.2.across = bf16[4,128,256]{2,1,0:T(8,128)(2,1)S(1)} collective-permute-done((bf16[4,128,256]{2,1,0:T(8,128)(2,1)}, bf16[4,128,256]{2,1,0:T(8,128)(2,1)S(1)}, u32[]{:S(2)}, u32[]{:S(2)}) %collective-permute-start.2) | collective-permute-done | bytes 262176 | tf_op jit(solution)/shard_map/ppermute | solution.py:22
  12.3 6.1 %collective-permute-done.1.ahead = bf16[4,128,256]{2,1,0:T(8,128)(2,1)S(1)} collective-permute-done((bf16[4,128,256]{2,1,0:T(8,128)(2,1)}, bf16[4,128,256]{2,1,0:T(8,128)(2,1)S(1)}, u32[]{:S(2)}, u32[]{:S(2)}) %collective-permute-start.1) | collective-permute-done | bytes 262176 | tf_op jit(solution)/shard_map/ppermute | solution.py:22
  20.2 3.9 %collective-permute-start.4 = (bf16[4,2,128,256]{3,2,1,0:T(8,128)(2,1)S(1)}, bf16[4,2,128,256]{3,2,1,0:T(8,128)(2,1)S(1)}, u32[]{:S(2)}, u32[]{:S(2)}) collective-permute-start(bf16[4,2,128,256]{3,2,1,0:T(8,128)(2,1)S(1)} %get-tuple-element.69.own), channel_id=1, source_target_pairs={{0,24},{8,0},{16,8},{24,16},{1,25},{9,1},{17,9},{25,17},{2,26},{10... | collective-permute-start | bytes 1572872 | tf_op jit(solution)/shard_map/ppermute | solution.py:22
  24.1 2.5 %collective-permute-start.8 = (bf16[4,2,128,256]{3,2,1,0:T(8,128)(2,1)S(1)}, bf16[4,2,128,256]{3,2,1,0:T(8,128)(2,1)S(1)}, u32[]{:S(2)}, u32[]{:S(2)}) collective-permute-start(bf16[4,2,128,256]{3,2,1,0:T(8,128)(2,1)S(1)} %get-tuple-element.72.own), channel_id=1, source_target_pairs={{0,6},{2,0},{4,2},{6,4},{1,7},{3,1},{5,3},{7,5},{8,14},{10,8},{12,... | collective-permute-start | bytes 1572872 | tf_op jit(solution)/shard_map/ppermute | solution.py:22
  34.2 3.1 %collective-permute-done.3.behind = bf16[4,2,128,256]{3,2,1,0:T(8,128)(2,1)S(1)} collective-permute-done((bf16[4,2,128,256]{3,2,1,0:T(8,128)(2,1)S(1)}, bf16[4,2,128,256]{3,2,1,0:T(8,128)(2,1)S(1)}, u32[]{:S(2)}, u32[]{:S(2)}) %collective-permute-start.3) | collective-permute-done | bytes 524320 | tf_op jit(solution)/shard_map/ppermute | solution.py:22
  38.2 2.7 %collective-permute-start.6 = (bf16[2,2,128,256]{3,2,1,0:T(8,128)(2,1)}, bf16[2,2,128,256]{3,2,1,0:T(8,128)(2,1)}, u32[]{:S(2)}, u32[]{:S(2)}) collective-permute-start(bf16[2,2,128,256]{3,2,1,0:T(8,128)(2,1)} %get-tuple-element.71), channel_id=1, source_target_pairs={{0,24},{8,0},{16,8},{24,16},{1,25},{9,1},{17,9},{25,17},{2,26},{10... | collective-permute-start | bytes 786440 | tf_op jit(solution)/shard_map/ppermute | solution.py:22
  49.6 2.7 %collective-permute-start.13 = (bf16[4,4,2,128,256]{4,3,2,1,0:T(8,128)(2,1)S(1)}, bf16[4,4,2,128,256]{4,3,2,1,0:T(8,128)(2,1)S(1)}, u32[]{:S(2)}, u32[]{:S(2)}) collective-permute-start(bf16[4,4,2,128,256]{4,3,2,1,0:T(8,128)(2,1)S(1)} %shard_map.97.refs_0_.refs_5_), channel_id=1, source_target_pairs={{0,6},{2,0},{4,2},{6,4},{1,7},{3,1},{5,3},{7,5},{8,14},{10,8},{12,... | collective-permute-start | bytes 6291464 | tf_op jit(solution)/shard_map/ppermute | solution.py:22
  53.9 39.2 %collective-permute-done.13.refs_2_.refs_7_ = bf16[4,4,2,128,256]{4,3,2,1,0:T(8,128)(2,1)S(1)} collective-permute-done((bf16[4,4,2,128,256]{4,3,2,1,0:T(8,128)(2,1)S(1)}, bf16[4,4,2,128,256]{4,3,2,1,0:T(8,128)(2,1)S(1)}, u32[]{:S(2)}, u32[]{:S(2)}) %collective-permute-start.13) | collective-permute-done | bytes 2097184 | tf_op jit(solution)/shard_map/ppermute | solution.py:22
  93.1 3.5 %collective-permute-start.15 = (bf16[2,4,2,128,256]{4,3,2,1,0:T(8,128)(2,1)S(1)}, bf16[2,4,2,128,256]{4,3,2,1,0:T(8,128)(2,1)S(1)}, u32[]{:S(2)}, u32[]{:S(2)}) collective-permute-start(bf16[2,4,2,128,256]{4,3,2,1,0:T(8,128)(2,1)S(1)} %slice.33), channel_id=1, source_target_pairs={{0,6},{2,0},{4,2},{6,4},{1,7},{3,1},{5,3},{7,5},{8,14},{10,8},{12,... | collective-permute-start | bytes 3145736 | tf_op jit(solution)/shard_map/ppermute | solution.py:22
  98.9 15.8 %collective-permute-done.15.refs_4_.refs_9_ = bf16[2,4,2,128,256]{4,3,2,1,0:T(8,128)(2,1)S(1)} collective-permute-done((bf16[2,4,2,128,256]{4,3,2,1,0:T(8,128)(2,1)S(1)}, bf16[2,4,2,128,256]{4,3,2,1,0:T(8,128)(2,1)S(1)}, u32[]{:S(2)}, u32[]{:S(2)}) %collective-permute-start.15) | collective-permute-done | bytes 1048608 | tf_op jit(solution)/shard_map/ppermute | solution.py:22
  114.6 3.0 %collective-permute-done.14.refs_3_.refs_8_ = bf16[2,4,2,128,256]{4,3,2,1,0:T(8,128)(2,1)S(1)} collective-permute-done((bf16[2,4,2,128,256]{4,3,2,1,0:T(8,128)(2,1)S(1)}, bf16[2,4,2,128,256]{4,3,2,1,0:T(8,128)(2,1)S(1)}, u32[]{:S(2)}, u32[]{:S(2)}) %collective-permute-start.14) | collective-permute-done | bytes 1048608 | tf_op jit(solution)/shard_map/ppermute | solution.py:22
  118.1 6.6 %collective-permute-start.16 = (f32[64,640]{1,0:T(8,128)S(1)}, f32[64,640]{1,0:T(8,128)S(1)}, u32[]{:S(2)}, u32[]{:S(2)}) collective-permute-start(f32[64,640]{1,0:T(8,128)S(1)} %shard_map.101.own_ref), channel_id=1, source_target_pairs={{0,1},{1,0},{2,3},{3,2},{4,5},{5,4},{6,7},{7,6},{8,9},{9,8},{10,11... | collective-permute-start | bytes 491528 | tf_op jit(solution)/shard_map/ppermute | solution.py:26
  146.2 2.7 %collective-permute-start.29 = (bf16[2,4,128,256]{3,2,1,0:T(8,128)(2,1)S(1)}, bf16[2,4,128,256]{3,2,1,0:T(8,128)(2,1)S(1)}, u32[]{:S(2)}, u32[]{:S(2)}) collective-permute-start(bf16[2,4,128,256]{3,2,1,0:T(8,128)(2,1)S(1)} %get-tuple-element.105), channel_id=1, source_target_pairs={{0,24},{8,0},{16,8},{24,16},{1,25},{9,1},{17,9},{25,17},{2,26},{10... | collective-permute-start | bytes 1572872 | tf_op jit(solution)/shard_map/ppermute | solution.py:22
  148.9 2.7 %collective-permute-start.31 = (bf16[2,4,128,256]{3,2,1,0:T(8,128)(2,1)S(1)}, bf16[2,4,128,256]{3,2,1,0:T(8,128)(2,1)S(1)}, u32[]{:S(2)}, u32[]{:S(2)}) collective-permute-start(bf16[2,4,128,256]{3,2,1,0:T(8,128)(2,1)S(1)} %get-tuple-element.109), channel_id=1, source_target_pairs={{0,6},{2,0},{4,2},{6,4},{1,7},{3,1},{5,3},{7,5},{8,14},{10,8},{12,... | collective-permute-start | bytes 1572872 | tf_op jit(solution)/shard_map/ppermute | solution.py:22
  153.7 6.9 %collective-permute-done.28.refs_2_ = bf16[2,4,128,256]{3,2,1,0:T(8,128)(2,1)S(1)} collective-permute-done((bf16[2,4,128,256]{3,2,1,0:T(8,128)(2,1)S(1)}, bf16[2,4,128,256]{3,2,1,0:T(8,128)(2,1)S(1)}, u32[]{:S(2)}, u32[]{:S(2)}) %collective-permute-start.28) | collective-permute-done | bytes 524320 | tf_op jit(solution)/shard_map/ppermute | solution.py:22
  163.2 2.7 %collective-permute-start.33 = (bf16[4,4,128,256]{3,2,1,0:T(8,128)(2,1)S(1)}, bf16[4,4,128,256]{3,2,1,0:T(8,128)(2,1)S(1)}, u32[]{:S(2)}, u32[]{:S(2)}) collective-permute-start(bf16[4,4,128,256]{3,2,1,0:T(8,128)(2,1)S(1)} %get-tuple-element.111), channel_id=1, source_target_pairs={{0,24},{8,0},{16,8},{24,16},{1,25},{9,1},{17,9},{25,17},{2,26},{10... | collective-permute-start | bytes 3145736 | tf_op jit(solution)/shard_map/ppermute | solution.py:22
  166.2 2.3 collective-permute-start.38
  168.6 18.7 %collective-permute-done.32.behind = bf16[4,4,128,256]{3,2,1,0:T(8,128)(2,1)S(1)} collective-permute-done((bf16[4,4,128,256]{3,2,1,0:T(8,128)(2,1)S(1)}, bf16[4,4,128,256]{3,2,1,0:T(8,128)(2,1)S(1)}, u32[]{:S(2)}, u32[]{:S(2)}) %collective-permute-start.32) | collective-permute-done | bytes 1048608 | tf_op jit(solution)/shard_map/ppermute | solution.py:22
  188.1 2.3 collective-permute-start.35
  191.5 2.7 %collective-permute-start.40 = (bf16[4,128,256]{2,1,0:T(8,128)(2,1)S(1)}, bf16[4,128,256]{2,1,0:T(8,128)(2,1)S(1)}, u32[]{:S(2)}, u32[]{:S(2)}) collective-permute-start(bf16[4,128,256]{2,1,0:T(8,128)(2,1)S(1)} %get-tuple-element.121), channel_id=1, source_target_pairs={{0,24},{8,0},{16,8},{24,16},{1,25},{9,1},{17,9},{25,17},{2,26},{10... | collective-permute-start | bytes 786440 | tf_op jit(solution)/shard_map/ppermute | solution.py:22
  196.2 5.6 %collective-permute-done.36.refs_3_ = bf16[4,128,256]{2,1,0:T(8,128)(2,1)S(1)} collective-permute-done((bf16[4,128,256]{2,1,0:T(8,128)(2,1)S(1)}, bf16[4,128,256]{2,1,0:T(8,128)(2,1)S(1)}, u32[]{:S(2)}, u32[]{:S(2)}) %collective-permute-start.36) | collective-permute-done | bytes 262176 | tf_op jit(solution)/shard_map/ppermute | solution.py:22
  210.5 2.9 %collective-permute-done.44.b3 = bf16[256,256]{1,0:T(8,128)(2,1)S(1)} collective-permute-done((bf16[256,256]{1,0:T(8,128)(2,1)S(1)}, bf16[256,256]{1,0:T(8,128)(2,1)S(1)}, u32[]{:S(2)}, u32[]{:S(2)}) %collective-permute-start.44) | collective-permute-done | bytes 131104 | tf_op jit(solution)/shard_map/ppermute | solution.py:22
  213.6 21.8 %all_to_all.5 = f32[128,1,128]{2,1,0:T(1,128)S(1)} all-to-all(f32[128,1,128]{2,1,0:T(1,128)S(1)} %broadcast_in_dim.16), channel_id=1, replica_groups=mesh['y'=4,'z'=4,'x'=4,'c'=2] {'y','z','x','c'}, dimensions={0} | all-to-all | bytes 131072 | tf_op jit(solution)/shard_map/all_to_all | solution.py:507
  (113 shorter events, 66.9 us)
Async XLA Ops:
  6.3 12.1 %collective-permute-start.1 = (bf16[4,128,256]{2,1,0:T(8,128)(2,1)}, bf16[4,128,256]{2,1,0:T(8,128)(2,1)S(1)}, u32[]{:S(2)}, u32[]{:S(2)}) collective-permute-start(bf16[4,128,256]{2,1,0:T(8,128)(2,1)} %get-tuple-element.68.own), channel_id=1, source_target_pairs={{0,96},{32,0},{64,32},{96,64},{1,97},{33,1},{65,33},{97,65},{2,98}... | collective-permute-start | bytes 786440 | tf_op jit(solution)/shard_map/ppermute | solution.py:22
  7.1 11.6 %collective-permute-start = (bf16[4,128,256]{2,1,0:T(8,128)(2,1)}, bf16[4,128,256]{2,1,0:T(8,128)(2,1)S(1)}, u32[]{:S(2)}, u32[]{:S(2)}) collective-permute-start(bf16[4,128,256]{2,1,0:T(8,128)(2,1)} %get-tuple-element.68.own), channel_id=1, source_target_pairs={{0,32},{32,64},{64,96},{96,0},{1,33},{33,65},{65,97},{97,1},{2,34}... | collective-permute-start | bytes 786440 | tf_op jit(solution)/shard_map/ppermute | solution.py:22
  20.2 14.0 %collective-permute-start.4 = (bf16[4,2,128,256]{3,2,1,0:T(8,128)(2,1)S(1)}, bf16[4,2,128,256]{3,2,1,0:T(8,128)(2,1)S(1)}, u32[]{:S(2)}, u32[]{:S(2)}) collective-permute-start(bf16[4,2,128,256]{3,2,1,0:T(8,128)(2,1)S(1)} %get-tuple-element.69.own), channel_id=1, source_target_pairs={{0,24},{8,0},{16,8},{24,16},{1,25},{9,1},{17,9},{25,17},{2,26},{10... | collective-permute-start | bytes 1572872 | tf_op jit(solution)/shard_map/ppermute | solution.py:22
  24.1 13.3 %collective-permute-start.3 = (bf16[4,2,128,256]{3,2,1,0:T(8,128)(2,1)S(1)}, bf16[4,2,128,256]{3,2,1,0:T(8,128)(2,1)S(1)}, u32[]{:S(2)}, u32[]{:S(2)}) collective-permute-start(bf16[4,2,128,256]{3,2,1,0:T(8,128)(2,1)S(1)} %get-tuple-element.69.own), channel_id=1, source_target_pairs={{0,8},{8,16},{16,24},{24,0},{1,9},{9,17},{17,25},{25,1},{2,10},{10... | collective-permute-start | bytes 1572872 | tf_op jit(solution)/shard_map/ppermute | solution.py:22
  24.1 16.8 %collective-permute-start.8 = (bf16[4,2,128,256]{3,2,1,0:T(8,128)(2,1)S(1)}, bf16[4,2,128,256]{3,2,1,0:T(8,128)(2,1)S(1)}, u32[]{:S(2)}, u32[]{:S(2)}) collective-permute-start(bf16[4,2,128,256]{3,2,1,0:T(8,128)(2,1)S(1)} %get-tuple-element.72.own), channel_id=1, source_target_pairs={{0,6},{2,0},{4,2},{6,4},{1,7},{3,1},{5,3},{7,5},{8,14},{10,8},{12,... | collective-permute-start | bytes 1572872 | tf_op jit(solution)/shard_map/ppermute | solution.py:22
  26.6 14.3 %collective-permute-start.7 = (bf16[4,2,128,256]{3,2,1,0:T(8,128)(2,1)S(1)}, bf16[4,2,128,256]{3,2,1,0:T(8,128)(2,1)S(1)}, u32[]{:S(2)}, u32[]{:S(2)}) collective-permute-start(bf16[4,2,128,256]{3,2,1,0:T(8,128)(2,1)S(1)} %get-tuple-element.72.own), channel_id=1, source_target_pairs={{0,2},{2,4},{4,6},{6,0},{1,3},{3,5},{5,7},{7,1},{8,10},{10,12},{12... | collective-permute-start | bytes 1572872 | tf_op jit(solution)/shard_map/ppermute | solution.py:22
  30.5 14.0 %collective-permute-start.11 = (bf16[2,32,2048]{2,1,0:T(8,128)(2,1)}, bf16[2,32,2048]{2,1,0:T(8,128)(2,1)}, u32[]{:S(2)}, u32[]{:S(2)}) collective-permute-start(bf16[2,32,2048]{2,1,0:T(8,128)(2,1)} %get-tuple-element.76), channel_id=1, source_target_pairs={{0,1},{1,0},{2,3},{3,2},{4,5},{5,4},{6,7},{7,6},{8,9},{9,8},{10,11... | collective-permute-start | bytes 786440 | tf_op jit(solution)/shard_map/ppermute | solution.py:26
  49.6 43.4 %collective-permute-start.13 = (bf16[4,4,2,128,256]{4,3,2,1,0:T(8,128)(2,1)S(1)}, bf16[4,4,2,128,256]{4,3,2,1,0:T(8,128)(2,1)S(1)}, u32[]{:S(2)}, u32[]{:S(2)}) collective-permute-start(bf16[4,4,2,128,256]{4,3,2,1,0:T(8,128)(2,1)S(1)} %shard_map.97.refs_0_.refs_5_), channel_id=1, source_target_pairs={{0,6},{2,0},{4,2},{6,4},{1,7},{3,1},{5,3},{7,5},{8,14},{10,8},{12,... | collective-permute-start | bytes 6291464 | tf_op jit(solution)/shard_map/ppermute | solution.py:22
  52.4 44.2 %collective-permute-start.12 = (bf16[4,4,2,128,256]{4,3,2,1,0:T(8,128)(2,1)S(1)}, bf16[4,4,2,128,256]{4,3,2,1,0:T(8,128)(2,1)S(1)}, u32[]{:S(2)}, u32[]{:S(2)}) collective-permute-start(bf16[4,4,2,128,256]{4,3,2,1,0:T(8,128)(2,1)S(1)} %shard_map.97.refs_0_.refs_5_), channel_id=1, source_target_pairs={{0,2},{2,4},{4,6},{6,0},{1,3},{3,5},{5,7},{7,1},{8,10},{10,12},{12... | collective-permute-start | bytes 6291464 | tf_op jit(solution)/shard_map/ppermute | solution.py:22
  52.4 44.4 %collective-permute-start.18 = (bf16[4,4,2,128,256]{4,3,2,1,0:T(8,128)(2,1)S(1)}, bf16[4,4,2,128,256]{4,3,2,1,0:T(8,128)(2,1)S(1)}, u32[]{:S(2)}, u32[]{:S(2)}) collective-permute-start(bf16[4,4,2,128,256]{4,3,2,1,0:T(8,128)(2,1)S(1)} %shard_map.99.refs_0_.refs_5_), channel_id=1, source_target_pairs={{0,24},{8,0},{16,8},{24,16},{1,25},{9,1},{17,9},{25,17},{2,26},{10... | collective-permute-start | bytes 6291464 | tf_op jit(solution)/shard_map/ppermute | solution.py:22
  53.8 44.8 %collective-permute-start.17 = (bf16[4,4,2,128,256]{4,3,2,1,0:T(8,128)(2,1)S(1)}, bf16[4,4,2,128,256]{4,3,2,1,0:T(8,128)(2,1)S(1)}, u32[]{:S(2)}, u32[]{:S(2)}) collective-permute-start(bf16[4,4,2,128,256]{4,3,2,1,0:T(8,128)(2,1)S(1)} %shard_map.99.refs_0_.refs_5_), channel_id=1, source_target_pairs={{0,8},{8,16},{16,24},{24,0},{1,9},{9,17},{17,25},{25,1},{2,10},{10... | collective-permute-start | bytes 6291464 | tf_op jit(solution)/shard_map/ppermute | solution.py:22
  93.1 21.5 %collective-permute-start.15 = (bf16[2,4,2,128,256]{4,3,2,1,0:T(8,128)(2,1)S(1)}, bf16[2,4,2,128,256]{4,3,2,1,0:T(8,128)(2,1)S(1)}, u32[]{:S(2)}, u32[]{:S(2)}) collective-permute-start(bf16[2,4,2,128,256]{4,3,2,1,0:T(8,128)(2,1)S(1)} %slice.33), channel_id=1, source_target_pairs={{0,6},{2,0},{4,2},{6,4},{1,7},{3,1},{5,3},{7,5},{8,14},{10,8},{12,... | collective-permute-start | bytes 3145736 | tf_op jit(solution)/shard_map/ppermute | solution.py:22
  96.7 20.9 %collective-permute-start.14 = (bf16[2,4,2,128,256]{4,3,2,1,0:T(8,128)(2,1)S(1)}, bf16[2,4,2,128,256]{4,3,2,1,0:T(8,128)(2,1)S(1)}, u32[]{:S(2)}, u32[]{:S(2)}) collective-permute-start(bf16[2,4,2,128,256]{4,3,2,1,0:T(8,128)(2,1)S(1)} %slice.32), channel_id=1, source_target_pairs={{0,2},{2,4},{4,6},{6,0},{1,3},{3,5},{5,7},{7,1},{8,10},{10,12},{12... | collective-permute-start | bytes 3145736 | tf_op jit(solution)/shard_map/ppermute | solution.py:22
  96.9 27.8 %collective-permute-start.20 = (bf16[2,4,2,128,256]{4,3,2,1,0:T(8,128)(2,1)S(1)}, bf16[2,4,2,128,256]{4,3,2,1,0:T(8,128)(2,1)S(1)}, u32[]{:S(2)}, u32[]{:S(2)}) collective-permute-start(bf16[2,4,2,128,256]{4,3,2,1,0:T(8,128)(2,1)S(1)} %slice.35), channel_id=1, source_target_pairs={{0,24},{8,0},{16,8},{24,16},{1,25},{9,1},{17,9},{25,17},{2,26},{10... | collective-permute-start | bytes 3145736 | tf_op jit(solution)/shard_map/ppermute | solution.py:22
  98.7 26.0 %collective-permute-start.19 = (bf16[2,4,2,128,256]{4,3,2,1,0:T(8,128)(2,1)S(1)}, bf16[2,4,2,128,256]{4,3,2,1,0:T(8,128)(2,1)S(1)}, u32[]{:S(2)}, u32[]{:S(2)}) collective-permute-start(bf16[2,4,2,128,256]{4,3,2,1,0:T(8,128)(2,1)S(1)} %slice.34), channel_id=1, source_target_pairs={{0,8},{8,16},{16,24},{24,0},{1,9},{9,17},{17,25},{25,1},{2,10},{10... | collective-permute-start | bytes 3145736 | tf_op jit(solution)/shard_map/ppermute | solution.py:22
  146.1 14.4 %collective-permute-start.28 = (bf16[2,4,128,256]{3,2,1,0:T(8,128)(2,1)S(1)}, bf16[2,4,128,256]{3,2,1,0:T(8,128)(2,1)S(1)}, u32[]{:S(2)}, u32[]{:S(2)}) collective-permute-start(bf16[2,4,128,256]{3,2,1,0:T(8,128)(2,1)S(1)} %get-tuple-element.104), channel_id=1, source_target_pairs={{0,8},{8,16},{16,24},{24,0},{1,9},{9,17},{17,25},{25,1},{2,10},{10... | collective-permute-start | bytes 1572872 | tf_op jit(solution)/shard_map/ppermute | solution.py:22
  146.2 14.3 %collective-permute-start.29 = (bf16[2,4,128,256]{3,2,1,0:T(8,128)(2,1)S(1)}, bf16[2,4,128,256]{3,2,1,0:T(8,128)(2,1)S(1)}, u32[]{:S(2)}, u32[]{:S(2)}) collective-permute-start(bf16[2,4,128,256]{3,2,1,0:T(8,128)(2,1)S(1)} %get-tuple-element.105), channel_id=1, source_target_pairs={{0,24},{8,0},{16,8},{24,16},{1,25},{9,1},{17,9},{25,17},{2,26},{10... | collective-permute-start | bytes 1572872 | tf_op jit(solution)/shard_map/ppermute | solution.py:22
  148.9 13.7 %collective-permute-start.30 = (bf16[2,4,128,256]{3,2,1,0:T(8,128)(2,1)S(1)}, bf16[2,4,128,256]{3,2,1,0:T(8,128)(2,1)S(1)}, u32[]{:S(2)}, u32[]{:S(2)}) collective-permute-start(bf16[2,4,128,256]{3,2,1,0:T(8,128)(2,1)S(1)} %get-tuple-element.108), channel_id=1, source_target_pairs={{0,2},{2,4},{4,6},{6,0},{1,3},{3,5},{5,7},{7,1},{8,10},{10,12},{12... | collective-permute-start | bytes 1572872 | tf_op jit(solution)/shard_map/ppermute | solution.py:22
  148.9 13.7 %collective-permute-start.31 = (bf16[2,4,128,256]{3,2,1,0:T(8,128)(2,1)S(1)}, bf16[2,4,128,256]{3,2,1,0:T(8,128)(2,1)S(1)}, u32[]{:S(2)}, u32[]{:S(2)}) collective-permute-start(bf16[2,4,128,256]{3,2,1,0:T(8,128)(2,1)S(1)} %get-tuple-element.109), channel_id=1, source_target_pairs={{0,6},{2,0},{4,2},{6,4},{1,7},{3,1},{5,3},{7,5},{8,14},{10,8},{12,... | collective-permute-start | bytes 1572872 | tf_op jit(solution)/shard_map/ppermute | solution.py:22
  163.2 24.1 %collective-permute-start.32 = (bf16[4,4,128,256]{3,2,1,0:T(8,128)(2,1)S(1)}, bf16[4,4,128,256]{3,2,1,0:T(8,128)(2,1)S(1)}, u32[]{:S(2)}, u32[]{:S(2)}) collective-permute-start(bf16[4,4,128,256]{3,2,1,0:T(8,128)(2,1)S(1)} %get-tuple-element.110), channel_id=1, source_target_pairs={{0,8},{8,16},{16,24},{24,0},{1,9},{9,17},{17,25},{25,1},{2,10},{10... | collective-permute-start | bytes 3145736 | tf_op jit(solution)/shard_map/ppermute | solution.py:22
  163.2 24.0 %collective-permute-start.33 = (bf16[4,4,128,256]{3,2,1,0:T(8,128)(2,1)S(1)}, bf16[4,4,128,256]{3,2,1,0:T(8,128)(2,1)S(1)}, u32[]{:S(2)}, u32[]{:S(2)}) collective-permute-start(bf16[4,4,128,256]{3,2,1,0:T(8,128)(2,1)S(1)} %get-tuple-element.111), channel_id=1, source_target_pairs={{0,24},{8,0},{16,8},{24,16},{1,25},{9,1},{17,9},{25,17},{2,26},{10... | collective-permute-start | bytes 3145736 | tf_op jit(solution)/shard_map/ppermute | solution.py:22
  165.9 25.1 %collective-permute-start.37 = (bf16[4,4,128,256]{3,2,1,0:T(8,128)(2,1)S(1)}, bf16[4,4,128,256]{3,2,1,0:T(8,128)(2,1)S(1)}, u32[]{:S(2)}, u32[]{:S(2)}) collective-permute-start(bf16[4,4,128,256]{3,2,1,0:T(8,128)(2,1)S(1)} %get-tuple-element.117), channel_id=1, source_target_pairs={{0,2},{2,4},{4,6},{6,0},{1,3},{3,5},{5,7},{7,1},{8,10},{10,12},{12... | collective-permute-start | bytes 3145736 | tf_op jit(solution)/shard_map/ppermute | solution.py:22
  166.2 24.7 %collective-permute-start.38 = (bf16[4,4,128,256]{3,2,1,0:T(8,128)(2,1)S(1)}, bf16[4,4,128,256]{3,2,1,0:T(8,128)(2,1)S(1)}, u32[]{:S(2)}, u32[]{:S(2)}) collective-permute-start(bf16[4,4,128,256]{3,2,1,0:T(8,128)(2,1)S(1)} %get-tuple-element.118), channel_id=1, source_target_pairs={{0,6},{2,0},{4,2},{6,4},{1,7},{3,1},{5,3},{7,5},{8,14},{10,8},{12,... | collective-permute-start | bytes 3145736 | tf_op jit(solution)/shard_map/ppermute | solution.py:22
  190.4 11.4 %collective-permute-start.36 = (bf16[4,128,256]{2,1,0:T(8,128)(2,1)S(1)}, bf16[4,128,256]{2,1,0:T(8,128)(2,1)S(1)}, u32[]{:S(2)}, u32[]{:S(2)}) collective-permute-start(bf16[4,128,256]{2,1,0:T(8,128)(2,1)S(1)} %get-tuple-element.115), channel_id=1, source_target_pairs={{0,4},{2,6},{4,0},{6,2},{1,5},{3,7},{5,1},{7,3},{8,12},{10,14},{12... | collective-permute-start | bytes 786440 | tf_op jit(solution)/shard_map/ppermute | solution.py:22
  (27 other events, 171.1 us)

commit v6 on v5

--- a/solution.py
+++ b/solution.py
@@ -68,12 +68,12 @@
 FARS = (0, 3, 1, 2)
 
 
-def chunk_kernel(gain_hbm, down_hbm, vector_hbm, up_hbm, up_vector_hbm, *refs):
-    chunk_ref, column_ref, gain_ref, down_ref, vector_ref, up_ref, up_vector_ref, sems = refs
+def chunk_kernel(gain_ref, down_hbm, vector_hbm, up_hbm, up_vector_hbm, *refs):
+    chunk_ref, column_ref, down_ref, vector_ref, up_ref, up_vector_ref, sems = refs
     copies = [
         pltpu.make_async_copy(source, target, sems.at[i])
         for i, (source, target) in enumerate(
-            zip((gain_hbm, down_hbm, vector_hbm, up_hbm, up_vector_hbm), refs[2:7])
+            zip((down_hbm, vector_hbm, up_hbm, up_vector_hbm), refs[2:6])
         )
     ]
     for copy in copies:
@@ -391,13 +391,12 @@
     core = place[3]
     chunk, column = call(
         chunk_kernel,
-        [ANY] * 5,
+        [VMEM] + [ANY] * 4,
         [shape((4, 128, RANK), BF16), shape((128, 128), F32)],
         scratch=[
-            pltpu.VMEM((1, 128), BF16),
             *[pltpu.VMEM((1, 128, RANK), BF16)] * 2,
             *[pltpu.VMEM((1, RANK, 128), BF16)] * 2,
-            pltpu.SemaphoreType.DMA((5,)),
+            pltpu.SemaphoreType.DMA((4,)),
         ],
         grant=60,
     )(norm_gain, down_weight, down_vector, up_weight, up_vector)

time: 237 us -> 237 us (level)
  no operation moved by 1% of the time
where the time goes in v6:
time: 237 us
  waiting for transfers between devices  124 us (52%)
  starting transfers between devices  59.7 us (25%)
  Pallas kernels  24.1 us (10%)
  blocking collectives  21.8 us (9%)
  local copies, waits for them, and re-layouts  4.71 us (2%)
    ppermute x36, waiting for transfers between devices, shift(): return lax.ppermute(value, axis, [(i, (i + steps) % 4) for i in range(4)])  116 us
    ppermute x36, starting transfers between devices, shift(): return lax.ppermute(value, axis, [(i, (i + steps) % 4) for i in range(4)])  48.2 us
    all_to_all x1, blocking collectives, local(): lax.all_to_all(totals, ('y', 'z', 'x', 'c'), 0, 0).reshape(128, 128)  21.8 us
    ppermute x9, starting transfers between devices, swap(): return lax.ppermute(value, 'c', [(0, 1), (1, 0)])  11.5 us
    ppermute x9, waiting for transfers between devices, swap(): return lax.ppermute(value, 'c', [(0, 1), (1, 0)])  8.07 us
  transfers between devices with their start and end apart: 45, of which 25 were waited for; matrix products, arithmetic and copies ran while one was open for 1% of the time, Pallas kernels for 3%

profile of v6, /device:TPU:1, one launch (start us, length us, event | category | flops | bytes accessed | tf_op | source)
XLA Modules:
  0.0 236.9 jit_solution(858299284475198900)
XLA Ops:
  0.6 2.5 %shard_map.94 = (bf16[4,128,256]{2,1,0:T(8,128)(2,1)}, f32[128,128]{1,0:T(8,128)}) custom-call(bf16[1,128]{1,0:T(2,128)(2,1)} %gain_ref.1, bf16[1,128,256]{2,1,0:T(8,128)(2,1)} %down_hbm.1, bf16[1,128,256]{2,1,0:T(8,128)(2,1)} %vector_hbm.1, bf16[1,256,128]{2,1,0:T(8,128)(2,1)} %up_hbm.1, bf16[1,256,128]{2,1,0:T(8,128)(2,1)} %up_vector_hbm.1), custom_call_target="tpu_custom_call" | custom-call | flops 1048576 | bytes 1048576 | tf_op jit(solution)/shard_map/pallas_call | solution.py:392
  3.1 3.8 %collective-permute-start.2 = (bf16[4,128,256]{2,1,0:T(8,128)(2,1)}, bf16[4,128,256]{2,1,0:T(8,128)(2,1)S(1)}, u32[]{:S(2)}, u32[]{:S(2)}) collective-permute-start(bf16[4,128,256]{2,1,0:T(8,128)(2,1)} %get-tuple-element.68.own), channel_id=1, source_target_pairs={{0,64},{32,96},{64,0},{96,32},{1,65},{33,97},{65,1},{97,33},{2,66}... | collective-permute-start | bytes 786440 | tf_op jit(solution)/shard_map/ppermute | solution.py:22
  8.5 4.4 %collective-permute-done.2.across = bf16[4,128,256]{2,1,0:T(8,128)(2,1)S(1)} collective-permute-done((bf16[4,128,256]{2,1,0:T(8,128)(2,1)}, bf16[4,128,256]{2,1,0:T(8,128)(2,1)S(1)}, u32[]{:S(2)}, u32[]{:S(2)}) %collective-permute-start.2) | collective-permute-done | bytes 262176 | tf_op jit(solution)/shard_map/ppermute | solution.py:22
  12.9 6.1 %collective-permute-done.1.ahead = bf16[4,128,256]{2,1,0:T(8,128)(2,1)S(1)} collective-permute-done((bf16[4,128,256]{2,1,0:T(8,128)(2,1)}, bf16[4,128,256]{2,1,0:T(8,128)(2,1)S(1)}, u32[]{:S(2)}, u32[]{:S(2)}) %collective-permute-start.1) | collective-permute-done | bytes 262176 | tf_op jit(solution)/shard_map/ppermute | solution.py:22
  20.9 3.9 %collective-permute-start.4 = (bf16[4,2,128,256]{3,2,1,0:T(8,128)(2,1)S(1)}, bf16[4,2,128,256]{3,2,1,0:T(8,128)(2,1)S(1)}, u32[]{:S(2)}, u32[]{:S(2)}) collective-permute-start(bf16[4,2,128,256]{3,2,1,0:T(8,128)(2,1)S(1)} %get-tuple-element.69.own), channel_id=1, source_target_pairs={{0,24},{8,0},{16,8},{24,16},{1,25},{9,1},{17,9},{25,17},{2,26},{10... | collective-permute-start | bytes 1572872 | tf_op jit(solution)/shard_map/ppermute | solution.py:22
  24.8 2.5 %collective-permute-start.8 = (bf16[4,2,128,256]{3,2,1,0:T(8,128)(2,1)S(1)}, bf16[4,2,128,256]{3,2,1,0:T(8,128)(2,1)S(1)}, u32[]{:S(2)}, u32[]{:S(2)}) collective-permute-start(bf16[4,2,128,256]{3,2,1,0:T(8,128)(2,1)S(1)} %get-tuple-element.72.own), channel_id=1, source_target_pairs={{0,6},{2,0},{4,2},{6,4},{1,7},{3,1},{5,3},{7,5},{8,14},{10,8},{12,... | collective-permute-start | bytes 1572872 | tf_op jit(solution)/shard_map/ppermute | solution.py:22
  34.9 3.1 %collective-permute-done.3.behind = bf16[4,2,128,256]{3,2,1,0:T(8,128)(2,1)S(1)} collective-permute-done((bf16[4,2,128,256]{3,2,1,0:T(8,128)(2,1)S(1)}, bf16[4,2,128,256]{3,2,1,0:T(8,128)(2,1)S(1)}, u32[]{:S(2)}, u32[]{:S(2)}) %collective-permute-start.3) | collective-permute-done | bytes 524320 | tf_op jit(solution)/shard_map/ppermute | solution.py:22
  38.8 2.7 %collective-permute-start.6 = (bf16[2,2,128,256]{3,2,1,0:T(8,128)(2,1)}, bf16[2,2,128,256]{3,2,1,0:T(8,128)(2,1)}, u32[]{:S(2)}, u32[]{:S(2)}) collective-permute-start(bf16[2,2,128,256]{3,2,1,0:T(8,128)(2,1)} %get-tuple-element.71), channel_id=1, source_target_pairs={{0,24},{8,0},{16,8},{24,16},{1,25},{9,1},{17,9},{25,17},{2,26},{10... | collective-permute-start | bytes 786440 | tf_op jit(solution)/shard_map/ppermute | solution.py:22
  50.3 2.7 %collective-permute-start.13 = (bf16[4,4,2,128,256]{4,3,2,1,0:T(8,128)(2,1)S(1)}, bf16[4,4,2,128,256]{4,3,2,1,0:T(8,128)(2,1)S(1)}, u32[]{:S(2)}, u32[]{:S(2)}) collective-permute-start(bf16[4,4,2,128,256]{4,3,2,1,0:T(8,128)(2,1)S(1)} %shard_map.97.refs_0_.refs_5_), channel_id=1, source_target_pairs={{0,6},{2,0},{4,2},{6,4},{1,7},{3,1},{5,3},{7,5},{8,14},{10,8},{12,... | collective-permute-start | bytes 6291464 | tf_op jit(solution)/shard_map/ppermute | solution.py:22
  54.5 39.2 %collective-permute-done.13.refs_2_.refs_7_ = bf16[4,4,2,128,256]{4,3,2,1,0:T(8,128)(2,1)S(1)} collective-permute-done((bf16[4,4,2,128,256]{4,3,2,1,0:T(8,128)(2,1)S(1)}, bf16[4,4,2,128,256]{4,3,2,1,0:T(8,128)(2,1)S(1)}, u32[]{:S(2)}, u32[]{:S(2)}) %collective-permute-start.13) | collective-permute-done | bytes 2097184 | tf_op jit(solution)/shard_map/ppermute | solution.py:22
  93.7 3.5 %collective-permute-start.15 = (bf16[2,4,2,128,256]{4,3,2,1,0:T(8,128)(2,1)S(1)}, bf16[2,4,2,128,256]{4,3,2,1,0:T(8,128)(2,1)S(1)}, u32[]{:S(2)}, u32[]{:S(2)}) collective-permute-start(bf16[2,4,2,128,256]{4,3,2,1,0:T(8,128)(2,1)S(1)} %slice.33), channel_id=1, source_target_pairs={{0,6},{2,0},{4,2},{6,4},{1,7},{3,1},{5,3},{7,5},{8,14},{10,8},{12,... | collective-permute-start | bytes 3145736 | tf_op jit(solution)/shard_map/ppermute | solution.py:22
  99.5 15.8 %collective-permute-done.15.refs_4_.refs_9_ = bf16[2,4,2,128,256]{4,3,2,1,0:T(8,128)(2,1)S(1)} collective-permute-done((bf16[2,4,2,128,256]{4,3,2,1,0:T(8,128)(2,1)S(1)}, bf16[2,4,2,128,256]{4,3,2,1,0:T(8,128)(2,1)S(1)}, u32[]{:S(2)}, u32[]{:S(2)}) %collective-permute-start.15) | collective-permute-done | bytes 1048608 | tf_op jit(solution)/shard_map/ppermute | solution.py:22
  115.3 3.0 %collective-permute-done.14.refs_3_.refs_8_ = bf16[2,4,2,128,256]{4,3,2,1,0:T(8,128)(2,1)S(1)} collective-permute-done((bf16[2,4,2,128,256]{4,3,2,1,0:T(8,128)(2,1)S(1)}, bf16[2,4,2,128,256]{4,3,2,1,0:T(8,128)(2,1)S(1)}, u32[]{:S(2)}, u32[]{:S(2)}) %collective-permute-start.14) | collective-permute-done | bytes 1048608 | tf_op jit(solution)/shard_map/ppermute | solution.py:22
  118.7 6.6 %collective-permute-start.16 = (f32[64,640]{1,0:T(8,128)S(1)}, f32[64,640]{1,0:T(8,128)S(1)}, u32[]{:S(2)}, u32[]{:S(2)}) collective-permute-start(f32[64,640]{1,0:T(8,128)S(1)} %shard_map.101.own_ref), channel_id=1, source_target_pairs={{0,1},{1,0},{2,3},{3,2},{4,5},{5,4},{6,7},{7,6},{8,9},{9,8},{10,11... | collective-permute-start | bytes 491528 | tf_op jit(solution)/shard_map/ppermute | solution.py:26
  146.9 2.7 %collective-permute-start.29 = (bf16[2,4,128,256]{3,2,1,0:T(8,128)(2,1)S(1)}, bf16[2,4,128,256]{3,2,1,0:T(8,128)(2,1)S(1)}, u32[]{:S(2)}, u32[]{:S(2)}) collective-permute-start(bf16[2,4,128,256]{3,2,1,0:T(8,128)(2,1)S(1)} %get-tuple-element.105), channel_id=1, source_target_pairs={{0,24},{8,0},{16,8},{24,16},{1,25},{9,1},{17,9},{25,17},{2,26},{10... | collective-permute-start | bytes 1572872 | tf_op jit(solution)/shard_map/ppermute | solution.py:22
  149.5 2.7 %collective-permute-start.31 = (bf16[2,4,128,256]{3,2,1,0:T(8,128)(2,1)S(1)}, bf16[2,4,128,256]{3,2,1,0:T(8,128)(2,1)S(1)}, u32[]{:S(2)}, u32[]{:S(2)}) collective-permute-start(bf16[2,4,128,256]{3,2,1,0:T(8,128)(2,1)S(1)} %get-tuple-element.109), channel_id=1, source_target_pairs={{0,6},{2,0},{4,2},{6,4},{1,7},{3,1},{5,3},{7,5},{8,14},{10,8},{12,... | collective-permute-start | bytes 1572872 | tf_op jit(solution)/shard_map/ppermute | solution.py:22
  154.3 6.9 %collective-permute-done.28.refs_2_ = bf16[2,4,128,256]{3,2,1,0:T(8,128)(2,1)S(1)} collective-permute-done((bf16[2,4,128,256]{3,2,1,0:T(8,128)(2,1)S(1)}, bf16[2,4,128,256]{3,2,1,0:T(8,128)(2,1)S(1)}, u32[]{:S(2)}, u32[]{:S(2)}) %collective-permute-start.28) | collective-permute-done | bytes 524320 | tf_op jit(solution)/shard_map/ppermute | solution.py:22
  163.9 2.7 %collective-permute-start.33 = (bf16[4,4,128,256]{3,2,1,0:T(8,128)(2,1)S(1)}, bf16[4,4,128,256]{3,2,1,0:T(8,128)(2,1)S(1)}, u32[]{:S(2)}, u32[]{:S(2)}) collective-permute-start(bf16[4,4,128,256]{3,2,1,0:T(8,128)(2,1)S(1)} %get-tuple-element.111), channel_id=1, source_target_pairs={{0,24},{8,0},{16,8},{24,16},{1,25},{9,1},{17,9},{25,17},{2,26},{10... | collective-permute-start | bytes 3145736 | tf_op jit(solution)/shard_map/ppermute | solution.py:22
  166.9 2.3 collective-permute-start.38
  169.2 18.7 %collective-permute-done.32.behind = bf16[4,4,128,256]{3,2,1,0:T(8,128)(2,1)S(1)} collective-permute-done((bf16[4,4,128,256]{3,2,1,0:T(8,128)(2,1)S(1)}, bf16[4,4,128,256]{3,2,1,0:T(8,128)(2,1)S(1)}, u32[]{:S(2)}, u32[]{:S(2)}) %collective-permute-start.32) | collective-permute-done | bytes 1048608 | tf_op jit(solution)/shard_map/ppermute | solution.py:22
  192.1 2.7 %collective-permute-start.40 = (bf16[4,128,256]{2,1,0:T(8,128)(2,1)S(1)}, bf16[4,128,256]{2,1,0:T(8,128)(2,1)S(1)}, u32[]{:S(2)}, u32[]{:S(2)}) collective-permute-start(bf16[4,128,256]{2,1,0:T(8,128)(2,1)S(1)} %get-tuple-element.121), channel_id=1, source_target_pairs={{0,24},{8,0},{16,8},{24,16},{1,25},{9,1},{17,9},{25,17},{2,26},{10... | collective-permute-start | bytes 786440 | tf_op jit(solution)/shard_map/ppermute | solution.py:22
  196.8 5.6 %collective-permute-done.36.refs_3_ = bf16[4,128,256]{2,1,0:T(8,128)(2,1)S(1)} collective-permute-done((bf16[4,128,256]{2,1,0:T(8,128)(2,1)S(1)}, bf16[4,128,256]{2,1,0:T(8,128)(2,1)S(1)}, u32[]{:S(2)}, u32[]{:S(2)}) %collective-permute-start.36) | collective-permute-done | bytes 262176 | tf_op jit(solution)/shard_map/ppermute | solution.py:22
  211.1 2.9 %collective-permute-done.44.b3 = bf16[256,256]{1,0:T(8,128)(2,1)S(1)} collective-permute-done((bf16[256,256]{1,0:T(8,128)(2,1)S(1)}, bf16[256,256]{1,0:T(8,128)(2,1)S(1)}, u32[]{:S(2)}, u32[]{:S(2)}) %collective-permute-start.44) | collective-permute-done | bytes 131104 | tf_op jit(solution)/shard_map/ppermute | solution.py:22
  214.3 21.8 %all_to_all.5 = f32[128,1,128]{2,1,0:T(1,128)S(1)} all-to-all(f32[128,1,128]{2,1,0:T(1,128)S(1)} %broadcast_in_dim.16), channel_id=1, replica_groups=mesh['y'=4,'z'=4,'x'=4,'c'=2] {'y','z','x','c'}, dimensions={0} | all-to-all | bytes 131072 | tf_op jit(solution)/shard_map/all_to_all | solution.py:506
  (113 shorter events, 67.4 us)
Async XLA Ops:
  6.9 12.1 %collective-permute-start.1 = (bf16[4,128,256]{2,1,0:T(8,128)(2,1)}, bf16[4,128,256]{2,1,0:T(8,128)(2,1)S(1)}, u32[]{:S(2)}, u32[]{:S(2)}) collective-permute-start(bf16[4,128,256]{2,1,0:T(8,128)(2,1)} %get-tuple-element.68.own), channel_id=1, source_target_pairs={{0,96},{32,0},{64,32},{96,64},{1,97},{33,1},{65,33},{97,65},{2,98}... | collective-permute-start | bytes 786440 | tf_op jit(solution)/shard_map/ppermute | solution.py:22
  7.7 11.6 %collective-permute-start = (bf16[4,128,256]{2,1,0:T(8,128)(2,1)}, bf16[4,128,256]{2,1,0:T(8,128)(2,1)S(1)}, u32[]{:S(2)}, u32[]{:S(2)}) collective-permute-start(bf16[4,128,256]{2,1,0:T(8,128)(2,1)} %get-tuple-element.68.own), channel_id=1, source_target_pairs={{0,32},{32,64},{64,96},{96,0},{1,33},{33,65},{65,97},{97,1},{2,34}... | collective-permute-start | bytes 786440 | tf_op jit(solution)/shard_map/ppermute | solution.py:22
  20.9 14.0 %collective-permute-start.4 = (bf16[4,2,128,256]{3,2,1,0:T(8,128)(2,1)S(1)}, bf16[4,2,128,256]{3,2,1,0:T(8,128)(2,1)S(1)}, u32[]{:S(2)}, u32[]{:S(2)}) collective-permute-start(bf16[4,2,128,256]{3,2,1,0:T(8,128)(2,1)S(1)} %get-tuple-element.69.own), channel_id=1, source_target_pairs={{0,24},{8,0},{16,8},{24,16},{1,25},{9,1},{17,9},{25,17},{2,26},{10... | collective-permute-start | bytes 1572872 | tf_op jit(solution)/shard_map/ppermute | solution.py:22
  24.8 13.3 %collective-permute-start.3 = (bf16[4,2,128,256]{3,2,1,0:T(8,128)(2,1)S(1)}, bf16[4,2,128,256]{3,2,1,0:T(8,128)(2,1)S(1)}, u32[]{:S(2)}, u32[]{:S(2)}) collective-permute-start(bf16[4,2,128,256]{3,2,1,0:T(8,128)(2,1)S(1)} %get-tuple-element.69.own), channel_id=1, source_target_pairs={{0,8},{8,16},{16,24},{24,0},{1,9},{9,17},{17,25},{25,1},{2,10},{10... | collective-permute-start | bytes 1572872 | tf_op jit(solution)/shard_map/ppermute | solution.py:22
  24.8 16.8 %collective-permute-start.8 = (bf16[4,2,128,256]{3,2,1,0:T(8,128)(2,1)S(1)}, bf16[4,2,128,256]{3,2,1,0:T(8,128)(2,1)S(1)}, u32[]{:S(2)}, u32[]{:S(2)}) collective-permute-start(bf16[4,2,128,256]{3,2,1,0:T(8,128)(2,1)S(1)} %get-tuple-element.72.own), channel_id=1, source_target_pairs={{0,6},{2,0},{4,2},{6,4},{1,7},{3,1},{5,3},{7,5},{8,14},{10,8},{12,... | collective-permute-start | bytes 1572872 | tf_op jit(solution)/shard_map/ppermute | solution.py:22
  27.2 14.3 %collective-permute-start.7 = (bf16[4,2,128,256]{3,2,1,0:T(8,128)(2,1)S(1)}, bf16[4,2,128,256]{3,2,1,0:T(8,128)(2,1)S(1)}, u32[]{:S(2)}, u32[]{:S(2)}) collective-permute-start(bf16[4,2,128,256]{3,2,1,0:T(8,128)(2,1)S(1)} %get-tuple-element.72.own), channel_id=1, source_target_pairs={{0,2},{2,4},{4,6},{6,0},{1,3},{3,5},{5,7},{7,1},{8,10},{10,12},{12... | collective-permute-start | bytes 1572872 | tf_op jit(solution)/shard_map/ppermute | solution.py:22
  31.1 14.0 %collective-permute-start.11 = (bf16[2,32,2048]{2,1,0:T(8,128)(2,1)}, bf16[2,32,2048]{2,1,0:T(8,128)(2,1)}, u32[]{:S(2)}, u32[]{:S(2)}) collective-permute-start(bf16[2,32,2048]{2,1,0:T(8,128)(2,1)} %get-tuple-element.76), channel_id=1, source_target_pairs={{0,1},{1,0},{2,3},{3,2},{4,5},{5,4},{6,7},{7,6},{8,9},{9,8},{10,11... | collective-permute-start | bytes 786440 | tf_op jit(solution)/shard_map/ppermute | solution.py:26
  50.3 43.4 %collective-permute-start.13 = (bf16[4,4,2,128,256]{4,3,2,1,0:T(8,128)(2,1)S(1)}, bf16[4,4,2,128,256]{4,3,2,1,0:T(8,128)(2,1)S(1)}, u32[]{:S(2)}, u32[]{:S(2)}) collective-permute-start(bf16[4,4,2,128,256]{4,3,2,1,0:T(8,128)(2,1)S(1)} %shard_map.97.refs_0_.refs_5_), channel_id=1, source_target_pairs={{0,6},{2,0},{4,2},{6,4},{1,7},{3,1},{5,3},{7,5},{8,14},{10,8},{12,... | collective-permute-start | bytes 6291464 | tf_op jit(solution)/shard_map/ppermute | solution.py:22
  53.0 44.2 %collective-permute-start.12 = (bf16[4,4,2,128,256]{4,3,2,1,0:T(8,128)(2,1)S(1)}, bf16[4,4,2,128,256]{4,3,2,1,0:T(8,128)(2,1)S(1)}, u32[]{:S(2)}, u32[]{:S(2)}) collective-permute-start(bf16[4,4,2,128,256]{4,3,2,1,0:T(8,128)(2,1)S(1)} %shard_map.97.refs_0_.refs_5_), channel_id=1, source_target_pairs={{0,2},{2,4},{4,6},{6,0},{1,3},{3,5},{5,7},{7,1},{8,10},{10,12},{12... | collective-permute-start | bytes 6291464 | tf_op jit(solution)/shard_map/ppermute | solution.py:22
  53.0 44.4 %collective-permute-start.18 = (bf16[4,4,2,128,256]{4,3,2,1,0:T(8,128)(2,1)S(1)}, bf16[4,4,2,128,256]{4,3,2,1,0:T(8,128)(2,1)S(1)}, u32[]{:S(2)}, u32[]{:S(2)}) collective-permute-start(bf16[4,4,2,128,256]{4,3,2,1,0:T(8,128)(2,1)S(1)} %shard_map.99.refs_0_.refs_5_), channel_id=1, source_target_pairs={{0,24},{8,0},{16,8},{24,16},{1,25},{9,1},{17,9},{25,17},{2,26},{10... | collective-permute-start | bytes 6291464 | tf_op jit(solution)/shard_map/ppermute | solution.py:22
  54.4 44.8 %collective-permute-start.17 = (bf16[4,4,2,128,256]{4,3,2,1,0:T(8,128)(2,1)S(1)}, bf16[4,4,2,128,256]{4,3,2,1,0:T(8,128)(2,1)S(1)}, u32[]{:S(2)}, u32[]{:S(2)}) collective-permute-start(bf16[4,4,2,128,256]{4,3,2,1,0:T(8,128)(2,1)S(1)} %shard_map.99.refs_0_.refs_5_), channel_id=1, source_target_pairs={{0,8},{8,16},{16,24},{24,0},{1,9},{9,17},{17,25},{25,1},{2,10},{10... | collective-permute-start | bytes 6291464 | tf_op jit(solution)/shard_map/ppermute | solution.py:22
  93.7 21.5 %collective-permute-start.15 = (bf16[2,4,2,128,256]{4,3,2,1,0:T(8,128)(2,1)S(1)}, bf16[2,4,2,128,256]{4,3,2,1,0:T(8,128)(2,1)S(1)}, u32[]{:S(2)}, u32[]{:S(2)}) collective-permute-start(bf16[2,4,2,128,256]{4,3,2,1,0:T(8,128)(2,1)S(1)} %slice.33), channel_id=1, source_target_pairs={{0,6},{2,0},{4,2},{6,4},{1,7},{3,1},{5,3},{7,5},{8,14},{10,8},{12,... | collective-permute-start | bytes 3145736 | tf_op jit(solution)/shard_map/ppermute | solution.py:22
  97.3 20.9 %collective-permute-start.14 = (bf16[2,4,2,128,256]{4,3,2,1,0:T(8,128)(2,1)S(1)}, bf16[2,4,2,128,256]{4,3,2,1,0:T(8,128)(2,1)S(1)}, u32[]{:S(2)}, u32[]{:S(2)}) collective-permute-start(bf16[2,4,2,128,256]{4,3,2,1,0:T(8,128)(2,1)S(1)} %slice.32), channel_id=1, source_target_pairs={{0,2},{2,4},{4,6},{6,0},{1,3},{3,5},{5,7},{7,1},{8,10},{10,12},{12... | collective-permute-start | bytes 3145736 | tf_op jit(solution)/shard_map/ppermute | solution.py:22
  97.5 27.8 %collective-permute-start.20 = (bf16[2,4,2,128,256]{4,3,2,1,0:T(8,128)(2,1)S(1)}, bf16[2,4,2,128,256]{4,3,2,1,0:T(8,128)(2,1)S(1)}, u32[]{:S(2)}, u32[]{:S(2)}) collective-permute-start(bf16[2,4,2,128,256]{4,3,2,1,0:T(8,128)(2,1)S(1)} %slice.35), channel_id=1, source_target_pairs={{0,24},{8,0},{16,8},{24,16},{1,25},{9,1},{17,9},{25,17},{2,26},{10... | collective-permute-start | bytes 3145736 | tf_op jit(solution)/shard_map/ppermute | solution.py:22
  99.3 26.0 %collective-permute-start.19 = (bf16[2,4,2,128,256]{4,3,2,1,0:T(8,128)(2,1)S(1)}, bf16[2,4,2,128,256]{4,3,2,1,0:T(8,128)(2,1)S(1)}, u32[]{:S(2)}, u32[]{:S(2)}) collective-permute-start(bf16[2,4,2,128,256]{4,3,2,1,0:T(8,128)(2,1)S(1)} %slice.34), channel_id=1, source_target_pairs={{0,8},{8,16},{16,24},{24,0},{1,9},{9,17},{17,25},{25,1},{2,10},{10... | collective-permute-start | bytes 3145736 | tf_op jit(solution)/shard_map/ppermute | solution.py:22
  146.8 14.4 %collective-permute-start.28 = (bf16[2,4,128,256]{3,2,1,0:T(8,128)(2,1)S(1)}, bf16[2,4,128,256]{3,2,1,0:T(8,128)(2,1)S(1)}, u32[]{:S(2)}, u32[]{:S(2)}) collective-permute-start(bf16[2,4,128,256]{3,2,1,0:T(8,128)(2,1)S(1)} %get-tuple-element.104), channel_id=1, source_target_pairs={{0,8},{8,16},{16,24},{24,0},{1,9},{9,17},{17,25},{25,1},{2,10},{10... | collective-permute-start | bytes 1572872 | tf_op jit(solution)/shard_map/ppermute | solution.py:22
  146.9 14.3 %collective-permute-start.29 = (bf16[2,4,128,256]{3,2,1,0:T(8,128)(2,1)S(1)}, bf16[2,4,128,256]{3,2,1,0:T(8,128)(2,1)S(1)}, u32[]{:S(2)}, u32[]{:S(2)}) collective-permute-start(bf16[2,4,128,256]{3,2,1,0:T(8,128)(2,1)S(1)} %get-tuple-element.105), channel_id=1, source_target_pairs={{0,24},{8,0},{16,8},{24,16},{1,25},{9,1},{17,9},{25,17},{2,26},{10... | collective-permute-start | bytes 1572872 | tf_op jit(solution)/shard_map/ppermute | solution.py:22
  149.5 13.7 %collective-permute-start.30 = (bf16[2,4,128,256]{3,2,1,0:T(8,128)(2,1)S(1)}, bf16[2,4,128,256]{3,2,1,0:T(8,128)(2,1)S(1)}, u32[]{:S(2)}, u32[]{:S(2)}) collective-permute-start(bf16[2,4,128,256]{3,2,1,0:T(8,128)(2,1)S(1)} %get-tuple-element.108), channel_id=1, source_target_pairs={{0,2},{2,4},{4,6},{6,0},{1,3},{3,5},{5,7},{7,1},{8,10},{10,12},{12... | collective-permute-start | bytes 1572872 | tf_op jit(solution)/shard_map/ppermute | solution.py:22
  149.5 13.7 %collective-permute-start.31 = (bf16[2,4,128,256]{3,2,1,0:T(8,128)(2,1)S(1)}, bf16[2,4,128,256]{3,2,1,0:T(8,128)(2,1)S(1)}, u32[]{:S(2)}, u32[]{:S(2)}) collective-permute-start(bf16[2,4,128,256]{3,2,1,0:T(8,128)(2,1)S(1)} %get-tuple-element.109), channel_id=1, source_target_pairs={{0,6},{2,0},{4,2},{6,4},{1,7},{3,1},{5,3},{7,5},{8,14},{10,8},{12,... | collective-permute-start | bytes 1572872 | tf_op jit(solution)/shard_map/ppermute | solution.py:22
  163.8 24.1 %collective-permute-start.32 = (bf16[4,4,128,256]{3,2,1,0:T(8,128)(2,1)S(1)}, bf16[4,4,128,256]{3,2,1,0:T(8,128)(2,1)S(1)}, u32[]{:S(2)}, u32[]{:S(2)}) collective-permute-start(bf16[4,4,128,256]{3,2,1,0:T(8,128)(2,1)S(1)} %get-tuple-element.110), channel_id=1, source_target_pairs={{0,8},{8,16},{16,24},{24,0},{1,9},{9,17},{17,25},{25,1},{2,10},{10... | collective-permute-start | bytes 3145736 | tf_op jit(solution)/shard_map/ppermute | solution.py:22
  163.9 24.0 %collective-permute-start.33 = (bf16[4,4,128,256]{3,2,1,0:T(8,128)(2,1)S(1)}, bf16[4,4,128,256]{3,2,1,0:T(8,128)(2,1)S(1)}, u32[]{:S(2)}, u32[]{:S(2)}) collective-permute-start(bf16[4,4,128,256]{3,2,1,0:T(8,128)(2,1)S(1)} %get-tuple-element.111), channel_id=1, source_target_pairs={{0,24},{8,0},{16,8},{24,16},{1,25},{9,1},{17,9},{25,17},{2,26},{10... | collective-permute-start | bytes 3145736 | tf_op jit(solution)/shard_map/ppermute | solution.py:22
  166.5 25.1 %collective-permute-start.37 = (bf16[4,4,128,256]{3,2,1,0:T(8,128)(2,1)S(1)}, bf16[4,4,128,256]{3,2,1,0:T(8,128)(2,1)S(1)}, u32[]{:S(2)}, u32[]{:S(2)}) collective-permute-start(bf16[4,4,128,256]{3,2,1,0:T(8,128)(2,1)S(1)} %get-tuple-element.117), channel_id=1, source_target_pairs={{0,2},{2,4},{4,6},{6,0},{1,3},{3,5},{5,7},{7,1},{8,10},{10,12},{12... | collective-permute-start | bytes 3145736 | tf_op jit(solution)/shard_map/ppermute | solution.py:22
  166.9 24.7 %collective-permute-start.38 = (bf16[4,4,128,256]{3,2,1,0:T(8,128)(2,1)S(1)}, bf16[4,4,128,256]{3,2,1,0:T(8,128)(2,1)S(1)}, u32[]{:S(2)}, u32[]{:S(2)}) collective-permute-start(bf16[4,4,128,256]{3,2,1,0:T(8,128)(2,1)S(1)} %get-tuple-element.118), channel_id=1, source_target_pairs={{0,6},{2,0},{4,2},{6,4},{1,7},{3,1},{5,3},{7,5},{8,14},{10,8},{12,... | collective-permute-start | bytes 3145736 | tf_op jit(solution)/shard_map/ppermute | solution.py:22
  191.0 11.4 %collective-permute-start.36 = (bf16[4,128,256]{2,1,0:T(8,128)(2,1)S(1)}, bf16[4,128,256]{2,1,0:T(8,128)(2,1)S(1)}, u32[]{:S(2)}, u32[]{:S(2)}) collective-permute-start(bf16[4,128,256]{2,1,0:T(8,128)(2,1)S(1)} %get-tuple-element.115), channel_id=1, source_target_pairs={{0,4},{2,6},{4,0},{6,2},{1,5},{3,7},{5,1},{7,3},{8,12},{10,14},{12... | collective-permute-start | bytes 786440 | tf_op jit(solution)/shard_map/ppermute | solution.py:22
  (27 other events, 171.1 us)

commit v7 on v6

--- a/solution.py
+++ b/solution.py
@@ -423,6 +423,7 @@
     )
     a_all, b_all, rows = lax.optimization_barrier((a_all, b_all, rows))
     a_all, b_all = ring_gather(a_all, "x"), ring_gather(b_all, "z")
+    a_all, b_all = lax.optimization_barrier((a_all, b_all))
     h, goal = rows[0], rows[1]
     x = jnp.concatenate([h, jnp.zeros_like(h)], 0)
 

time: 237 us -> 239 us (level)
  no operation moved by 1% of the time
where the time goes in v7:
time: 239 us
  waiting for transfers between devices  124 us (52%)
  starting transfers between devices  61.4 us (26%)
  Pallas kernels  24.1 us (10%)
  blocking collectives  21.8 us (9%)
  local copies, waits for them, and re-layouts  4.67 us (2%)
    ppermute x36, waiting for transfers between devices, shift(): return lax.ppermute(value, axis, [(i, (i + steps) % 4) for i in range(4)])  116 us
    ppermute x36, starting transfers between devices, shift(): return lax.ppermute(value, axis, [(i, (i + steps) % 4) for i in range(4)])  49.6 us
    all_to_all x1, blocking collectives, local(): lax.all_to_all(totals, ('y', 'z', 'x', 'c'), 0, 0).reshape(128, 128)  21.8 us
    ppermute x9, starting transfers between devices, swap(): return lax.ppermute(value, 'c', [(0, 1), (1, 0)])  11.8 us
    ppermute x9, waiting for transfers between devices, swap(): return lax.ppermute(value, 'c', [(0, 1), (1, 0)])  8.07 us
  transfers between devices with their start and end apart: 45, of which 25 were waited for; matrix products, arithmetic and copies ran while one was open for 1% of the time, Pallas kernels for 3%

profile of v7, /device:TPU:1, one launch (start us, length us, event | category | flops | bytes accessed | tf_op | source)
XLA Modules:
  0.0 238.8 jit_solution(13607167948097466806)
XLA Ops:
  0.6 2.5 %shard_map.94 = (bf16[4,128,256]{2,1,0:T(8,128)(2,1)}, f32[128,128]{1,0:T(8,128)}) custom-call(bf16[1,128]{1,0:T(2,128)(2,1)} %gain_ref.1, bf16[1,128,256]{2,1,0:T(8,128)(2,1)} %down_hbm.1, bf16[1,128,256]{2,1,0:T(8,128)(2,1)} %vector_hbm.1, bf16[1,256,128]{2,1,0:T(8,128)(2,1)} %up_hbm.1, bf16[1,256,128]{2,1,0:T(8,128)(2,1)} %up_vector_hbm.1), custom_call_target="tpu_custom_call" | custom-call | flops 1048576 | bytes 1048576 | tf_op jit(solution)/shard_map/pallas_call | solution.py:392
  3.1 3.8 %collective-permute-start.2 = (bf16[4,128,256]{2,1,0:T(8,128)(2,1)}, bf16[4,128,256]{2,1,0:T(8,128)(2,1)S(1)}, u32[]{:S(2)}, u32[]{:S(2)}) collective-permute-start(bf16[4,128,256]{2,1,0:T(8,128)(2,1)} %get-tuple-element.78.own), channel_id=1, source_target_pairs={{0,64},{32,96},{64,0},{96,32},{1,65},{33,97},{65,1},{97,33},{2,66}... | collective-permute-start | bytes 786440 | tf_op jit(solution)/shard_map/ppermute | solution.py:22
  8.5 4.4 %collective-permute-done.2.across = bf16[4,128,256]{2,1,0:T(8,128)(2,1)S(1)} collective-permute-done((bf16[4,128,256]{2,1,0:T(8,128)(2,1)}, bf16[4,128,256]{2,1,0:T(8,128)(2,1)S(1)}, u32[]{:S(2)}, u32[]{:S(2)}) %collective-permute-start.2) | collective-permute-done | bytes 262176 | tf_op jit(solution)/shard_map/ppermute | solution.py:22
  12.9 6.1 %collective-permute-done.1.ahead = bf16[4,128,256]{2,1,0:T(8,128)(2,1)S(1)} collective-permute-done((bf16[4,128,256]{2,1,0:T(8,128)(2,1)}, bf16[4,128,256]{2,1,0:T(8,128)(2,1)S(1)}, u32[]{:S(2)}, u32[]{:S(2)}) %collective-permute-start.1) | collective-permute-done | bytes 262176 | tf_op jit(solution)/shard_map/ppermute | solution.py:22
  20.9 3.9 %collective-permute-start.4 = (bf16[4,2,128,256]{3,2,1,0:T(8,128)(2,1)S(1)}, bf16[4,2,128,256]{3,2,1,0:T(8,128)(2,1)S(1)}, u32[]{:S(2)}, u32[]{:S(2)}) collective-permute-start(bf16[4,2,128,256]{3,2,1,0:T(8,128)(2,1)S(1)} %get-tuple-element.79.own), channel_id=1, source_target_pairs={{0,24},{8,0},{16,8},{24,16},{1,25},{9,1},{17,9},{25,17},{2,26},{10... | collective-permute-start | bytes 1572872 | tf_op jit(solution)/shard_map/ppermute | solution.py:22
  24.8 2.5 %collective-permute-start.8 = (bf16[4,2,128,256]{3,2,1,0:T(8,128)(2,1)S(1)}, bf16[4,2,128,256]{3,2,1,0:T(8,128)(2,1)S(1)}, u32[]{:S(2)}, u32[]{:S(2)}) collective-permute-start(bf16[4,2,128,256]{3,2,1,0:T(8,128)(2,1)S(1)} %get-tuple-element.82.own), channel_id=1, source_target_pairs={{0,6},{2,0},{4,2},{6,4},{1,7},{3,1},{5,3},{7,5},{8,14},{10,8},{12,... | collective-permute-start | bytes 1572872 | tf_op jit(solution)/shard_map/ppermute | solution.py:22
  34.9 3.1 %collective-permute-done.3.behind = bf16[4,2,128,256]{3,2,1,0:T(8,128)(2,1)S(1)} collective-permute-done((bf16[4,2,128,256]{3,2,1,0:T(8,128)(2,1)S(1)}, bf16[4,2,128,256]{3,2,1,0:T(8,128)(2,1)S(1)}, u32[]{:S(2)}, u32[]{:S(2)}) %collective-permute-start.3) | collective-permute-done | bytes 524320 | tf_op jit(solution)/shard_map/ppermute | solution.py:22
  38.8 2.7 %collective-permute-start.6 = (bf16[2,2,128,256]{3,2,1,0:T(8,128)(2,1)}, bf16[2,2,128,256]{3,2,1,0:T(8,128)(2,1)}, u32[]{:S(2)}, u32[]{:S(2)}) collective-permute-start(bf16[2,2,128,256]{3,2,1,0:T(8,128)(2,1)} %get-tuple-element.81), channel_id=1, source_target_pairs={{0,24},{8,0},{16,8},{24,16},{1,25},{9,1},{17,9},{25,17},{2,26},{10... | collective-permute-start | bytes 786440 | tf_op jit(solution)/shard_map/ppermute | solution.py:22
  50.3 2.7 %collective-permute-start.13 = (bf16[4,4,2,128,256]{4,3,2,1,0:T(8,128)(2,1)S(1)}, bf16[4,4,2,128,256]{4,3,2,1,0:T(8,128)(2,1)S(1)}, u32[]{:S(2)}, u32[]{:S(2)}) collective-permute-start(bf16[4,4,2,128,256]{4,3,2,1,0:T(8,128)(2,1)S(1)} %shard_map.97.refs_0_.refs_5_), channel_id=1, source_target_pairs={{0,6},{2,0},{4,2},{6,4},{1,7},{3,1},{5,3},{7,5},{8,14},{10,8},{12,... | collective-permute-start | bytes 6291464 | tf_op jit(solution)/shard_map/ppermute | solution.py:22
  54.5 39.2 %collective-permute-done.13.refs_2_.refs_7_ = bf16[4,4,2,128,256]{4,3,2,1,0:T(8,128)(2,1)S(1)} collective-permute-done((bf16[4,4,2,128,256]{4,3,2,1,0:T(8,128)(2,1)S(1)}, bf16[4,4,2,128,256]{4,3,2,1,0:T(8,128)(2,1)S(1)}, u32[]{:S(2)}, u32[]{:S(2)}) %collective-permute-start.13) | collective-permute-done | bytes 2097184 | tf_op jit(solution)/shard_map/ppermute | solution.py:22
  93.7 3.5 %collective-permute-start.15 = (bf16[2,4,2,128,256]{4,3,2,1,0:T(8,128)(2,1)S(1)}, bf16[2,4,2,128,256]{4,3,2,1,0:T(8,128)(2,1)S(1)}, u32[]{:S(2)}, u32[]{:S(2)}) collective-permute-start(bf16[2,4,2,128,256]{4,3,2,1,0:T(8,128)(2,1)S(1)} %slice.33), channel_id=1, source_target_pairs={{0,6},{2,0},{4,2},{6,4},{1,7},{3,1},{5,3},{7,5},{8,14},{10,8},{12,... | collective-permute-start | bytes 3145736 | tf_op jit(solution)/shard_map/ppermute | solution.py:22
  99.5 15.8 %collective-permute-done.15.refs_4_.refs_9_ = bf16[2,4,2,128,256]{4,3,2,1,0:T(8,128)(2,1)S(1)} collective-permute-done((bf16[2,4,2,128,256]{4,3,2,1,0:T(8,128)(2,1)S(1)}, bf16[2,4,2,128,256]{4,3,2,1,0:T(8,128)(2,1)S(1)}, u32[]{:S(2)}, u32[]{:S(2)}) %collective-permute-start.15) | collective-permute-done | bytes 1048608 | tf_op jit(solution)/shard_map/ppermute | solution.py:22
  115.3 3.0 %collective-permute-done.14.refs_3_.refs_8_ = bf16[2,4,2,128,256]{4,3,2,1,0:T(8,128)(2,1)S(1)} collective-permute-done((bf16[2,4,2,128,256]{4,3,2,1,0:T(8,128)(2,1)S(1)}, bf16[2,4,2,128,256]{4,3,2,1,0:T(8,128)(2,1)S(1)}, u32[]{:S(2)}, u32[]{:S(2)}) %collective-permute-start.14) | collective-permute-done | bytes 1048608 | tf_op jit(solution)/shard_map/ppermute | solution.py:22
  119.9 6.8 %collective-permute-start.20 = (f32[64,640]{1,0:T(8,128)S(1)}, f32[64,640]{1,0:T(8,128)S(1)}, u32[]{:S(2)}, u32[]{:S(2)}) collective-permute-start(f32[64,640]{1,0:T(8,128)S(1)} %shard_map.101.own_ref), channel_id=1, source_target_pairs={{0,1},{1,0},{2,3},{3,2},{4,5},{5,4},{6,7},{7,6},{8,9},{9,8},{10,11... | collective-permute-start | bytes 491528 | tf_op jit(solution)/shard_map/ppermute | solution.py:26
  148.3 2.7 %collective-permute-start.29 = (bf16[2,4,128,256]{3,2,1,0:T(8,128)(2,1)S(1)}, bf16[2,4,128,256]{3,2,1,0:T(8,128)(2,1)S(1)}, u32[]{:S(2)}, u32[]{:S(2)}) collective-permute-start(bf16[2,4,128,256]{3,2,1,0:T(8,128)(2,1)S(1)} %get-tuple-element.125), channel_id=1, source_target_pairs={{0,24},{8,0},{16,8},{24,16},{1,25},{9,1},{17,9},{25,17},{2,26},{10... | collective-permute-start | bytes 1572872 | tf_op jit(solution)/shard_map/ppermute | solution.py:22
  150.9 2.7 %collective-permute-start.31 = (bf16[2,4,128,256]{3,2,1,0:T(8,128)(2,1)S(1)}, bf16[2,4,128,256]{3,2,1,0:T(8,128)(2,1)S(1)}, u32[]{:S(2)}, u32[]{:S(2)}) collective-permute-start(bf16[2,4,128,256]{3,2,1,0:T(8,128)(2,1)S(1)} %get-tuple-element.129), channel_id=1, source_target_pairs={{0,6},{2,0},{4,2},{6,4},{1,7},{3,1},{5,3},{7,5},{8,14},{10,8},{12,... | collective-permute-start | bytes 1572872 | tf_op jit(solution)/shard_map/ppermute | solution.py:22
  155.7 6.9 %collective-permute-done.28.refs_2_ = bf16[2,4,128,256]{3,2,1,0:T(8,128)(2,1)S(1)} collective-permute-done((bf16[2,4,128,256]{3,2,1,0:T(8,128)(2,1)S(1)}, bf16[2,4,128,256]{3,2,1,0:T(8,128)(2,1)S(1)}, u32[]{:S(2)}, u32[]{:S(2)}) %collective-permute-start.28) | collective-permute-done | bytes 524320 | tf_op jit(solution)/shard_map/ppermute | solution.py:22
  165.3 2.7 %collective-permute-start.33 = (bf16[4,4,128,256]{3,2,1,0:T(8,128)(2,1)S(1)}, bf16[4,4,128,256]{3,2,1,0:T(8,128)(2,1)S(1)}, u32[]{:S(2)}, u32[]{:S(2)}) collective-permute-start(bf16[4,4,128,256]{3,2,1,0:T(8,128)(2,1)S(1)} %get-tuple-element.131), channel_id=1, source_target_pairs={{0,24},{8,0},{16,8},{24,16},{1,25},{9,1},{17,9},{25,17},{2,26},{10... | collective-permute-start | bytes 3145736 | tf_op jit(solution)/shard_map/ppermute | solution.py:22
  170.6 18.7 %collective-permute-done.32.behind = bf16[4,4,128,256]{3,2,1,0:T(8,128)(2,1)S(1)} collective-permute-done((bf16[4,4,128,256]{3,2,1,0:T(8,128)(2,1)S(1)}, bf16[4,4,128,256]{3,2,1,0:T(8,128)(2,1)S(1)}, u32[]{:S(2)}, u32[]{:S(2)}) %collective-permute-start.32) | collective-permute-done | bytes 1048608 | tf_op jit(solution)/shard_map/ppermute | solution.py:22
  193.7 2.7 %collective-permute-start.40 = (bf16[4,128,256]{2,1,0:T(8,128)(2,1)S(1)}, bf16[4,128,256]{2,1,0:T(8,128)(2,1)S(1)}, u32[]{:S(2)}, u32[]{:S(2)}) collective-permute-start(bf16[4,128,256]{2,1,0:T(8,128)(2,1)S(1)} %get-tuple-element.141), channel_id=1, source_target_pairs={{0,24},{8,0},{16,8},{24,16},{1,25},{9,1},{17,9},{25,17},{2,26},{10... | collective-permute-start | bytes 786440 | tf_op jit(solution)/shard_map/ppermute | solution.py:22
  197.4 6.5 %collective-permute-done.36.refs_3_ = bf16[4,128,256]{2,1,0:T(8,128)(2,1)S(1)} collective-permute-done((bf16[4,128,256]{2,1,0:T(8,128)(2,1)S(1)}, bf16[4,128,256]{2,1,0:T(8,128)(2,1)S(1)}, u32[]{:S(2)}, u32[]{:S(2)}) %collective-permute-start.36) | collective-permute-done | bytes 262176 | tf_op jit(solution)/shard_map/ppermute | solution.py:22
  206.3 2.5 %collective-permute-start.42 = (bf16[256,256]{1,0:T(8,128)(2,1)S(1)}, bf16[256,256]{1,0:T(8,128)(2,1)S(1)}, u32[]{:S(2)}, u32[]{:S(2)}) collective-permute-start(bf16[256,256]{1,0:T(8,128)(2,1)S(1)} %get-tuple-element.144), channel_id=1, source_target_pairs={{0,32},{32,64},{64,96},{96,0},{1,33},{33,65},{65,97},{97,1},{2,34}... | collective-permute-start | bytes 393224 | tf_op jit(solution)/shard_map/ppermute | solution.py:22
  213.0 2.9 %collective-permute-done.44.b3 = bf16[256,256]{1,0:T(8,128)(2,1)S(1)} collective-permute-done((bf16[256,256]{1,0:T(8,128)(2,1)S(1)}, bf16[256,256]{1,0:T(8,128)(2,1)S(1)}, u32[]{:S(2)}, u32[]{:S(2)}) %collective-permute-start.44) | collective-permute-done | bytes 131104 | tf_op jit(solution)/shard_map/ppermute | solution.py:22
  216.2 21.8 %all_to_all.5 = f32[128,1,128]{2,1,0:T(1,128)S(1)} all-to-all(f32[128,1,128]{2,1,0:T(1,128)S(1)} %broadcast_in_dim.16), channel_id=1, replica_groups=mesh['y'=4,'z'=4,'x'=4,'c'=2] {'y','z','x','c'}, dimensions={0} | all-to-all | bytes 131072 | tf_op jit(solution)/shard_map/all_to_all | solution.py:507
  (113 shorter events, 68.0 us)
Async XLA Ops:
  6.9 12.1 %collective-permute-start.1 = (bf16[4,128,256]{2,1,0:T(8,128)(2,1)}, bf16[4,128,256]{2,1,0:T(8,128)(2,1)S(1)}, u32[]{:S(2)}, u32[]{:S(2)}) collective-permute-start(bf16[4,128,256]{2,1,0:T(8,128)(2,1)} %get-tuple-element.78.own), channel_id=1, source_target_pairs={{0,96},{32,0},{64,32},{96,64},{1,97},{33,1},{65,33},{97,65},{2,98}... | collective-permute-start | bytes 786440 | tf_op jit(solution)/shard_map/ppermute | solution.py:22
  7.7 11.6 %collective-permute-start = (bf16[4,128,256]{2,1,0:T(8,128)(2,1)}, bf16[4,128,256]{2,1,0:T(8,128)(2,1)S(1)}, u32[]{:S(2)}, u32[]{:S(2)}) collective-permute-start(bf16[4,128,256]{2,1,0:T(8,128)(2,1)} %get-tuple-element.78.own), channel_id=1, source_target_pairs={{0,32},{32,64},{64,96},{96,0},{1,33},{33,65},{65,97},{97,1},{2,34}... | collective-permute-start | bytes 786440 | tf_op jit(solution)/shard_map/ppermute | solution.py:22
  20.9 14.0 %collective-permute-start.4 = (bf16[4,2,128,256]{3,2,1,0:T(8,128)(2,1)S(1)}, bf16[4,2,128,256]{3,2,1,0:T(8,128)(2,1)S(1)}, u32[]{:S(2)}, u32[]{:S(2)}) collective-permute-start(bf16[4,2,128,256]{3,2,1,0:T(8,128)(2,1)S(1)} %get-tuple-element.79.own), channel_id=1, source_target_pairs={{0,24},{8,0},{16,8},{24,16},{1,25},{9,1},{17,9},{25,17},{2,26},{10... | collective-permute-start | bytes 1572872 | tf_op jit(solution)/shard_map/ppermute | solution.py:22
  24.8 13.3 %collective-permute-start.3 = (bf16[4,2,128,256]{3,2,1,0:T(8,128)(2,1)S(1)}, bf16[4,2,128,256]{3,2,1,0:T(8,128)(2,1)S(1)}, u32[]{:S(2)}, u32[]{:S(2)}) collective-permute-start(bf16[4,2,128,256]{3,2,1,0:T(8,128)(2,1)S(1)} %get-tuple-element.79.own), channel_id=1, source_target_pairs={{0,8},{8,16},{16,24},{24,0},{1,9},{9,17},{17,25},{25,1},{2,10},{10... | collective-permute-start | bytes 1572872 | tf_op jit(solution)/shard_map/ppermute | solution.py:22
  24.8 16.8 %collective-permute-start.8 = (bf16[4,2,128,256]{3,2,1,0:T(8,128)(2,1)S(1)}, bf16[4,2,128,256]{3,2,1,0:T(8,128)(2,1)S(1)}, u32[]{:S(2)}, u32[]{:S(2)}) collective-permute-start(bf16[4,2,128,256]{3,2,1,0:T(8,128)(2,1)S(1)} %get-tuple-element.82.own), channel_id=1, source_target_pairs={{0,6},{2,0},{4,2},{6,4},{1,7},{3,1},{5,3},{7,5},{8,14},{10,8},{12,... | collective-permute-start | bytes 1572872 | tf_op jit(solution)/shard_map/ppermute | solution.py:22
  27.2 14.3 %collective-permute-start.7 = (bf16[4,2,128,256]{3,2,1,0:T(8,128)(2,1)S(1)}, bf16[4,2,128,256]{3,2,1,0:T(8,128)(2,1)S(1)}, u32[]{:S(2)}, u32[]{:S(2)}) collective-permute-start(bf16[4,2,128,256]{3,2,1,0:T(8,128)(2,1)S(1)} %get-tuple-element.82.own), channel_id=1, source_target_pairs={{0,2},{2,4},{4,6},{6,0},{1,3},{3,5},{5,7},{7,1},{8,10},{10,12},{12... | collective-permute-start | bytes 1572872 | tf_op jit(solution)/shard_map/ppermute | solution.py:22
  31.1 14.0 %collective-permute-start.11 = (bf16[2,32,2048]{2,1,0:T(8,128)(2,1)}, bf16[2,32,2048]{2,1,0:T(8,128)(2,1)}, u32[]{:S(2)}, u32[]{:S(2)}) collective-permute-start(bf16[2,32,2048]{2,1,0:T(8,128)(2,1)} %get-tuple-element.86), channel_id=1, source_target_pairs={{0,1},{1,0},{2,3},{3,2},{4,5},{5,4},{6,7},{7,6},{8,9},{9,8},{10,11... | collective-permute-start | bytes 786440 | tf_op jit(solution)/shard_map/ppermute | solution.py:26
  50.3 43.4 %collective-permute-start.13 = (bf16[4,4,2,128,256]{4,3,2,1,0:T(8,128)(2,1)S(1)}, bf16[4,4,2,128,256]{4,3,2,1,0:T(8,128)(2,1)S(1)}, u32[]{:S(2)}, u32[]{:S(2)}) collective-permute-start(bf16[4,4,2,128,256]{4,3,2,1,0:T(8,128)(2,1)S(1)} %shard_map.97.refs_0_.refs_5_), channel_id=1, source_target_pairs={{0,6},{2,0},{4,2},{6,4},{1,7},{3,1},{5,3},{7,5},{8,14},{10,8},{12,... | collective-permute-start | bytes 6291464 | tf_op jit(solution)/shard_map/ppermute | solution.py:22
  53.0 44.2 %collective-permute-start.12 = (bf16[4,4,2,128,256]{4,3,2,1,0:T(8,128)(2,1)S(1)}, bf16[4,4,2,128,256]{4,3,2,1,0:T(8,128)(2,1)S(1)}, u32[]{:S(2)}, u32[]{:S(2)}) collective-permute-start(bf16[4,4,2,128,256]{4,3,2,1,0:T(8,128)(2,1)S(1)} %shard_map.97.refs_0_.refs_5_), channel_id=1, source_target_pairs={{0,2},{2,4},{4,6},{6,0},{1,3},{3,5},{5,7},{7,1},{8,10},{10,12},{12... | collective-permute-start | bytes 6291464 | tf_op jit(solution)/shard_map/ppermute | solution.py:22
  53.0 44.4 %collective-permute-start.17 = (bf16[4,4,2,128,256]{4,3,2,1,0:T(8,128)(2,1)S(1)}, bf16[4,4,2,128,256]{4,3,2,1,0:T(8,128)(2,1)S(1)}, u32[]{:S(2)}, u32[]{:S(2)}) collective-permute-start(bf16[4,4,2,128,256]{4,3,2,1,0:T(8,128)(2,1)S(1)} %shard_map.99.refs_0_.refs_5_), channel_id=1, source_target_pairs={{0,24},{8,0},{16,8},{24,16},{1,25},{9,1},{17,9},{25,17},{2,26},{10... | collective-permute-start | bytes 6291464 | tf_op jit(solution)/shard_map/ppermute | solution.py:22
  54.4 44.8 %collective-permute-start.16 = (bf16[4,4,2,128,256]{4,3,2,1,0:T(8,128)(2,1)S(1)}, bf16[4,4,2,128,256]{4,3,2,1,0:T(8,128)(2,1)S(1)}, u32[]{:S(2)}, u32[]{:S(2)}) collective-permute-start(bf16[4,4,2,128,256]{4,3,2,1,0:T(8,128)(2,1)S(1)} %shard_map.99.refs_0_.refs_5_), channel_id=1, source_target_pairs={{0,8},{8,16},{16,24},{24,0},{1,9},{9,17},{17,25},{25,1},{2,10},{10... | collective-permute-start | bytes 6291464 | tf_op jit(solution)/shard_map/ppermute | solution.py:22
  93.7 21.5 %collective-permute-start.15 = (bf16[2,4,2,128,256]{4,3,2,1,0:T(8,128)(2,1)S(1)}, bf16[2,4,2,128,256]{4,3,2,1,0:T(8,128)(2,1)S(1)}, u32[]{:S(2)}, u32[]{:S(2)}) collective-permute-start(bf16[2,4,2,128,256]{4,3,2,1,0:T(8,128)(2,1)S(1)} %slice.33), channel_id=1, source_target_pairs={{0,6},{2,0},{4,2},{6,4},{1,7},{3,1},{5,3},{7,5},{8,14},{10,8},{12,... | collective-permute-start | bytes 3145736 | tf_op jit(solution)/shard_map/ppermute | solution.py:22
  97.3 20.9 %collective-permute-start.14 = (bf16[2,4,2,128,256]{4,3,2,1,0:T(8,128)(2,1)S(1)}, bf16[2,4,2,128,256]{4,3,2,1,0:T(8,128)(2,1)S(1)}, u32[]{:S(2)}, u32[]{:S(2)}) collective-permute-start(bf16[2,4,2,128,256]{4,3,2,1,0:T(8,128)(2,1)S(1)} %slice.32), channel_id=1, source_target_pairs={{0,2},{2,4},{4,6},{6,0},{1,3},{3,5},{5,7},{7,1},{8,10},{10,12},{12... | collective-permute-start | bytes 3145736 | tf_op jit(solution)/shard_map/ppermute | solution.py:22
  97.5 20.8 %collective-permute-start.19 = (bf16[2,4,2,128,256]{4,3,2,1,0:T(8,128)(2,1)S(1)}, bf16[2,4,2,128,256]{4,3,2,1,0:T(8,128)(2,1)S(1)}, u32[]{:S(2)}, u32[]{:S(2)}) collective-permute-start(bf16[2,4,2,128,256]{4,3,2,1,0:T(8,128)(2,1)S(1)} %slice.35), channel_id=1, source_target_pairs={{0,24},{8,0},{16,8},{24,16},{1,25},{9,1},{17,9},{25,17},{2,26},{10... | collective-permute-start | bytes 3145736 | tf_op jit(solution)/shard_map/ppermute | solution.py:22
  99.3 20.1 %collective-permute-start.18 = (bf16[2,4,2,128,256]{4,3,2,1,0:T(8,128)(2,1)S(1)}, bf16[2,4,2,128,256]{4,3,2,1,0:T(8,128)(2,1)S(1)}, u32[]{:S(2)}, u32[]{:S(2)}) collective-permute-start(bf16[2,4,2,128,256]{4,3,2,1,0:T(8,128)(2,1)S(1)} %slice.34), channel_id=1, source_target_pairs={{0,8},{8,16},{16,24},{24,0},{1,9},{9,17},{17,25},{25,1},{2,10},{10... | collective-permute-start | bytes 3145736 | tf_op jit(solution)/shard_map/ppermute | solution.py:22
  148.2 14.4 %collective-permute-start.28 = (bf16[2,4,128,256]{3,2,1,0:T(8,128)(2,1)S(1)}, bf16[2,4,128,256]{3,2,1,0:T(8,128)(2,1)S(1)}, u32[]{:S(2)}, u32[]{:S(2)}) collective-permute-start(bf16[2,4,128,256]{3,2,1,0:T(8,128)(2,1)S(1)} %get-tuple-element.124), channel_id=1, source_target_pairs={{0,8},{8,16},{16,24},{24,0},{1,9},{9,17},{17,25},{25,1},{2,10},{10... | collective-permute-start | bytes 1572872 | tf_op jit(solution)/shard_map/ppermute | solution.py:22
  148.3 14.3 %collective-permute-start.29 = (bf16[2,4,128,256]{3,2,1,0:T(8,128)(2,1)S(1)}, bf16[2,4,128,256]{3,2,1,0:T(8,128)(2,1)S(1)}, u32[]{:S(2)}, u32[]{:S(2)}) collective-permute-start(bf16[2,4,128,256]{3,2,1,0:T(8,128)(2,1)S(1)} %get-tuple-element.125), channel_id=1, source_target_pairs={{0,24},{8,0},{16,8},{24,16},{1,25},{9,1},{17,9},{25,17},{2,26},{10... | collective-permute-start | bytes 1572872 | tf_op jit(solution)/shard_map/ppermute | solution.py:22
  150.9 13.7 %collective-permute-start.30 = (bf16[2,4,128,256]{3,2,1,0:T(8,128)(2,1)S(1)}, bf16[2,4,128,256]{3,2,1,0:T(8,128)(2,1)S(1)}, u32[]{:S(2)}, u32[]{:S(2)}) collective-permute-start(bf16[2,4,128,256]{3,2,1,0:T(8,128)(2,1)S(1)} %get-tuple-element.128), channel_id=1, source_target_pairs={{0,2},{2,4},{4,6},{6,0},{1,3},{3,5},{5,7},{7,1},{8,10},{10,12},{12... | collective-permute-start | bytes 1572872 | tf_op jit(solution)/shard_map/ppermute | solution.py:22
  150.9 13.7 %collective-permute-start.31 = (bf16[2,4,128,256]{3,2,1,0:T(8,128)(2,1)S(1)}, bf16[2,4,128,256]{3,2,1,0:T(8,128)(2,1)S(1)}, u32[]{:S(2)}, u32[]{:S(2)}) collective-permute-start(bf16[2,4,128,256]{3,2,1,0:T(8,128)(2,1)S(1)} %get-tuple-element.129), channel_id=1, source_target_pairs={{0,6},{2,0},{4,2},{6,4},{1,7},{3,1},{5,3},{7,5},{8,14},{10,8},{12,... | collective-permute-start | bytes 1572872 | tf_op jit(solution)/shard_map/ppermute | solution.py:22
  165.2 24.1 %collective-permute-start.32 = (bf16[4,4,128,256]{3,2,1,0:T(8,128)(2,1)S(1)}, bf16[4,4,128,256]{3,2,1,0:T(8,128)(2,1)S(1)}, u32[]{:S(2)}, u32[]{:S(2)}) collective-permute-start(bf16[4,4,128,256]{3,2,1,0:T(8,128)(2,1)S(1)} %get-tuple-element.130), channel_id=1, source_target_pairs={{0,8},{8,16},{16,24},{24,0},{1,9},{9,17},{17,25},{25,1},{2,10},{10... | collective-permute-start | bytes 3145736 | tf_op jit(solution)/shard_map/ppermute | solution.py:22
  165.3 24.0 %collective-permute-start.33 = (bf16[4,4,128,256]{3,2,1,0:T(8,128)(2,1)S(1)}, bf16[4,4,128,256]{3,2,1,0:T(8,128)(2,1)S(1)}, u32[]{:S(2)}, u32[]{:S(2)}) collective-permute-start(bf16[4,4,128,256]{3,2,1,0:T(8,128)(2,1)S(1)} %get-tuple-element.131), channel_id=1, source_target_pairs={{0,24},{8,0},{16,8},{24,16},{1,25},{9,1},{17,9},{25,17},{2,26},{10... | collective-permute-start | bytes 3145736 | tf_op jit(solution)/shard_map/ppermute | solution.py:22
  167.9 25.3 %collective-permute-start.37 = (bf16[4,4,128,256]{3,2,1,0:T(8,128)(2,1)S(1)}, bf16[4,4,128,256]{3,2,1,0:T(8,128)(2,1)S(1)}, u32[]{:S(2)}, u32[]{:S(2)}) collective-permute-start(bf16[4,4,128,256]{3,2,1,0:T(8,128)(2,1)S(1)} %get-tuple-element.137), channel_id=1, source_target_pairs={{0,2},{2,4},{4,6},{6,0},{1,3},{3,5},{5,7},{7,1},{8,10},{10,12},{12... | collective-permute-start | bytes 3145736 | tf_op jit(solution)/shard_map/ppermute | solution.py:22
  168.8 24.5 %collective-permute-start.38 = (bf16[4,4,128,256]{3,2,1,0:T(8,128)(2,1)S(1)}, bf16[4,4,128,256]{3,2,1,0:T(8,128)(2,1)S(1)}, u32[]{:S(2)}, u32[]{:S(2)}) collective-permute-start(bf16[4,4,128,256]{3,2,1,0:T(8,128)(2,1)S(1)} %get-tuple-element.138), channel_id=1, source_target_pairs={{0,6},{2,0},{4,2},{6,4},{1,7},{3,1},{5,3},{7,5},{8,14},{10,8},{12,... | collective-permute-start | bytes 3145736 | tf_op jit(solution)/shard_map/ppermute | solution.py:22
  192.4 11.4 %collective-permute-start.36 = (bf16[4,128,256]{2,1,0:T(8,128)(2,1)S(1)}, bf16[4,128,256]{2,1,0:T(8,128)(2,1)S(1)}, u32[]{:S(2)}, u32[]{:S(2)}) collective-permute-start(bf16[4,128,256]{2,1,0:T(8,128)(2,1)S(1)} %get-tuple-element.135), channel_id=1, source_target_pairs={{0,4},{2,6},{4,0},{6,2},{1,5},{3,7},{5,1},{7,3},{8,12},{10,14},{12... | collective-permute-start | bytes 786440 | tf_op jit(solution)/shard_map/ppermute | solution.py:22
  (27 other events, 170.8 us)

commit v8 on v6

--- a/solution.py
+++ b/solution.py
@@ -372,18 +372,9 @@
     return [own, shift(ahead, axis, 1), shift(behind, axis, -1), shift(across, axis, 2)]
 
 
-def ring_near(block, axis):
-    return shift(block, axis, 1), shift(block, axis, -1)
-
-
 def ring_far(behind, ahead, axis):
     cut = behind.shape[0] // 2
     return shift(behind[:cut], axis, 1), shift(ahead[cut:], axis, -1)
-
-
-def ring_gather(block, axis):
-    near = ring_near(block, axis)
-    return [block, *near, *ring_far(*near, axis)]
 
 
 def local(tokens, targets, norm_gain, down_weight, up_weight, down_vector, up_vector):
@@ -421,8 +412,11 @@
     rows = jnp.where(
         core == 0, jnp.concatenate([kept, got], 1), jnp.concatenate([got, kept], 1)
     )
-    a_all, b_all, rows = lax.optimization_barrier((a_all, b_all, rows))
-    a_all, b_all = ring_gather(a_all, "x"), ring_gather(b_all, "z")
+    a_near = shift(a_all, "x", 1), shift(a_all, "x", -1)
+    b_near = shift(b_all, "z", 1), shift(b_all, "z", -1)
+    a_near, b_near, rows = lax.optimization_barrier((a_near, b_near, rows))
+    a_all = [a_all, *a_near, *ring_far(*a_near, "x")]
+    b_all = [b_all, *b_near, *ring_far(*b_near, "z")]
     h, goal = rows[0], rows[1]
     x = jnp.concatenate([h, jnp.zeros_like(h)], 0)
 

time: 237 us -> 271 us (1.14)
  Pallas kernels: 24.1 us -> 50.7 us
  starting transfers between devices: 59.7 us -> 67.6 us
    pallas_call x3, Pallas kernels: 3.71 us -> 15.9 us  [local(): call(functools.partial(forward_kernel, layer), [VMEM] * 13, [wide, sums,...]
    pallas_call x3, Pallas kernels: 3.88 us -> 16 us  [backward(): call(functools.partial(backward_kernel, layer), [VMEM] * 15, [wide, e_sum...]
    slice x4, local copies, waits for them, and re-layouts: 0.34 us -> 5.24 us  [ring_far(): return (shift(behind[:cut], axis, 1), shift(ahead[cut:], axis, -1))]
    ppermute x9, starting transfers between devices: 11.5 us -> 16 us  [swap(): return lax.ppermute(value, 'c', [(0, 1), (1, 0)])]
    ppermute x36, starting transfers between devices: 48.2 us -> 51.6 us  [shift(): return lax.ppermute(value, axis, [(i, (i + steps) % 4) for i in range(4)])]
    pallas_call x1, Pallas kernels: 1.24 us -> 4.09 us  [local(): call(seed_kernel, [VMEM] * 9, [wide, e_sums, sums], work, 3 << 20)]
  transfers between devices with their start and end apart: 45 -> 45, of which waited for: 25 -> 28; matrix products, arithmetic and copies ran while one was open for 1% -> 1% of each run, Pallas kernels for 3% -> 3%
where the time goes in v8:
time: 271 us; the launch traced here: 270 us
  waiting for transfers between devices  123 us (45%)
  starting transfers between devices  67.6 us (25%)
  Pallas kernels  50.7 us (19%)
  blocking collectives  21.1 us (8%)
  local copies, waits for them, and re-layouts  7.17 us (3%)
    ppermute x36, waiting for transfers between devices, shift(): return lax.ppermute(value, axis, [(i, (i + steps) % 4) for i in range(4)])  114 us
    ppermute x36, starting transfers between devices, shift(): return lax.ppermute(value, axis, [(i, (i + steps) % 4) for i in range(4)])  51.6 us
    all_to_all x1, blocking collectives, local(): lax.all_to_all(totals, ('y', 'z', 'x', 'c'), 0, 0).reshape(128, 128)  21.1 us
    pallas_call x3, Pallas kernels, backward(): call(functools.partial(backward_kernel, layer), [VMEM] * 15, [wide, e_sum...  16 us
    ppermute x9, starting transfers between devices, swap(): return lax.ppermute(value, 'c', [(0, 1), (1, 0)])  16 us
    pallas_call x3, Pallas kernels, local(): call(functools.partial(forward_kernel, layer), [VMEM] * 13, [wide, sums,...  15.9 us
    ppermute x9, waiting for transfers between devices, swap(): return lax.ppermute(value, 'c', [(0, 1), (1, 0)])  9.22 us
  transfers between devices with their start and end apart: 45, of which 28 were waited for; matrix products, arithmetic and copies ran while one was open for 1% of the time, Pallas kernels for 3%

profile of v8, /device:TPU:1, one launch (start us, length us, event | category | flops | bytes accessed | tf_op | source)
XLA Modules:
  0.0 270.5 jit_solution(16209187766227554665)
XLA Ops:
  3.1 3.8 %collective-permute-start.2 = (bf16[4,128,256]{2,1,0:T(8,128)(2,1)}, bf16[4,128,256]{2,1,0:T(8,128)(2,1)S(1)}, u32[]{:S(2)}, u32[]{:S(2)}) collective-permute-start(bf16[4,128,256]{2,1,0:T(8,128)(2,1)} %get-tuple-element.70.own), channel_id=1, source_target_pairs={{0,64},{32,96},{64,0},{96,32},{1,65},{33,97},{65,1},{97,33},{2,66}... | collective-permute-start | bytes 786440 | tf_op jit(solution)/shard_map/ppermute | solution.py:22
  8.5 4.4 %collective-permute-done.2.across = bf16[4,128,256]{2,1,0:T(8,128)(2,1)S(1)} collective-permute-done((bf16[4,128,256]{2,1,0:T(8,128)(2,1)}, bf16[4,128,256]{2,1,0:T(8,128)(2,1)S(1)}, u32[]{:S(2)}, u32[]{:S(2)}) %collective-permute-start.2) | collective-permute-done | bytes 262176 | tf_op jit(solution)/shard_map/ppermute | solution.py:22
  12.9 6.1 %collective-permute-done.1.ahead = bf16[4,128,256]{2,1,0:T(8,128)(2,1)S(1)} collective-permute-done((bf16[4,128,256]{2,1,0:T(8,128)(2,1)}, bf16[4,128,256]{2,1,0:T(8,128)(2,1)S(1)}, u32[]{:S(2)}, u32[]{:S(2)}) %collective-permute-start.1) | collective-permute-done | bytes 262176 | tf_op jit(solution)/shard_map/ppermute | solution.py:22
  23.5 3.8 %collective-permute-start.4 = (bf16[4,2,128,256]{3,2,1,0:T(8,128)(2,1)S(1)}, bf16[4,2,128,256]{3,2,1,0:T(8,128)(2,1)S(1)}, u32[]{:S(2)}, u32[]{:S(2)}) collective-permute-start(bf16[4,2,128,256]{3,2,1,0:T(8,128)(2,1)S(1)} %get-tuple-element.71.own), channel_id=1, source_target_pairs={{0,24},{8,0},{16,8},{24,16},{1,25},{9,1},{17,9},{25,17},{2,26},{10... | collective-permute-start | bytes 1572872 | tf_op jit(solution)/shard_map/ppermute | solution.py:22
  27.3 6.4 %collective-permute-done.10.ahead = bf16[4,2,128,256]{3,2,1,0:T(8,128)(2,1)S(1)} collective-permute-done((bf16[4,2,128,256]{3,2,1,0:T(8,128)(2,1)S(1)}, bf16[4,2,128,256]{3,2,1,0:T(8,128)(2,1)S(1)}, u32[]{:S(2)}, u32[]{:S(2)}) %collective-permute-start.10) | collective-permute-done | bytes 524320 | tf_op jit(solution)/shard_map/ppermute | solution.py:22
  33.6 3.1 %collective-permute-done.9.behind = bf16[4,2,128,256]{3,2,1,0:T(8,128)(2,1)S(1)} collective-permute-done((bf16[4,2,128,256]{3,2,1,0:T(8,128)(2,1)S(1)}, bf16[4,2,128,256]{3,2,1,0:T(8,128)(2,1)S(1)}, u32[]{:S(2)}, u32[]{:S(2)}) %collective-permute-start.9) | collective-permute-done | bytes 524320 | tf_op jit(solution)/shard_map/ppermute | solution.py:22
  45.0 3.6 %collective-permute-start.14 = (bf16[4,4,2,128,256]{4,3,2,1,0:T(8,128)(2,1)}, bf16[4,4,2,128,256]{4,3,2,1,0:T(8,128)(2,1)}, u32[]{:S(2)}, u32[]{:S(2)}) collective-permute-start(bf16[4,4,2,128,256]{4,3,2,1,0:T(8,128)(2,1)} %shard_map.99.refs_0_.refs_5_), channel_id=1, source_target_pairs={{0,24},{8,0},{16,8},{24,16},{1,25},{9,1},{17,9},{25,17},{2,26},{10... | collective-permute-start | bytes 6291464 | tf_op jit(solution)/shard_map/ppermute | solution.py:22
  52.2 4.4 %collective-permute-start.15 = (bf16[2,32,2048]{2,1,0:T(8,128)(2,1)S(1)}, bf16[2,32,2048]{2,1,0:T(8,128)(2,1)S(1)}, u32[]{:S(2)}, u32[]{:S(2)}) collective-permute-start(bf16[2,32,2048]{2,1,0:T(8,128)(2,1)S(1)} %get-tuple-element.78), channel_id=1, source_target_pairs={{0,1},{1,0},{2,3},{3,2},{4,5},{5,4},{6,7},{7,6},{8,9},{9,8},{10,11... | collective-permute-start | bytes 786440 | tf_op jit(solution)/shard_map/ppermute | solution.py:26
  57.8 35.1 %collective-permute-done.14.refs_2_.refs_7_ = bf16[4,4,2,128,256]{4,3,2,1,0:T(8,128)(2,1)} collective-permute-done((bf16[4,4,2,128,256]{4,3,2,1,0:T(8,128)(2,1)}, bf16[4,4,2,128,256]{4,3,2,1,0:T(8,128)(2,1)}, u32[]{:S(2)}, u32[]{:S(2)}) %collective-permute-start.14) | collective-permute-done | bytes 2097184 | tf_op jit(solution)/shard_map/ppermute | solution.py:22
  105.0 12.8 %collective-permute-done.17.refs_4_.refs_9_ = bf16[2,4,2,128,256]{4,3,2,1,0:T(8,128)(2,1)S(1)} collective-permute-done((bf16[2,4,2,128,256]{4,3,2,1,0:T(8,128)(2,1)S(1)}, bf16[2,4,2,128,256]{4,3,2,1,0:T(8,128)(2,1)S(1)}, u32[]{:S(2)}, u32[]{:S(2)}) %collective-permute-start.17) | collective-permute-done | bytes 1048608 | tf_op jit(solution)/shard_map/ppermute | solution.py:22
  121.9 6.2 %collective-permute-start.18 = (f32[64,640]{1,0:T(8,128)S(1)}, f32[64,640]{1,0:T(8,128)S(1)}, u32[]{:S(2)}, u32[]{:S(2)}) collective-permute-start(f32[64,640]{1,0:T(8,128)S(1)} %shard_map.101.own_ref), channel_id=1, source_target_pairs={{0,1},{1,0},{2,3},{3,2},{4,5},{5,4},{6,7},{7,6},{8,9},{9,8},{10,11... | collective-permute-start | bytes 491528 | tf_op jit(solution)/shard_map/ppermute | solution.py:26
  129.2 5.3 %shard_map.102 = (bf16[128,2048]{1,0:T(8,128)(2,1)S(1)}, f32[64,640]{1,0:T(8,128)S(1)}, f32[64,640]{1,0:T(8,128)S(1)}) custom-call(bf16[128,2048]{1,0:T(8,128)(2,1)S(1)} %concatenate.14.x_ref.refs_12_, f32[64,640]{1,0:T(8,128)S(1)} %shard_map.101.own_ref, f32[64,640]{1,0:T(8,128)S(1)} %collective-permute-done.18.got_ref, ...), custom_call_target="tpu_custom_call" | custom-call | flops 402653184 | bytes 5242880 | tf_op jit(solution)/shard_map/pallas_call | solution.py:436
  138.1 5.3 %shard_map.103 = (bf16[128,2048]{1,0:T(8,128)(2,1)S(1)}, f32[64,640]{1,0:T(8,128)S(1)}, f32[64,640]{1,0:T(8,128)S(1)}) custom-call(bf16[128,2048]{1,0:T(8,128)(2,1)S(1)} %get-tuple-element.84.x_ref.refs_0_, f32[64,640]{1,0:T(8,128)S(1)} %get-tuple-element.85.own_ref, f32[64,640]{1,0:T(8,128)S(1)} %collective-permute-done.21.got_ref, ...), custom_call_target="tpu_custom_call" | custom-call | flops 402653184 | bytes 5242880 | tf_op jit(solution)/shard_map/pallas_call | solution.py:436
  145.0 5.3 %shard_map.104 = (bf16[128,2048]{1,0:T(8,128)(2,1)S(1)}, f32[64,640]{1,0:T(8,128)S(1)}, f32[64,640]{1,0:T(8,128)S(1)}) custom-call(bf16[128,2048]{1,0:T(8,128)(2,1)S(1)} %get-tuple-element.86.x_ref.refs_4_, f32[64,640]{1,0:T(8,128)S(1)} %get-tuple-element.87.own_ref, f32[64,640]{1,0:T(8,128)S(1)} %collective-permute-done.22.got_ref, ...), custom_call_target="tpu_custom_call" | custom-call | flops 402653184 | bytes 5242880 | tf_op jit(solution)/shard_map/pallas_call | solution.py:436
  151.8 4.1 %shard_map.105 = (bf16[128,2048]{1,0:T(8,128)(2,1)S(1)}, f32[64,512]{1,0:T(8,128)S(1)}, f32[64,640]{1,0:T(8,128)S(1)}) custom-call(bf16[128,2048]{1,0:T(8,128)(2,1)S(1)} %get-tuple-element.88.x_ref.refs_8_, f32[64,640]{1,0:T(8,128)S(1)} %get-tuple-element.89.own_ref, f32[64,640]{1,0:T(8,128)S(1)} %collective-permute-done.23.got_ref, ...), custom_call_target="tpu_custom_call" | custom-call | flops 402653184 | bytes 3145728 | tf_op jit(solution)/shard_map/pallas_call | solution.py:445
  157.3 5.3 %shard_map.106 = (bf16[128,2048]{1,0:T(8,128)(2,1)S(1)}, f32[64,512]{1,0:T(8,128)S(1)}, f32[64,512]{1,0:T(8,128)S(1)}) custom-call(bf16[128,2048]{1,0:T(8,128)(2,1)S(1)} %get-tuple-element.88.x_ref.refs_8_, bf16[128,2048]{1,0:T(8,128)(2,1)S(1)} %get-tuple-element.90.cot_ref.refs_9_, f32[64,640]{1,0:T(8,128)S(1)} %get-tuple-element.91.full_ref.refs_10_, ...), custom_call_target="tpu_custom_call" | custom-call | flops 402653184 | bytes 5242880 | tf_op jit(solution)/shard_map/pallas_call | solution.py:455
  164.1 5.3 %shard_map.107 = (bf16[128,2048]{1,0:T(8,128)(2,1)S(1)}, f32[64,512]{1,0:T(8,128)S(1)}, f32[64,512]{1,0:T(8,128)S(1)}) custom-call(bf16[128,2048]{1,0:T(8,128)(2,1)S(1)} %get-tuple-element.86.x_ref.refs_4_, bf16[128,2048]{1,0:T(8,128)(2,1)S(1)} %get-tuple-element.93.cot_ref.refs_5_, f32[64,640]{1,0:T(8,128)S(1)} %get-tuple-element.94.full_ref.refs_6_, ...), custom_call_target="tpu_custom_call" | custom-call | flops 402653184 | bytes 5242880 | tf_op jit(solution)/shard_map/pallas_call | solution.py:455
  170.9 5.3 %shard_map.108 = (bf16[128,2048]{1,0:T(8,128)(2,1)S(1)}, f32[64,512]{1,0:T(8,128)S(1)}, f32[64,512]{1,0:T(8,128)S(1)}) custom-call(bf16[128,2048]{1,0:T(8,128)(2,1)S(1)} %get-tuple-element.84.x_ref.refs_0_, bf16[128,2048]{1,0:T(8,128)(2,1)S(1)} %get-tuple-element.96.cot_ref.refs_1_, f32[64,640]{1,0:T(8,128)S(1)} %get-tuple-element.97.full_ref.refs_2_, ...), custom_call_target="tpu_custom_call" | custom-call | flops 402653184 | bytes 5242880 | tf_op jit(solution)/shard_map/pallas_call | solution.py:455
  186.4 6.9 %collective-permute-done.28.refs_2_ = bf16[2,4,128,256]{3,2,1,0:T(8,128)(2,1)S(1)} collective-permute-done((bf16[2,4,128,256]{3,2,1,0:T(8,128)(2,1)S(1)}, bf16[2,4,128,256]{3,2,1,0:T(8,128)(2,1)S(1)}, u32[]{:S(2)}, u32[]{:S(2)}) %collective-permute-start.28) | collective-permute-done | bytes 524320 | tf_op jit(solution)/shard_map/ppermute | solution.py:22
  201.4 18.7 %collective-permute-done.32.behind = bf16[4,4,128,256]{3,2,1,0:T(8,128)(2,1)S(1)} collective-permute-done((bf16[4,4,128,256]{3,2,1,0:T(8,128)(2,1)S(1)}, bf16[4,4,128,256]{3,2,1,0:T(8,128)(2,1)S(1)}, u32[]{:S(2)}, u32[]{:S(2)}) %collective-permute-start.32) | collective-permute-done | bytes 1048608 | tf_op jit(solution)/shard_map/ppermute | solution.py:22
  229.3 5.3 %collective-permute-done.36.refs_3_ = bf16[4,128,256]{2,1,0:T(8,128)(2,1)S(1)} collective-permute-done((bf16[4,128,256]{2,1,0:T(8,128)(2,1)S(1)}, bf16[4,128,256]{2,1,0:T(8,128)(2,1)S(1)}, u32[]{:S(2)}, u32[]{:S(2)}) %collective-permute-start.36) | collective-permute-done | bytes 262176 | tf_op jit(solution)/shard_map/ppermute | solution.py:22
  237.7 3.2 %collective-permute-start.42 = (bf16[256,256]{1,0:T(8,128)(2,1)S(1)}, bf16[256,256]{1,0:T(8,128)(2,1)S(1)}, u32[]{:S(2)}, u32[]{:S(2)}) collective-permute-start(bf16[256,256]{1,0:T(8,128)(2,1)S(1)} %get-tuple-element.128), channel_id=1, source_target_pairs={{0,32},{32,64},{64,96},{96,0},{1,33},{33,65},{65,97},{97,1},{2,34}... | collective-permute-start | bytes 393224 | tf_op jit(solution)/shard_map/ppermute | solution.py:22
  245.4 2.9 %collective-permute-done.44.b3 = bf16[256,256]{1,0:T(8,128)(2,1)S(1)} collective-permute-done((bf16[256,256]{1,0:T(8,128)(2,1)S(1)}, bf16[256,256]{1,0:T(8,128)(2,1)S(1)}, u32[]{:S(2)}, u32[]{:S(2)}) %collective-permute-start.44) | collective-permute-done | bytes 131104 | tf_op jit(solution)/shard_map/ppermute | solution.py:22
  248.5 21.1 %all_to_all.5 = f32[128,1,128]{2,1,0:T(1,128)S(1)} all-to-all(f32[128,1,128]{2,1,0:T(1,128)S(1)} %broadcast_in_dim.16), channel_id=1, replica_groups=mesh['y'=4,'z'=4,'x'=4,'c'=2] {'y','z','x','c'}, dimensions={0} | all-to-all | bytes 131072 | tf_op jit(solution)/shard_map/all_to_all | solution.py:500
  (111 shorter events, 85.7 us)
Async XLA Ops:
  6.9 12.1 %collective-permute-start.1 = (bf16[4,128,256]{2,1,0:T(8,128)(2,1)}, bf16[4,128,256]{2,1,0:T(8,128)(2,1)S(1)}, u32[]{:S(2)}, u32[]{:S(2)}) collective-permute-start(bf16[4,128,256]{2,1,0:T(8,128)(2,1)} %get-tuple-element.70.own), channel_id=1, source_target_pairs={{0,96},{32,0},{64,32},{96,64},{1,97},{33,1},{65,33},{97,65},{2,98}... | collective-permute-start | bytes 786440 | tf_op jit(solution)/shard_map/ppermute | solution.py:22
  7.7 11.6 %collective-permute-start = (bf16[4,128,256]{2,1,0:T(8,128)(2,1)}, bf16[4,128,256]{2,1,0:T(8,128)(2,1)S(1)}, u32[]{:S(2)}, u32[]{:S(2)}) collective-permute-start(bf16[4,128,256]{2,1,0:T(8,128)(2,1)} %get-tuple-element.70.own), channel_id=1, source_target_pairs={{0,32},{32,64},{64,96},{96,0},{1,33},{33,65},{65,97},{97,1},{2,34}... | collective-permute-start | bytes 786440 | tf_op jit(solution)/shard_map/ppermute | solution.py:22
  20.9 12.7 %collective-permute-start.10 = (bf16[4,2,128,256]{3,2,1,0:T(8,128)(2,1)S(1)}, bf16[4,2,128,256]{3,2,1,0:T(8,128)(2,1)S(1)}, u32[]{:S(2)}, u32[]{:S(2)}) collective-permute-start(bf16[4,2,128,256]{3,2,1,0:T(8,128)(2,1)S(1)} %get-tuple-element.74.own), channel_id=1, source_target_pairs={{0,6},{2,0},{4,2},{6,4},{1,7},{3,1},{5,3},{7,5},{8,14},{10,8},{12,... | collective-permute-start | bytes 1572872 | tf_op jit(solution)/shard_map/ppermute | solution.py:22
  23.5 13.3 %collective-permute-start.9 = (bf16[4,2,128,256]{3,2,1,0:T(8,128)(2,1)S(1)}, bf16[4,2,128,256]{3,2,1,0:T(8,128)(2,1)S(1)}, u32[]{:S(2)}, u32[]{:S(2)}) collective-permute-start(bf16[4,2,128,256]{3,2,1,0:T(8,128)(2,1)S(1)} %get-tuple-element.74.own), channel_id=1, source_target_pairs={{0,2},{2,4},{4,6},{6,0},{1,3},{3,5},{5,7},{7,1},{8,10},{10,12},{12... | collective-permute-start | bytes 1572872 | tf_op jit(solution)/shard_map/ppermute | solution.py:22
  23.5 16.0 %collective-permute-start.4 = (bf16[4,2,128,256]{3,2,1,0:T(8,128)(2,1)S(1)}, bf16[4,2,128,256]{3,2,1,0:T(8,128)(2,1)S(1)}, u32[]{:S(2)}, u32[]{:S(2)}) collective-permute-start(bf16[4,2,128,256]{3,2,1,0:T(8,128)(2,1)S(1)} %get-tuple-element.71.own), channel_id=1, source_target_pairs={{0,24},{8,0},{16,8},{24,16},{1,25},{9,1},{17,9},{25,17},{2,26},{10... | collective-permute-start | bytes 1572872 | tf_op jit(solution)/shard_map/ppermute | solution.py:22
  27.2 13.0 %collective-permute-start.3 = (bf16[4,2,128,256]{3,2,1,0:T(8,128)(2,1)S(1)}, bf16[4,2,128,256]{3,2,1,0:T(8,128)(2,1)S(1)}, u32[]{:S(2)}, u32[]{:S(2)}) collective-permute-start(bf16[4,2,128,256]{3,2,1,0:T(8,128)(2,1)S(1)} %get-tuple-element.71.own), channel_id=1, source_target_pairs={{0,8},{8,16},{16,24},{24,0},{1,9},{9,17},{17,25},{25,1},{2,10},{10... | collective-permute-start | bytes 1572872 | tf_op jit(solution)/shard_map/ppermute | solution.py:22
  45.0 48.0 %collective-permute-start.14 = (bf16[4,4,2,128,256]{4,3,2,1,0:T(8,128)(2,1)}, bf16[4,4,2,128,256]{4,3,2,1,0:T(8,128)(2,1)}, u32[]{:S(2)}, u32[]{:S(2)}) collective-permute-start(bf16[4,4,2,128,256]{4,3,2,1,0:T(8,128)(2,1)} %shard_map.99.refs_0_.refs_5_), channel_id=1, source_target_pairs={{0,24},{8,0},{16,8},{24,16},{1,25},{9,1},{17,9},{25,17},{2,26},{10... | collective-permute-start | bytes 6291464 | tf_op jit(solution)/shard_map/ppermute | solution.py:22
  48.5 44.9 %collective-permute-start.13 = (bf16[4,4,2,128,256]{4,3,2,1,0:T(8,128)(2,1)}, bf16[4,4,2,128,256]{4,3,2,1,0:T(8,128)(2,1)}, u32[]{:S(2)}, u32[]{:S(2)}) collective-permute-start(bf16[4,4,2,128,256]{4,3,2,1,0:T(8,128)(2,1)} %shard_map.99.refs_0_.refs_5_), channel_id=1, source_target_pairs={{0,8},{8,16},{16,24},{24,0},{1,9},{9,17},{17,25},{25,1},{2,10},{10... | collective-permute-start | bytes 6291464 | tf_op jit(solution)/shard_map/ppermute | solution.py:22
  48.7 44.7 %collective-permute-start.8 = (bf16[4,4,2,128,256]{4,3,2,1,0:T(8,128)(2,1)S(1)}, bf16[4,4,2,128,256]{4,3,2,1,0:T(8,128)(2,1)}, u32[]{:S(2)}, u32[]{:S(2)}) collective-permute-start(bf16[4,4,2,128,256]{4,3,2,1,0:T(8,128)(2,1)S(1)} %shard_map.97.refs_0_.refs_5_), channel_id=1, source_target_pairs={{0,6},{2,0},{4,2},{6,4},{1,7},{3,1},{5,3},{7,5},{8,14},{10,8},{12,... | collective-permute-start | bytes 6291464 | tf_op jit(solution)/shard_map/ppermute | solution.py:22
  51.4 44.1 %collective-permute-start.7 = (bf16[4,4,2,128,256]{4,3,2,1,0:T(8,128)(2,1)S(1)}, bf16[4,4,2,128,256]{4,3,2,1,0:T(8,128)(2,1)}, u32[]{:S(2)}, u32[]{:S(2)}) collective-permute-start(bf16[4,4,2,128,256]{4,3,2,1,0:T(8,128)(2,1)S(1)} %shard_map.97.refs_0_.refs_5_), channel_id=1, source_target_pairs={{0,2},{2,4},{4,6},{6,0},{1,3},{3,5},{5,7},{7,1},{8,10},{10,12},{12... | collective-permute-start | bytes 6291464 | tf_op jit(solution)/shard_map/ppermute | solution.py:22
  98.2 19.5 %collective-permute-start.17 = (bf16[2,4,2,128,256]{4,3,2,1,0:T(8,128)(2,1)S(1)}, bf16[2,4,2,128,256]{4,3,2,1,0:T(8,128)(2,1)S(1)}, u32[]{:S(2)}, u32[]{:S(2)}) collective-permute-start(bf16[2,4,2,128,256]{4,3,2,1,0:T(8,128)(2,1)S(1)} %slice.26), channel_id=1, source_target_pairs={{0,6},{2,0},{4,2},{6,4},{1,7},{3,1},{5,3},{7,5},{8,14},{10,8},{12,... | collective-permute-start | bytes 3145736 | tf_op jit(solution)/shard_map/ppermute | solution.py:22
  98.6 20.7 %collective-permute-start.16 = (bf16[2,4,2,128,256]{4,3,2,1,0:T(8,128)(2,1)S(1)}, bf16[2,4,2,128,256]{4,3,2,1,0:T(8,128)(2,1)S(1)}, u32[]{:S(2)}, u32[]{:S(2)}) collective-permute-start(bf16[2,4,2,128,256]{4,3,2,1,0:T(8,128)(2,1)S(1)} %slice.25), channel_id=1, source_target_pairs={{0,2},{2,4},{4,6},{6,0},{1,3},{3,5},{5,7},{7,1},{8,10},{10,12},{12... | collective-permute-start | bytes 3145736 | tf_op jit(solution)/shard_map/ppermute | solution.py:22
  102.4 25.8 %collective-permute-start.20 = (bf16[2,4,2,128,256]{4,3,2,1,0:T(8,128)(2,1)S(1)}, bf16[2,4,2,128,256]{4,3,2,1,0:T(8,128)(2,1)S(1)}, u32[]{:S(2)}, u32[]{:S(2)}) collective-permute-start(bf16[2,4,2,128,256]{4,3,2,1,0:T(8,128)(2,1)S(1)} %slice.28), channel_id=1, source_target_pairs={{0,24},{8,0},{16,8},{24,16},{1,25},{9,1},{17,9},{25,17},{2,26},{10... | collective-permute-start | bytes 3145736 | tf_op jit(solution)/shard_map/ppermute | solution.py:22
  104.9 23.3 %collective-permute-start.19 = (bf16[2,4,2,128,256]{4,3,2,1,0:T(8,128)(2,1)S(1)}, bf16[2,4,2,128,256]{4,3,2,1,0:T(8,128)(2,1)S(1)}, u32[]{:S(2)}, u32[]{:S(2)}) collective-permute-start(bf16[2,4,2,128,256]{4,3,2,1,0:T(8,128)(2,1)S(1)} %slice.27), channel_id=1, source_target_pairs={{0,8},{8,16},{16,24},{24,0},{1,9},{9,17},{17,25},{25,1},{2,10},{10... | collective-permute-start | bytes 3145736 | tf_op jit(solution)/shard_map/ppermute | solution.py:22
  178.9 14.4 %collective-permute-start.28 = (bf16[2,4,128,256]{3,2,1,0:T(8,128)(2,1)S(1)}, bf16[2,4,128,256]{3,2,1,0:T(8,128)(2,1)S(1)}, u32[]{:S(2)}, u32[]{:S(2)}) collective-permute-start(bf16[2,4,128,256]{3,2,1,0:T(8,128)(2,1)S(1)} %get-tuple-element.108), channel_id=1, source_target_pairs={{0,8},{8,16},{16,24},{24,0},{1,9},{9,17},{17,25},{25,1},{2,10},{10... | collective-permute-start | bytes 1572872 | tf_op jit(solution)/shard_map/ppermute | solution.py:22
  179.0 14.3 %collective-permute-start.29 = (bf16[2,4,128,256]{3,2,1,0:T(8,128)(2,1)S(1)}, bf16[2,4,128,256]{3,2,1,0:T(8,128)(2,1)S(1)}, u32[]{:S(2)}, u32[]{:S(2)}) collective-permute-start(bf16[2,4,128,256]{3,2,1,0:T(8,128)(2,1)S(1)} %get-tuple-element.109), channel_id=1, source_target_pairs={{0,24},{8,0},{16,8},{24,16},{1,25},{9,1},{17,9},{25,17},{2,26},{10... | collective-permute-start | bytes 1572872 | tf_op jit(solution)/shard_map/ppermute | solution.py:22
  181.7 13.7 %collective-permute-start.30 = (bf16[2,4,128,256]{3,2,1,0:T(8,128)(2,1)S(1)}, bf16[2,4,128,256]{3,2,1,0:T(8,128)(2,1)S(1)}, u32[]{:S(2)}, u32[]{:S(2)}) collective-permute-start(bf16[2,4,128,256]{3,2,1,0:T(8,128)(2,1)S(1)} %get-tuple-element.112), channel_id=1, source_target_pairs={{0,2},{2,4},{4,6},{6,0},{1,3},{3,5},{5,7},{7,1},{8,10},{10,12},{12... | collective-permute-start | bytes 1572872 | tf_op jit(solution)/shard_map/ppermute | solution.py:22
  181.7 13.7 %collective-permute-start.31 = (bf16[2,4,128,256]{3,2,1,0:T(8,128)(2,1)S(1)}, bf16[2,4,128,256]{3,2,1,0:T(8,128)(2,1)S(1)}, u32[]{:S(2)}, u32[]{:S(2)}) collective-permute-start(bf16[2,4,128,256]{3,2,1,0:T(8,128)(2,1)S(1)} %get-tuple-element.113), channel_id=1, source_target_pairs={{0,6},{2,0},{4,2},{6,4},{1,7},{3,1},{5,3},{7,5},{8,14},{10,8},{12,... | collective-permute-start | bytes 1572872 | tf_op jit(solution)/shard_map/ppermute | solution.py:22
  195.9 24.1 %collective-permute-start.32 = (bf16[4,4,128,256]{3,2,1,0:T(8,128)(2,1)S(1)}, bf16[4,4,128,256]{3,2,1,0:T(8,128)(2,1)S(1)}, u32[]{:S(2)}, u32[]{:S(2)}) collective-permute-start(bf16[4,4,128,256]{3,2,1,0:T(8,128)(2,1)S(1)} %get-tuple-element.114), channel_id=1, source_target_pairs={{0,8},{8,16},{16,24},{24,0},{1,9},{9,17},{17,25},{25,1},{2,10},{10... | collective-permute-start | bytes 3145736 | tf_op jit(solution)/shard_map/ppermute | solution.py:22
  196.0 24.0 %collective-permute-start.33 = (bf16[4,4,128,256]{3,2,1,0:T(8,128)(2,1)S(1)}, bf16[4,4,128,256]{3,2,1,0:T(8,128)(2,1)S(1)}, u32[]{:S(2)}, u32[]{:S(2)}) collective-permute-start(bf16[4,4,128,256]{3,2,1,0:T(8,128)(2,1)S(1)} %get-tuple-element.115), channel_id=1, source_target_pairs={{0,24},{8,0},{16,8},{24,16},{1,25},{9,1},{17,9},{25,17},{2,26},{10... | collective-permute-start | bytes 3145736 | tf_op jit(solution)/shard_map/ppermute | solution.py:22
  198.7 25.1 %collective-permute-start.37 = (bf16[4,4,128,256]{3,2,1,0:T(8,128)(2,1)S(1)}, bf16[4,4,128,256]{3,2,1,0:T(8,128)(2,1)S(1)}, u32[]{:S(2)}, u32[]{:S(2)}) collective-permute-start(bf16[4,4,128,256]{3,2,1,0:T(8,128)(2,1)S(1)} %get-tuple-element.121), channel_id=1, source_target_pairs={{0,2},{2,4},{4,6},{6,0},{1,3},{3,5},{5,7},{7,1},{8,10},{10,12},{12... | collective-permute-start | bytes 3145736 | tf_op jit(solution)/shard_map/ppermute | solution.py:22
  198.7 25.1 %collective-permute-start.38 = (bf16[4,4,128,256]{3,2,1,0:T(8,128)(2,1)S(1)}, bf16[4,4,128,256]{3,2,1,0:T(8,128)(2,1)S(1)}, u32[]{:S(2)}, u32[]{:S(2)}) collective-permute-start(bf16[4,4,128,256]{3,2,1,0:T(8,128)(2,1)S(1)} %get-tuple-element.122), channel_id=1, source_target_pairs={{0,6},{2,0},{4,2},{6,4},{1,7},{3,1},{5,3},{7,5},{8,14},{10,8},{12,... | collective-permute-start | bytes 3145736 | tf_op jit(solution)/shard_map/ppermute | solution.py:22
  223.2 11.4 %collective-permute-start.36 = (bf16[4,128,256]{2,1,0:T(8,128)(2,1)S(1)}, bf16[4,128,256]{2,1,0:T(8,128)(2,1)S(1)}, u32[]{:S(2)}, u32[]{:S(2)}) collective-permute-start(bf16[4,128,256]{2,1,0:T(8,128)(2,1)S(1)} %get-tuple-element.119), channel_id=1, source_target_pairs={{0,4},{2,6},{4,0},{6,2},{1,5},{3,7},{5,1},{7,3},{8,12},{10,14},{12... | collective-permute-start | bytes 786440 | tf_op jit(solution)/shard_map/ppermute | solution.py:22
  224.2 10.4 %collective-permute-start.39 = (bf16[4,128,256]{2,1,0:T(8,128)(2,1)S(1)}, bf16[4,128,256]{2,1,0:T(8,128)(2,1)S(1)}, u32[]{:S(2)}, u32[]{:S(2)}) collective-permute-start(bf16[4,128,256]{2,1,0:T(8,128)(2,1)S(1)} %get-tuple-element.124), channel_id=1, source_target_pairs={{0,8},{8,16},{16,24},{24,0},{1,9},{9,17},{17,25},{25,1},{2,10},{10... | collective-permute-start | bytes 786440 | tf_op jit(solution)/shard_map/ppermute | solution.py:22
  (26 other events, 176.8 us)
